TPU v7x, 32 devices: a whole 2x2x4 slice. The times are simulated.
32 devices in a mesh: dp: 8 (over z, y), mp: 4 (over x, core).
Axes of the slice: x: 2, y: 2, z: 4, core: 2. Of those that a mesh axis runs over, the one named last changes fastest.
Arguments:
- residual: bfloat16 [1024, 2048], P('dp'), may hold values from -6 to 6
- lengths: int32 [8, 3], P('dp'), may hold values from 1 to 96, 128 in all within a row
- pair_order: int32 [16], replicated, may hold values from 0 to 15, each once
- token_ids: int32 [1024], P('dp'), may hold values from 0 to 25599
- desirable: int32 [24], P('dp'), may hold values 0 or 1
- ref_match: float32 [1024], P('dp'), may hold values from -14 to -10
- ref_pair: float32 [1024], P('dp'), may hold values from -14 to -10
- attn_gain: bfloat16 [2048], replicated, may hold values from 0.099609375 to 1.8984375
- attn_shift: bfloat16 [2048], replicated, may hold values from -3 to 3
- mlp_gain: bfloat16 [2048], replicated, may hold values from 0.099609375 to 1.8984375
- mlp_shift: bfloat16 [2048], replicated, may hold values from -3 to 3
- w_joined: bfloat16 [2048, 6144], P('dp', 'mp'), may hold values from -0.125 to 0.125
- b_joined: bfloat16 [6144], P('mp'), may hold values from -3 to 3
- w_dense: bfloat16 [2048, 2048], P('mp', 'dp'), may hold values from -0.5 to 0.5
- b_dense: bfloat16 [2048], replicated, may hold values from -3 to 3
- w_up: bfloat16 [2048, 8192], P('dp', 'mp'), may hold values from -0.125 to 0.125
- b_up: bfloat16 [8192], P('mp'), may hold values from -3 to 3
- w_down: bfloat16 [8192, 2048], P('mp', 'dp'), may hold values from -0.0625 to 0.0625
- b_down: bfloat16 [2048], replicated, may hold values from -3 to 3
- final_gain: bfloat16 [2048], replicated, may hold values from 0.099609375 to 1.8984375
- final_shift: bfloat16 [2048], replicated, may hold values from -3 to 3
- w_vocab: bfloat16 [2048, 25600], P('dp', 'mp'), may hold values from -0.25 to 0.25
Outputs:
- kto_loss: float32 [], replicated
- kl_estimate: float32 [], replicated
- grad_input: float32 [1024, 2048], P('dp')
- grad_attn_gain: float32 [2048], replicated
- grad_attn_shift: float32 [2048], replicated
- grad_mlp_gain: float32 [2048], replicated
- grad_mlp_shift: float32 [2048], replicated
- grad_w_joined: float32 [2048, 6144], P('dp', 'mp')
- grad_b_joined: float32 [6144], P('mp')
- grad_w_dense: float32 [2048, 2048], P('mp', 'dp')
- grad_b_dense: float32 [2048], replicated
- grad_w_up: float32 [2048, 8192], P('dp', 'mp')
- grad_b_up: float32 [8192], P('mp')
- grad_w_down: float32 [8192, 2048], P('mp', 'dp')
- grad_b_down: float32 [2048], replicated
- grad_final_gain: float32 [2048], replicated
- grad_final_shift: float32 [2048], replicated
- grad_w_vocab: float32 [2048, 25600], P('dp', 'mp')
Inputs may be any that keep to these rules, and one draw needn't show every extreme that they name: `lengths`: each row sums to 128, and its largest entry is 96. `pair_order`: a permutation of the 16 blocks.
All inputs are finite; a program needn't handle non-finite values. No bound on the sum of `desirable` on one device may be relied on, other than what follows from the above.
Results may differ from a plain program's by a relative error of at most 0.014.
Values may be sent and summed in bfloat16 or wider, within the bound.
A program may use at most 320 MiB of HBM per device.

v0:
```python
import math

import jax
import jax.numpy as jnp
from jax import lax
from jax.sharding import PartitionSpec as P

HD = 128
ROT = 32


kto_beta = 4.0
norm_eps = 1e-05
masked_score = -1e30


def joined(value, axis, join):
    pieces = jax.tree.map(lambda part: lax.all_gather(part, axis), value)
    head = jax.tree.map(lambda part: part[0], pieces)
    tail = jax.tree.map(lambda part: part[1:], pieces)
    subtotal, _ = lax.scan(lambda subtotal, piece: (join(subtotal, piece), None), head, tail)
    return subtotal


def layer_norm(values, norm_gain, norm_shift):
    centred = values - jnp.mean(values, axis=-1, keepdims=True)
    spread = jnp.mean(centred * centred, axis=-1, keepdims=True)
    return centred * lax.rsqrt(spread + norm_eps) * norm_gain + norm_shift


def rotate(values, position):
    half_rot = ROT // 2
    inverse = jnp.exp(jnp.arange(half_rot, dtype=jnp.float32) * (-2.0 * math.log(10000.0) / ROT))
    angles = position.astype(jnp.float32)[:, None] * inverse[None, :]
    cosine_table = jnp.cos(angles)[:, None, :]
    sine_table = jnp.sin(angles)[:, None, :]
    first_half = values[..., :half_rot]
    second_half = values[..., half_rot:ROT]
    return jnp.concatenate(
        [
            first_half * cosine_table - second_half * sine_table,
            second_half * cosine_table + first_half * sine_table,
            values[..., ROT:],
        ],
        axis=-1,
    )


def gelu_exact(values):
    return jax.nn.gelu(values, approximate=False)


def attention_scores(query_low, keys_low, allowed):
    raw_scores = jnp.einsum(
        "rhd,chd->hrc", query_low, keys_low, preferred_element_type=jnp.float32
    ) / math.sqrt(HD)
    return jnp.where(allowed[None], raw_scores, masked_score)


def combine_vocab(first, second):
    high_first, total_first, pick_first = first
    high_second, total_second, pick_second = second
    highest = jnp.maximum(high_first, high_second)
    merged_total = total_first * jnp.exp(high_first - highest) + total_second * jnp.exp(
        high_second - highest
    )
    return (highest, merged_total, pick_first + pick_second)


def gather_weights(weights_low):
    w_joined, w_up, w_vocab, w_dense, w_down = weights_low
    joined_all, up_all, vocab_all = (
        lax.all_gather(w_joined, "dp", axis=0, tiled=True),
        lax.all_gather(w_up, "dp", axis=0, tiled=True),
        lax.all_gather(w_vocab, "dp", axis=0, tiled=True),
    )
    dense_all, down_all = (
        lax.all_gather(w_dense, "dp", axis=1, tiled=True),
        lax.all_gather(w_down, "dp", axis=1, tiled=True),
    )
    return (joined_all, up_all, vocab_all, dense_all, down_all)


def forward_pass(gathered, smalls, rows_low, allowed, position, targets):
    joined_all, up_all, vocab_all, dense_all, down_all = gathered
    (
        attn_gain,
        attn_shift,
        mlp_gain,
        mlp_shift,
        b_joined,
        b_dense,
        b_up,
        b_down,
        final_gain,
        final_shift,
    ) = smalls
    rows_float = rows_low.astype(jnp.float32)
    count_rows = rows_float.shape[0]
    attn_low = layer_norm(rows_float, attn_gain, attn_shift).astype(jnp.bfloat16)
    mlp_low = layer_norm(rows_float, mlp_gain, mlp_shift).astype(jnp.bfloat16)
    joined_cols = jnp.dot(attn_low, joined_all, preferred_element_type=jnp.float32) + b_joined
    joined_cols = joined_cols.reshape(count_rows, -1, 3, HD)
    query_low = rotate(joined_cols[:, :, 0], position).astype(jnp.bfloat16)
    keys_low = rotate(joined_cols[:, :, 1], position).astype(jnp.bfloat16)
    values_low = joined_cols[:, :, 2].astype(jnp.bfloat16)
    scores = attention_scores(query_low, keys_low, allowed)
    highest = jnp.max(scores, axis=-1, keepdims=True)
    scaled_exp = jnp.exp(scores - highest)
    totals = jnp.sum(scaled_exp, axis=-1, keepdims=True)
    probs_low = (scaled_exp / totals).astype(jnp.bfloat16)
    score_lse = highest + jnp.log(totals)
    mixed_low = (
        jnp.einsum("hrc,chd->rhd", probs_low, values_low, preferred_element_type=jnp.float32)
        .reshape(count_rows, -1)
        .astype(jnp.bfloat16)
    )
    hidden = jnp.dot(mlp_low, up_all, preferred_element_type=jnp.float32) + b_up
    active_low = gelu_exact(hidden).astype(jnp.bfloat16)
    branch_part = jnp.dot(mixed_low, dense_all, preferred_element_type=jnp.float32) + jnp.dot(
        active_low, down_all, preferred_element_type=jnp.float32
    )
    branch = lax.psum(branch_part, "mp")
    resid_sum = rows_float + branch + b_dense + b_down
    final_low = layer_norm(resid_sum, final_gain, final_shift).astype(jnp.bfloat16)
    logits = jnp.dot(final_low, vocab_all, preferred_element_type=jnp.float32)
    local_high = jnp.max(logits, axis=-1)
    local_total = jnp.sum(jnp.exp(logits - local_high[:, None]), axis=-1)
    column = targets - lax.axis_index("mp") * logits.shape[1]
    target_hit = lax.broadcasted_iota(jnp.int32, logits.shape, 1) == column[:, None]
    local_pick = jnp.sum(jnp.where(target_hit, logits, 0.0), axis=-1)
    high_all, total_all, picked = joined((local_high, local_total, local_pick), "mp", combine_vocab)
    vocab_lse = high_all + jnp.log(total_all)
    return (
        attn_low,
        mlp_low,
        joined_cols,
        query_low,
        keys_low,
        values_low,
        score_lse,
        mixed_low,
        hidden,
        active_low,
        resid_sum,
        final_low,
        logits,
        vocab_lse,
        target_hit,
        picked - vocab_lse,
    )


def shards(
    residual,
    lengths,
    pair_order,
    token_ids,
    desirable,
    ref_match,
    ref_pair,
    attn_gain,
    attn_shift,
    mlp_gain,
    mlp_shift,
    w_joined,
    b_joined,
    w_dense,
    b_dense,
    w_up,
    b_up,
    w_down,
    b_down,
    final_gain,
    final_shift,
    w_vocab,
):
    dp_count = lax.axis_size("dp")
    tokens_here = residual.shape[0]
    piece_rows = tokens_here // 2
    width = residual.shape[1]
    seq_here = lengths.shape[1]
    block_count = 2 * dp_count
    my_index = lax.axis_index("dp")
    block_slots = jnp.arange(block_count, dtype=jnp.int32)
    my_blocks = 2 * my_index + jnp.arange(2, dtype=jnp.int32)
    my_targets = jnp.sum(
        jnp.where(block_slots[None, :] == my_blocks[:, None], pair_order[None, :], 0), axis=1
    )
    send_hot = my_targets[:, None] == block_slots[None, :]
    own_blocks = residual.reshape(2, piece_rows, width)
    own_ids = token_ids.reshape(2, piece_rows)
    sent_rows = jnp.einsum(
        "ht,hpd->tpd", send_hot.astype(jnp.bfloat16), own_blocks, preferred_element_type=jnp.float32
    ).astype(jnp.bfloat16)
    sent_ids = jnp.sum(jnp.where(send_hot[:, :, None], own_ids[:, None, :], 0), axis=0)
    got_rows, got_ids = (
        lax.all_to_all(
            sent_rows.reshape(dp_count, 2, piece_rows, width),
            "dp",
            split_axis=0,
            concat_axis=0,
            tiled=True,
        ),
        lax.all_to_all(
            sent_ids.reshape(dp_count, 2, piece_rows), "dp", split_axis=0, concat_axis=0, tiled=True
        ),
    )
    paired_rows = jnp.sum(got_rows.astype(jnp.float32), axis=0).astype(jnp.bfloat16)
    paired_ids = jnp.sum(got_ids, axis=0)
    rows_low = jnp.concatenate([residual, paired_rows.reshape(tokens_here, width)], axis=0)
    ids_all = jnp.concatenate([token_ids, paired_ids.reshape(tokens_here)], axis=0)
    seq_lengths = lengths[0]
    seq_ends = jnp.cumsum(seq_lengths)
    seq_starts = seq_ends - seq_lengths
    places = jnp.arange(tokens_here, dtype=jnp.int32)
    seq_slots = jnp.arange(seq_here, dtype=jnp.int32)
    segment = jnp.sum((places[:, None] >= seq_ends[None, :]).astype(jnp.int32), axis=1)
    own_start = jnp.sum(
        jnp.where(segment[:, None] == seq_slots[None, :], seq_starts[None, :], 0), axis=1
    )
    position_half = places - own_start
    segment_all = jnp.concatenate([segment, segment + seq_here])
    position = jnp.concatenate([position_half, position_half])
    count_rows = 2 * tokens_here
    row_index = jnp.arange(count_rows, dtype=jnp.int32)
    allowed = (segment_all[:, None] == segment_all[None, :]) & (
        row_index[None, :] <= row_index[:, None]
    )
    targets = jnp.concatenate([ids_all[1:], jnp.zeros((1,), jnp.int32)])
    scored = jnp.concatenate(
        [segment_all[1:] == segment_all[:-1], jnp.zeros((1,), jnp.bool_)]
    ).astype(jnp.float32)
    ref_rows = jnp.concatenate([ref_match, ref_pair])
    length_float = seq_lengths.astype(jnp.float32)
    length_both = jnp.concatenate([length_float, length_float])
    seq_match = segment_all[:, None] == jnp.arange(2 * seq_here, dtype=jnp.int32)[None, :]
    smalls = tuple(
        (
            value.astype(jnp.float32)
            for value in (
                attn_gain,
                attn_shift,
                mlp_gain,
                mlp_shift,
                b_joined,
                b_dense,
                b_up,
                b_down,
                final_gain,
                final_shift,
            )
        )
    )
    weights_low = (w_joined, w_up, w_vocab, w_dense, w_down)
    gathered = gather_weights(weights_low)
    first_pass = forward_pass(gathered, smalls, rows_low, allowed, position, targets)
    token_terms = (first_pass[15] - ref_rows) * scored
    seq_means = jnp.sum(jnp.where(seq_match, token_terms[:, None], 0.0), axis=0) / length_both
    kl_total = lax.psum(jnp.sum(seq_means[seq_here:]), "dp")
    seq_total = seq_here * dp_count
    kl_estimate = kl_total / seq_total
    signs = 2.0 * desirable.astype(jnp.float32) - 1.0
    sigmoid_val = jax.nn.sigmoid(kto_beta * signs * (seq_means[:seq_here] - kl_estimate))
    slope = -kto_beta * signs * sigmoid_val * (1.0 - sigmoid_val)
    kto_loss, slope_total = lax.psum((jnp.sum(1.0 - sigmoid_val), jnp.sum(slope)), "dp")
    seq_coef = (
        jnp.concatenate([slope, jnp.broadcast_to(-slope_total / seq_total, (seq_here,))])
        / length_both
    )
    token_coef = jnp.sum(jnp.where(seq_match, seq_coef[None, :], 0.0), axis=1) * scored
    matrices = gather_weights(weights_low)
    current = forward_pass(matrices, smalls, rows_low, allowed, position, targets)
    joined_all, up_all, vocab_all, dense_all, down_all = matrices
    (
        attn_low,
        mlp_low,
        joined_cols,
        query_low,
        keys_low,
        values_low,
        score_lse,
        mixed_low,
        hidden,
        active_low,
        resid_sum,
        final_low,
        logits,
        vocab_lse,
        target_hit,
        log_probs,
    ) = current
    softmax_local = jnp.exp(logits - vocab_lse[:, None])
    dlogits = (token_coef[:, None] * (jnp.where(target_hit, 1.0, 0.0) - softmax_local)).astype(
        jnp.bfloat16
    )
    grad_vocab = jnp.einsum("rd,rv->dv", final_low, dlogits, preferred_element_type=jnp.float32)
    dfinal_part = jnp.einsum("rv,dv->rd", dlogits, vocab_all, preferred_element_type=jnp.float32)
    dfinal = lax.psum(dfinal_part, "mp")
    _, final_pull = jax.vjp(layer_norm, resid_sum, smalls[8], smalls[9])
    dresid, grad_final_gain, grad_final_shift = final_pull(dfinal)
    grad_b_out = jnp.sum(dresid, axis=0)
    dbranch = dresid.astype(jnp.bfloat16)
    grad_dense = jnp.einsum("rk,rd->kd", mixed_low, dbranch, preferred_element_type=jnp.float32)
    grad_down = jnp.einsum("rf,rd->fd", active_low, dbranch, preferred_element_type=jnp.float32)
    dmixed = jnp.einsum("rd,kd->rk", dbranch, dense_all, preferred_element_type=jnp.float32).astype(
        jnp.bfloat16
    )
    dactive = jnp.einsum("rd,fd->rf", dbranch, down_all, preferred_element_type=jnp.float32)
    _, gelu_pull = jax.vjp(gelu_exact, hidden)
    dhidden = gelu_pull(dactive)[0].astype(jnp.bfloat16)
    grad_up = jnp.einsum("rd,rf->df", mlp_low, dhidden, preferred_element_type=jnp.float32)
    grad_b_up = jnp.sum(dhidden.astype(jnp.float32), axis=0)
    dmlp_part = jnp.einsum("rf,df->rd", dhidden, up_all, preferred_element_type=jnp.float32)
    dmixed_heads = dmixed.reshape(count_rows, -1, HD)
    scores = attention_scores(query_low, keys_low, allowed)
    probs_float = jnp.where(allowed[None], jnp.exp(scores - score_lse), 0.0)
    dvalues = jnp.einsum(
        "hrc,rhd->chd",
        probs_float.astype(jnp.bfloat16),
        dmixed_heads,
        preferred_element_type=jnp.float32,
    )
    dprobs = jnp.einsum(
        "rhd,chd->hrc", dmixed_heads, values_low, preferred_element_type=jnp.float32
    )
    inner_sum = jnp.sum(probs_float * dprobs, axis=-1, keepdims=True)
    dscores = (probs_float * (dprobs - inner_sum)).astype(jnp.bfloat16)
    dquery = jnp.einsum(
        "hrc,chd->rhd", dscores, keys_low, preferred_element_type=jnp.float32
    ) / math.sqrt(HD)
    dkeys = jnp.einsum(
        "hrc,rhd->chd", dscores, query_low, preferred_element_type=jnp.float32
    ) / math.sqrt(HD)
    _, rotate_pull = jax.vjp(lambda value: rotate(value, position), joined_cols[:, :, 0])
    dfused = jnp.stack([rotate_pull(dquery)[0], rotate_pull(dkeys)[0], dvalues], axis=2)
    dfused = dfused.reshape(count_rows, -1).astype(jnp.bfloat16)
    grad_joined = jnp.einsum("rd,re->de", attn_low, dfused, preferred_element_type=jnp.float32)
    grad_b_joined = jnp.sum(dfused.astype(jnp.float32), axis=0)
    dattn_part = jnp.einsum("re,de->rd", dfused, joined_all, preferred_element_type=jnp.float32)
    dattn, dmlp = lax.psum((dattn_part, dmlp_part), "mp")
    rows_float = rows_low.astype(jnp.float32)
    _, attn_pull = jax.vjp(layer_norm, rows_float, smalls[0], smalls[1])
    drows_attn, grad_attn_gain, grad_attn_shift = attn_pull(dattn)
    _, mlp_pull = jax.vjp(layer_norm, rows_float, smalls[2], smalls[3])
    drows_mlp, grad_mlp_gain, grad_mlp_shift = mlp_pull(dmlp)
    drows = dresid + drows_attn + drows_mlp
    my_slots = 2 * my_index + jnp.arange(2, dtype=jnp.int32)
    anchor = jnp.sum(
        jnp.where(pair_order[None, :] == my_slots[:, None], block_slots[None, :], 0), axis=1
    )
    back_hot = (anchor[:, None] == block_slots[None, :]).astype(jnp.float32)
    back_blocks = drows[tokens_here:].reshape(2, piece_rows, width)
    back_sent = jnp.einsum("st,spd->tpd", back_hot, back_blocks, precision=lax.Precision.HIGHEST)
    returned = lax.all_to_all(
        back_sent.reshape(dp_count, 2, piece_rows, width),
        "dp",
        split_axis=0,
        concat_axis=0,
        tiled=True,
    )
    grad_input = drows[:tokens_here] + jnp.sum(returned, axis=0).reshape(tokens_here, width)
    gw_joined, gw_up, gw_vocab = (
        lax.psum_scatter(grad_joined, "dp", scatter_dimension=0, tiled=True),
        lax.psum_scatter(grad_up, "dp", scatter_dimension=0, tiled=True),
        lax.psum_scatter(grad_vocab, "dp", scatter_dimension=0, tiled=True),
    )
    gw_dense, gw_down = (
        lax.psum_scatter(grad_dense, "dp", scatter_dimension=1, tiled=True),
        lax.psum_scatter(grad_down, "dp", scatter_dimension=1, tiled=True),
    )
    (
        sg_attn_gain,
        sg_attn_shift,
        sg_mlp_gain,
        sg_mlp_shift,
        sg_b_joined,
        sg_b_up,
        sg_b_out,
        sg_final_gain,
        sg_final_shift,
    ) = lax.psum(
        (
            grad_attn_gain,
            grad_attn_shift,
            grad_mlp_gain,
            grad_mlp_shift,
            grad_b_joined,
            grad_b_up,
            grad_b_out,
            grad_final_gain,
            grad_final_shift,
        ),
        "dp",
    )
    return (
        kto_loss,
        kl_estimate,
        grad_input,
        sg_attn_gain,
        sg_attn_shift,
        sg_mlp_gain,
        sg_mlp_shift,
        gw_joined,
        sg_b_joined,
        gw_dense,
        sg_b_out,
        gw_up,
        sg_b_up,
        gw_down,
        sg_b_out,
        sg_final_gain,
        sg_final_shift,
        gw_vocab,
    )


def solution(mesh):
    return jax.shard_map(
        shards,
        mesh=mesh,
        in_specs=(
            P("dp", None),
            P("dp", None),
            P(),
            P("dp"),
            P("dp"),
            P("dp"),
            P("dp"),
            P(),
            P(),
            P(),
            P(),
            P("dp", "mp"),
            P("mp"),
            P("mp", "dp"),
            P(),
            P("dp", "mp"),
            P("mp"),
            P("mp", "dp"),
            P(),
            P(),
            P(),
            P("dp", "mp"),
        ),
        out_specs=(
            P(),
            P(),
            P("dp", None),
            P(),
            P(),
            P(),
            P(),
            P("dp", "mp"),
            P("mp"),
            P("mp", "dp"),
            P(),
            P("dp", "mp"),
            P("mp"),
            P("mp", "dp"),
            P(),
            P(),
            P(),
            P("dp", "mp"),
        ),
        check_vma=False,
    )
```

profile of v0, /device:TPU:1, one launch (start us, length us, event | category | flops | bytes accessed | tf_op | source)
XLA Modules:
  0.0 3173.2 jit_solution(6965201930821528346)
XLA Ops:
  10.2 3.0 convolution_convert_fusion
  13.2 7.6 reshape.365
  20.8 8.0 copy.151
  28.9 6.4 all-to-all-start
  37.1 149.8 %all-to-all-done = bf16[8,2,64,2048]{3,1,2,0:T(2,128)(2,1)} async-done(((bf16[8,2,64,2048]{3,1,2,0:T(2,128)(2,1)}), bf16[8,2,64,2048]{3,1,2,0:T(2,128)(2,1)}, u32[]{:S(2)}, u32[]{:S(2)}) %all-to-all-start) | async-done | bytes 4194336 | tf_op jit(solution)/shard_map/all_to_all | solution.py:198
  186.9 6.3 reduce_sum.328
  194.1 5.8 convolution_add_fusion.1
  199.9 2.0 copy.154
  201.9 1.0 fusion.76
  203.2 1.2 copy.193
  206.4 0.8 copy-done.2
  207.2 1.4 convolution_convert_fusion.2
  208.6 106.5 %all-gather.16.cloned.1.call-done = bf16[2048,2048]{1,0:T(8,128)(2,1)} async-done(((bf16[256,2048]{1,0:T(8,128)(2,1)}), bf16[2048,2048]{1,0:T(8,128)(2,1)}) %all-gather.16.cloned.1.call-update) | async-done | bytes 8388624 | tf_op jit(solution)/shard_map/all_gather | solution.py:74
  315.1 10.8 multiply_convert_fusion.1
  325.9 114.8 %all-gather.18.cloned.1.call-done = bf16[2048,2048]{1,0:T(8,128)(2,1)} async-done(((bf16[2048,256]{1,0:T(8,128)(2,1)}), bf16[2048,2048]{1,0:T(8,128)(2,1)}) %all-gather.18.cloned.1.call-update) | async-done | bytes 8388624 | tf_op jit(solution)/shard_map/all_gather | solution.py:79
  440.7 6.0 fusion.79
  446.7 45.0 %all-gather.14.cloned.1.call-done = bf16[512,2048]{1,0:T(8,128)(2,1)} async-done(((bf16[512,256]{1,0:T(8,128)(2,1)}), bf16[512,2048]{1,0:T(8,128)(2,1)}) %all-gather.14.cloned.1.call-update) | async-done | bytes 2097168 | tf_op jit(solution)/shard_map/all_gather | solution.py:78
  491.7 3.6 convolution_add_fusion
  497.0 3.3 all-to-all-start.1
  500.5 5.0 all-to-all-done.1
  507.0 38.6 %all-reduce.14.cloned.1.call-done = f32[256,2048]{1,0:T(8,128)} async-done(((f32[256,2048]{1,0:T(8,128)}), f32[256,2048]{1,0:T(8,128)}) %all-reduce.14.cloned.1.call-update) | async-done | bytes 2097168 | tf_op jit(solution)/shard_map/psum | solution.py:123
  545.7 2.0 fusion.73
  548.1 499.3 %all-gather.20.cloned.1.call-done = bf16[2048,6400]{1,0:T(8,128)(2,1)} async-done(((bf16[256,6400]{1,0:T(8,128)(2,1)}), bf16[2048,6400]{1,0:T(8,128)(2,1)}) %all-gather.20.cloned.1.call-update) | async-done | bytes 26214416 | tf_op jit(solution)/shard_map/all_gather | solution.py:75
  1047.4 12.5 fusion.78
  1059.9 2.0 select_reduce_fusion
  1062.7 5.5 all-gather.4
  1068.2 5.1 all-gather.5
  1073.3 5.1 all-gather.3
  1079.7 17.0 psum.116
  1097.4 1.1 fusion.72
  1098.6 14.3 psum.118
  1113.7 15.1 fusion.68
  1129.4 56.6 %all-reduce.16.cloned.1.call-done = f32[256,2048]{1,0:T(8,128)} async-done(((f32[256,2048]{1,0:T(8,128)}), f32[256,2048]{1,0:T(8,128)}) %all-reduce.16.cloned.1.call-update) | async-done | bytes 2097168 | tf_op jit(solution)/shard_map/psum | solution.py:299
  1186.0 2.4 multiply_reduce_fusion
  1189.2 1.3 copy-done.4
  1190.6 1.0 copy-done.8
  1191.6 1.5 convolution_convert_fusion.1
  1193.0 1.1 copy.195
  1194.1 1.9 multiply_reduce_fusion.3
  1199.8 1.1 convert_reduce_fusion.2
  1200.9 2.3 copy.173
  1203.2 7.9 convert_reduce_fusion.1
  1211.2 7.4 fusion.81
  1218.6 6.1 fusion.80
  1224.8 0.9 copy-done.26
  1225.7 3.9 fusion.82
  1229.6 7.8 fusion.61
  1237.5 9.7 fusion.83
  1247.8 9.7 fusion.58
  1258.3 22.8 fusion.66
  1281.1 29.5 all-reduce.18.cloned.1.call-done
  1310.6 3.2 fusion.70
  1314.1 2.1 fusion.15
  1316.3 2.3 add_add_fusion.3
  1319.2 4.5 fusion.30
  1323.7 8.2 copy.175
  1331.9 5.4 all-to-all-start.2
  1337.9 236.9 %all-reduce.19 = (f32[]{:T(128)}, f32[2048]{0:T(1024)}, f32[2048]{0:T(1024)}, f32[2048]{0:T(1024)}, f32[2048]{0:T(1024)}, /*index=5*/f32[1536]{0:T(1024)}, f32[2...) all-reduce(f32[]{:T(128)} %subtract_reduce_fusion, ...), channel_id=1, replica_groups=mesh['dp'=8,'mp'=4] {'dp'}, use_global_device_ids=true, to_apply=%region_23.24 | all-reduce | flops 17921 | bytes 143368 | tf_op jit(solution)/shard_map/psum | solution.py:266
  1574.8 4.3 reduce_sum.370
  1579.1 1.1 slice_add_fusion
  1580.2 186.8 %reduce-scatter.6.cloned.1.call-done = f32[256,1536]{1,0:T(8,128)} async-done(((f32[2048,1536]{1,0:T(8,128)}), f32[256,1536]{1,0:T(8,128)}) %reduce-scatter.6.cloned.1.call-update) | async-done | bytes 1572880 | tf_op jit(solution)/shard_map/reduce_scatter | solution.py:364
  1767.0 286.2 %reduce-scatter.12.cloned.1.call-done = f32[2048,256]{1,0:T(8,128)} async-done(((f32[2048,2048]{1,0:T(8,128)}), f32[2048,256]{1,0:T(8,128)}) %reduce-scatter.12.cloned.1.call-update) | async-done | bytes 2097168 | tf_op jit(solution)/shard_map/reduce_scatter | solution.py:370
  2053.2 286.4 %reduce-scatter.10.cloned.1.call-done = f32[256,2048]{1,0:T(8,128)} async-done(((f32[2048,2048]{1,0:T(8,128)}), f32[256,2048]{1,0:T(8,128)}) %reduce-scatter.10.cloned.1.call-update) | async-done | bytes 2097168 | tf_op jit(solution)/shard_map/reduce_scatter | solution.py:365
  2339.6 825.0 %reduce-scatter.14.cloned.1.call-done = f32[256,6400]{1,0:T(8,128)} async-done(((f32[2048,6400]{1,0:T(8,128)}), f32[256,6400]{1,0:T(8,128)}) %reduce-scatter.14.cloned.1.call-update) | async-done | bytes 6553616 | tf_op jit(solution)/shard_map/reduce_scatter | solution.py:366
  (265 shorter events, 22.3 us)
Async XLA Ops:
  7.2 2.3 copy-start.58
  7.2 3.0 copy-start
  7.2 186.9 %all-gather.12.cloned.1.call-start = ((), (), s32[]{:S(2)}) async-start(), calls=%async_computation.8 | async-start | bytes 7077888 | tf_op jit(solution)/shard_map/all_gather | solution.py:73
  7.9 307.1 %all-gather.16.cloned.1.call-start = ((), (), s32[]{:S(2)}) async-start(), calls=%async_computation.10 | async-start | bytes 9437184 | tf_op jit(solution)/shard_map/all_gather | solution.py:74
  8.7 432.0 %all-gather.18.cloned.1.call-start = ((), (), s32[]{:S(2)}) async-start(), calls=%async_computation.11 | async-start | bytes 9437184 | tf_op jit(solution)/shard_map/all_gather | solution.py:79
  28.8 7.3 copy-start.46
  28.8 7.3 copy-start.47
  28.8 7.3 copy-start.48
  28.8 7.3 copy-start.49
  28.8 7.4 copy-start.50
  28.8 7.4 copy-start.51
  28.8 7.4 copy-start.59
  28.9 158.1 %all-to-all-start = ((bf16[8,2,64,2048]{3,1,2,0:T(2,128)(2,1)}), bf16[8,2,64,2048]{3,1,2,0:T(2,128)(2,1)}, u32[]{:S(2)}, u32[]{:S(2)}) async-start(bf16[8,2,64,2048]{3,1,2,0:T(2,128)(2,1)} %copy.151), calls=%async_computation | async-start | bytes 8388608 | tf_op jit(solution)/shard_map/all_to_all | solution.py:198
  35.3 456.4 %all-gather.14.cloned.1.call-start = ((), (), s32[]{:S(2)}) async-start(), calls=%async_computation.9 | async-start | bytes 2359296 | tf_op jit(solution)/shard_map/all_gather | solution.py:78
  35.9 509.8 %all-reduce.14.cloned.1.call-start = ((), (), s32[]{:S(2)}) async-start(), calls=%async_computation.12 | async-start | bytes 4194304 | tf_op jit(solution)/shard_map/psum | solution.py:123
  36.2 278.9 %copy-start.32 = (f32[2048]{0:T(1024)}, f32[2048]{0:T(1024)S(1)}, u32[]{:S(2)}) copy-start(f32[2048]{0:T(1024)S(1)} %convert_element_type.152) | copy-start | bytes 24580
  36.9 168.1 %copy-start.27 = (f32[256,16]{1,0:T(8,128)}, f32[256,16]{1,0:T(8,128)S(1)}, u32[]{:S(2)}) copy-start(f32[256,16]{1,0:T(8,128)S(1)} %copy.157) | copy-start | bytes 49156
  37.0 168.0 %copy-start.29 = (f32[256,16]{1,0:T(8,128)}, f32[256,16]{1,0:T(8,128)S(1)}, u32[]{:S(2)}) copy-start(f32[256,16]{1,0:T(8,128)S(1)} %copy.158) | copy-start | bytes 49156
  194.1 5.8 copy-start.36
  201.9 1.3 copy-start.10
  205.0 1.2 copy-start.14
  206.2 1.0 copy-start.2
  208.6 283.2 %copy-start.25 = (bf16[4,128,256]{2,1,0:T(8,128)(2,1)}, bf16[4,128,256]{2,1,0:T(8,128)(2,1)S(1)}, u32[]{:S(2)}) copy-start(bf16[4,128,256]{2,1,0:T(8,128)(2,1)S(1)} %convolution_convert_fusion.2) | copy-start | bytes 786436
  495.4 5.0 copy-start.52
  495.4 5.0 copy-start.53
  495.4 5.0 copy-start.54
  495.5 5.0 copy-start.55
  495.5 551.9 %all-gather.20.cloned.1.call-start = ((), (), s32[]{:S(2)}) async-start(), calls=%async_computation.13 | async-start | bytes 29491200 | tf_op jit(solution)/shard_map/all_gather | solution.py:75
  497.0 8.5 all-to-all-start.1
  500.3 685.7 %all-reduce.16.cloned.1.call-start = ((), (), s32[]{:S(2)}) async-start(), calls=%async_computation.14 | async-start | bytes 4194304 | tf_op jit(solution)/shard_map/psum | solution.py:299
  507.0 606.7 %copy-start.38 = (s32[256]{0:T(256)}, s32[256]{0:T(256)S(1)}, u32[]{:S(2)}) copy-start(s32[256]{0:T(256)S(1)} %add_subtract_fusion) | copy-start | bytes 3076
  1059.9 2.8 copy-start.1
  1059.9 18.7 copy-start.56
  1059.9 18.7 copy-start.57
  1059.9 37.5 %copy-start.61 = (s32[3]{0:T(128)S(1)}, s32[3]{0:T(128)}, u32[]{:S(2)}) copy-start(s32[3]{0:T(128)} %param.30) | copy-start | bytes 40
  1113.7 15.1 copy-start.42
  1113.7 15.1 copy-start.44
  1128.9 181.7 %all-reduce.18.cloned.1.call-start = ((), (), s32[]{:S(2)}) async-start(), calls=%async_computation.20 | async-start | bytes 8388608 | tf_op jit(solution)/shard_map/psum | solution.py:341
  1186.0 2.5 copy-start.9
  1189.1 1.3 copy-start.4
  1189.1 2.5 copy-start.24
  1189.1 3.9 copy-start.34
  1190.6 1.0 copy-start.8
  1194.1 1.9 copy-start.3
  1196.1 1.0 copy-start.21
  1196.1 1.1 copy-start.23
  1196.4 1.2 copy-start.15
  1196.4 1.2 copy-start.17
  1196.4 1.2 copy-start.19
  1211.1 7.5 copy-start.31
  1211.1 7.5 copy-start.11
  1224.8 355.4 %reduce-scatter.8.cloned.1.call-start = ((), (), s32[]{:S(2)}) async-start(), calls=%async_computation.16 | async-start | bytes 4718592 | tf_op jit(solution)/shard_map/reduce_scatter | solution.py:369
  1229.6 537.4 %reduce-scatter.6.cloned.1.call-start = ((), (), s32[]{:S(2)}) async-start(), calls=%async_computation.15 | async-start | bytes 14155776 | tf_op jit(solution)/shard_map/reduce_scatter | solution.py:364
  1237.4 815.8 %reduce-scatter.12.cloned.1.call-start = ((), (), s32[]{:S(2)}) async-start(), calls=%async_computation.18 | async-start | bytes 18874368 | tf_op jit(solution)/shard_map/reduce_scatter | solution.py:370
  1247.2 1092.5 %reduce-scatter.10.cloned.1.call-start = ((), (), s32[]{:S(2)}) async-start(), calls=%async_computation.17 | async-start | bytes 18874368 | tf_op jit(solution)/shard_map/reduce_scatter | solution.py:365
  1257.6 1907.1 %reduce-scatter.14.cloned.1.call-start = ((), (), s32[]{:S(2)}) async-start(), calls=%async_computation.19 | async-start | bytes 58982400 | tf_op jit(solution)/shard_map/reduce_scatter | solution.py:366
  1310.6 3.2 copy-start.37
  1310.6 3.3 copy-start.6
  1310.6 3.5 copy-start.7
  1314.1 2.1 copy-start.5
  1314.1 2.1 copy-start.35
  1331.9 5.4 copy-start.62
  1331.9 242.9 %all-to-all-start.2 = ((f32[8,2,64,2048]{3,2,1,0:T(8,128)}), f32[8,2,64,2048]{3,2,1,0:T(8,128)}, u32[]{:S(2)}, u32[]{:S(2)}) async-start(f32[8,2,64,2048]{3,2,1,0:T(8,128)} %copy.175), calls=%async_computation.2 | async-start | bytes 16777216 | tf_op jit(solution)/shard_map/all_to_all | solution.py:355
  1574.8 1589.9 %copy-start.40 = (f32[2048]{0:T(1024)}, f32[2048]{0:T(1024)S(1)}, u32[]{:S(2)}) copy-start(f32[2048]{0:T(1024)S(1)} %get-tuple-element.361) | copy-start | bytes 24580
  (15 other events, 12.2 us)
Sparse Core Ops, SparseCore 0:
  10.2 181.1 all-gather.11
  193.6 121.4 all-gather.15
  317.1 123.5 all-gather.17
  442.6 49.1 all-gather.13
  495.5 50.0 all-reduce.13
  547.1 500.2 all-gather.19
  1129.0 56.9 all-reduce.15
  1224.9 85.6 all-reduce.17
  1315.2 242.3 reduce-scatter.7
  1561.6 205.3 reduce-scatter.5
  1771.4 281.8 reduce-scatter.11
  2057.9 281.6 reduce-scatter.9
  2344.1 820.4 reduce-scatter.13
where the time goes:
time: 3180 us; the launch traced here: 3170 us
  waiting for transfers between devices  2630 us (83%)
  blocking collectives  284 us (9%)
  matrix products  143 us (4%)
  local copies, waits for them, and re-layouts  42.7 us (1%)
  other arithmetic  36.3 us (1%)
    reduce_scatter x1, waiting for transfers between devices, shards(): lax.psum_scatter(grad_vocab, 'dp', scatter_dimension=0, tiled=True)  825 us
    all_gather x1, waiting for transfers between devices, gather_weights(): lax.all_gather(w_vocab, 'dp', axis=0, tiled=True)  499 us
    reduce_scatter x1, waiting for transfers between devices, shards(): lax.psum_scatter(grad_up, 'dp', scatter_dimension=0, tiled=True)  286 us
    reduce_scatter x1, waiting for transfers between devices, shards(): lax.psum_scatter(grad_down, 'dp', scatter_dimension=1, tiled=True)  286 us
    psum x2, blocking collectives, shards(): lax.psum((jnp.sum(1.0 - sigmoid_val), jnp.sum(slope)), 'dp')  251 us
    reduce_scatter x1, waiting for transfers between devices, shards(): lax.psum_scatter(grad_joined, 'dp', scatter_dimension=0, tiled=True)  187 us
    all_to_all x1, waiting for transfers between devices, shards(): lax.all_to_all(sent_rows.reshape(dp_count, 2, piece_rows, width), 'dp', s...  150 us
    all_gather x1, waiting for transfers between devices, gather_weights(): lax.all_gather(w_down, 'dp', axis=1, tiled=True)  115 us
  transfers between devices with their start and end apart: 16, of which 13 were waited for; matrix products, arithmetic and copies ran while one was open for 4% of the time, Pallas kernels for 0%

commit v1 on v0

--- a/solution.py
+++ b/solution.py
@@ -1,8 +1,11 @@
+import functools
 import math
 
 import jax
 import jax.numpy as jnp
 from jax import lax
+from jax.experimental import pallas as pl
+from jax.experimental.pallas import tpu as pltpu
 from jax.sharding import PartitionSpec as P
 
 HD = 128
@@ -211,10 +214,12 @@
     rows_low = jnp.concatenate([residual, paired_rows.reshape(tokens_here, width)], axis=0)
     ids_all = jnp.concatenate([token_ids, paired_ids.reshape(tokens_here)], axis=0)
     seq_lengths = lengths[0]
-    seq_ends = jnp.cumsum(seq_lengths)
+    seq_slots = jnp.arange(seq_here, dtype=jnp.int32)
+    seq_ends = jnp.sum(
+        jnp.where(seq_slots[None, :] <= seq_slots[:, None], seq_lengths[None, :], 0), axis=1
+    )
     seq_starts = seq_ends - seq_lengths
     places = jnp.arange(tokens_here, dtype=jnp.int32)
-    seq_slots = jnp.arange(seq_here, dtype=jnp.int32)
     segment = jnp.sum((places[:, None] >= seq_ends[None, :]).astype(jnp.int32), axis=1)
     own_start = jnp.sum(
         jnp.where(segment[:, None] == seq_slots[None, :], seq_starts[None, :], 0), axis=1
@@ -415,53 +420,1261 @@
     )
 
 
+DP = ("z", "y")
+CHIPS = ("z", "y", "x")
+ALL = ("z", "y", "x", "c")
+SWAP = ((0, 1), (1, 0))
+F32, BF16 = jnp.float32, jnp.bfloat16
+
+
+def dot(a, b, contract):
+    return lax.dot_general(a, b, ((contract[:1], contract[1:]), ((), ())), preferred_element_type=F32)
+
+
+def swap(value):
+    return lax.ppermute(value, "c", SWAP)
+
+
+def normed(values):
+    centred = values - jnp.mean(values, axis=-1, keepdims=True)
+    inverse = lax.rsqrt(jnp.mean(centred * centred, axis=-1, keepdims=True) + norm_eps)
+    return centred * inverse, inverse
+
+
+def norm_back(t, hat, inverse):
+    return inverse * (
+        t - jnp.mean(t, axis=-1, keepdims=True) - hat * jnp.mean(t * hat, axis=-1, keepdims=True)
+    )
+
+
+def turn(values, cosine, sine):
+    half_rot = ROT // 2
+    first, second = values[:, :half_rot], values[:, half_rot:ROT]
+    return jnp.concatenate(
+        [first * cosine - second * sine, second * cosine + first * sine, values[:, ROT:]], axis=1
+    )
+
+
+def copy_block(order_ref, from_ref, to_ref):
+    to_ref[...] = from_ref[...]
+
+
+def take_blocks(values, order, piece):
+    count, width = values.shape[0] // piece, values.shape[1]
+    return pl.pallas_call(
+        copy_block,
+        out_shape=jax.ShapeDtypeStruct(values.shape, values.dtype),
+        grid_spec=pltpu.PrefetchScalarGridSpec(
+            num_scalar_prefetch=1,
+            grid=(count,),
+            in_specs=[pl.BlockSpec((piece, width), lambda i, order: (order[i], 0))],
+            out_specs=pl.BlockSpec((piece, width), lambda i, order: (i, 0)),
+        ),
+    )(order, values)
+
+
+def exchange(value):
+    return lax.all_to_all(value, DP, split_axis=0, concat_axis=0, tiled=True)
+
+
+def here():
+    return tuple(lax.axis_index(a) for a in ALL)
+
+
+def send(source, target, out_sem, in_sem, device):
+    copy = pltpu.make_async_remote_copy(
+        src_ref=source,
+        dst_ref=target,
+        send_sem=out_sem,
+        recv_sem=in_sem,
+        device_id=device,
+        device_id_type=pl.DeviceIdType.MESH,
+    )
+    copy.start()
+    return copy
+
+
+def arrived(target, out_sem, in_sem, device):
+    pltpu.make_async_remote_copy(
+        src_ref=target,
+        dst_ref=target,
+        send_sem=out_sem,
+        recv_sem=in_sem,
+        device_id=device,
+        device_id_type=pl.DeviceIdType.MESH,
+    ).wait_recv()
+
+
+def greet(devices):
+    barrier = pltpu.get_barrier_semaphore()
+    for device in devices:
+        pl.semaphore_signal(barrier, inc=1, device_id=device, device_id_type=pl.DeviceIdType.MESH)
+    pl.semaphore_wait(barrier, len(devices))
+
+
+def neighbours(nz):
+    iz, iy, ix, ic = here()
+    return [(lax.rem(iz + k, nz), iy, ix, ic) for k in range(1, nz)] + [
+        (iz, 1 - iy, ix, ic),
+        (iz, iy, 1 - ix, ic),
+    ]
+
+
+def other_core():
+    iz, iy, ix, ic = here()
+    return (iz, iy, ix, 1 - ic)
+
+
+class Reduce:
+    @staticmethod
+    def scratch(nz, half, width):
+        dma = pltpu.SemaphoreType.DMA
+        return [
+            pltpu.VMEM((2, nz, 2, half, width), BF16),
+            pltpu.VMEM((2, nz, half, width), BF16),
+            pltpu.VMEM((2, nz, half, width), BF16),
+            pltpu.VMEM((2, nz, half, width), BF16),
+            pltpu.VMEM((2, nz, half, width), BF16),
+            dma((2, nz, 2)),
+            dma((2, nz, 2)),
+            dma((2, nz)),
+            dma((2, nz)),
+            dma((2, nz)),
+            dma((2, nz)),
+        ]
+
+    def __init__(self, nz, half, part, refs):
+        self.nz, self.half, self.part = nz, half, part
+        (
+            self.in1,
+            self.out2,
+            self.in2,
+            self.out3,
+            self.in3,
+            self.s1,
+            self.r1,
+            self.s2,
+            self.r2,
+            self.s3,
+            self.r3,
+        ) = refs
+        self.copies = []
+
+    def along(self, h):
+        iz, iy, ix, ic = here()
+        across_x, across_y = (iz, iy, 1 - ix, ic), (iz, 1 - iy, ix, ic)
+        return (across_x, across_y) if h == 0 else (across_y, across_x)
+
+    def block(self, h, z, first_mine, second):
+        _, iy, ix, _ = here()
+        rows = pl.ds(h * self.half, self.half)
+        if h == 0:
+            return self.part.at[z, second, ix if first_mine else 1 - ix, rows]
+        return self.part.at[z, iy if first_mine else 1 - iy, second, rows]
+
+    def mine(self, h):
+        _, iy, ix, _ = here()
+        return iy if h == 0 else ix
+
+    def plane(self, k):
+        return lax.rem(here()[0] + k, self.nz)
+
+    def start(self, h, far):
+        first, _ = self.along(h)
+        second = 1 - self.mine(h) if far else self.mine(h)
+        for k in list(range(1, self.nz)) + [0]:
+            z = self.plane(k)
+            self.copies.append(
+                send(
+                    self.block(h, z, False, second),
+                    self.in1.at[h, z, second],
+                    self.s1.at[h, z, second],
+                    self.r1.at[h, z, second],
+                    first,
+                )
+            )
+
+    def second(self, h):
+        first, across = self.along(h)
+        far = 1 - self.mine(h)
+        for k in list(range(1, self.nz)) + [0]:
+            z = self.plane(k)
+            arrived(self.in1.at[h, z, far], self.s1.at[h, z, far], self.r1.at[h, z, far], first)
+            self.out2[h, z] = (
+                self.block(h, z, True, far)[...].astype(F32) + self.in1[h, z, far].astype(F32)
+            ).astype(BF16)
+            self.copies.append(
+                send(self.out2.at[h, z], self.in2.at[h, z], self.s2.at[h, z], self.r2.at[h, z], across)
+            )
+
+    def third(self, h):
+        iz, iy, ix, ic = here()
+        first, across = self.along(h)
+        near = self.mine(h)
+        for k in list(range(1, self.nz)) + [0]:
+            z = self.plane(k)
+            arrived(self.in1.at[h, z, near], self.s1.at[h, z, near], self.r1.at[h, z, near], first)
+            arrived(self.in2.at[h, z], self.s2.at[h, z], self.r2.at[h, z], across)
+            total = (
+                self.block(h, z, True, near)[...].astype(F32)
+                + self.in1[h, z, near].astype(F32)
+                + self.in2[h, z].astype(F32)
+            )
+            if k == 0:
+                return total
+            self.out3[h, k] = total.astype(BF16)
+            self.copies.append(
+                send(
+                    self.out3.at[h, k],
+                    self.in3.at[h, k],
+                    self.s3.at[h, k],
+                    self.r3.at[h, k],
+                    (z, iy, ix, ic),
+                )
+            )
+
+    def finish(self, h, total):
+        _, iy, ix, ic = here()
+        for k in range(1, self.nz):
+            z = self.plane(self.nz - k)
+            arrived(self.in3.at[h, k], self.s3.at[h, k], self.r3.at[h, k], (z, iy, ix, ic))
+            total = total + self.in3[h, k].astype(F32)
+        return total
+
+
+class Gather:
+    @staticmethod
+    def scratch(nz):
+        dma = pltpu.SemaphoreType.DMA
+        return [dma((2, nz)), dma((2, nz)), dma((2, nz, 2)), dma((2, nz, 2, 2)), dma((2,))]
+
+    def __init__(self, nz, half, out, refs, forward=None):
+        self.nz, self.half, self.out = nz, half, out
+        self.sz, self.sp, self.sq, self.r, self.local = refs
+        self.copies, self.locals, self.forward = [], [], forward
+
+    def axes(self, h):
+        iz, iy, ix, ic = here()
+        across_x, across_y = (iz, iy, 1 - ix, ic), (iz, 1 - iy, ix, ic)
+        return (across_y, across_x) if h == 0 else (across_x, across_y)
+
+    def block(self, h, z, y, x):
+        return self.out.at[z, y, x, pl.ds(h * self.half, self.half)]
+
+    def on(self, h, source, z, y, x, which):
+        iz, iy, ix, ic = here()
+        p, q = self.axes(h)
+        there, got = self.block(h, z, y, x), self.r.at[h, z, y, x]
+        if "z" in which:
+            for k in range(1, self.nz):
+                far = (lax.rem(iz + k, self.nz), iy, ix, ic)
+                self.copies.append(send(source, there, self.sz.at[h, k], got, far))
+        if "p" in which:
+            self.copies.append(send(source, there, self.sp.at[h, z], got, p))
+        if "q" in which:
+            side = x if h == 1 else y
+            self.copies.append(send(source, there, self.sq.at[h, z, side], got, q))
+        if self.forward is not None:
+            self.forward(h, source, z, y, x)
+
+    def start(self, h, source):
+        iz, iy, ix, _ = here()
+        copy = pltpu.make_async_copy(source, self.block(h, iz, iy, ix), self.local.at[h])
+        copy.start()
+        self.locals.append(copy)
+        self.on(h, source, iz, iy, ix, "zpq")
+
+    def got(self, h, z, y, x):
+        arrived(self.block(h, z, y, x), self.sz.at[h, 0], self.r.at[h, z, y, x], self.axes(h)[0])
+
+    def first(self, h, k):
+        iz, iy, ix, _ = here()
+        z = lax.rem(iz + k, self.nz)
+        self.got(h, z, iy, ix)
+        self.on(h, self.block(h, z, iy, ix), z, iy, ix, "pq")
+
+    def second(self, h, k):
+        iz, iy, ix, _ = here()
+        z = lax.rem(iz + k, self.nz)
+        y, x = (1 - iy, ix) if h == 0 else (iy, 1 - ix)
+        self.got(h, z, y, x)
+        self.on(h, self.block(h, z, y, x), z, y, x, "q")
+
+    def third(self, h, k):
+        iz, iy, ix, _ = here()
+        z = lax.rem(iz + k, self.nz)
+        for side in (0, 1):
+            if h == 0:
+                y, x = (iy if side == 0 else 1 - iy), 1 - ix
+            else:
+                y, x = 1 - iy, (ix if side == 0 else 1 - ix)
+            self.got(h, z, y, x)
+            if self.forward is not None:
+                self.forward(h, self.block(h, z, y, x), z, y, x)
+
+    def rest(self):
+        turns = [1, self.nz - 1] + [k for k in range(2, self.nz - 1)]
+        for h in (0, 1):
+            self.second(h, 0)
+        for k in turns:
+            for h in (0, 1):
+                self.first(h, k)
+        for k in turns:
+            for h in (0, 1):
+                self.second(h, k)
+        for k in [0] + turns:
+            for h in (0, 1):
+                self.third(h, k)
+
+    def end(self):
+        for copy in self.locals:
+            copy.wait()
+        for copy in self.copies:
+            copy.wait_send()
+
+
+def run_reduce(reduce):
+    for far in (True, False):
+        for h in (0, 1):
+            reduce.start(h, far)
+    for h in (0, 1):
+        reduce.second(h)
+
+
+def forward_kernel(nz, half, part, rows, bias, gain, shift, out, resid, fin, *refs):
+    reduce = Reduce(nz, half, part, refs[:11])
+    gather = Gather(nz, half, out, refs[11:])
+    greet(neighbours(nz))
+    run_reduce(reduce)
+    kept = [reduce.third(h) for h in (0, 1)]
+    for h in (0, 1):
+        at = pl.ds(h * half, half)
+        total = rows[at].astype(F32) + reduce.finish(h, kept[h]) + bias[...]
+        resid[at] = total
+        hat, _ = normed(total)
+        fin[h] = (hat * gain[...] + shift[...]).astype(BF16)
+        gather.start(h, fin.at[h])
+    gather.rest()
+    gather.end()
+    for copy in reduce.copies:
+        copy.wait_send()
+
+
+def backward_kernel(nz, half, part, resid, gain, out, vectors, fin, *refs):
+    reduce = Reduce(nz, half, part, refs[:11])
+    gather = Gather(nz, half, out, refs[11:])
+    greet(neighbours(nz))
+    run_reduce(reduce)
+    kept = [reduce.third(h) for h in (0, 1)]
+    sums = []
+    for h in (0, 1):
+        total = reduce.finish(h, kept[h])
+        hat, inverse = normed(resid[pl.ds(h * half, half)])
+        dresid = norm_back(total * gain[...], hat, inverse)
+        fin[h] = dresid.astype(BF16)
+        gather.start(h, fin.at[h])
+        sums.append([jnp.sum(v, axis=0, keepdims=True) for v in (total * hat, total, dresid)])
+    for i in range(3):
+        vectors[pl.ds(i, 1)] = sums[0][i] + sums[1][i]
+    gather.rest()
+    gather.end()
+    for copy in reduce.copies:
+        copy.wait_send()
+
+
+def vmem():
+    return pl.BlockSpec(memory_space=pltpu.VMEM)
+
+
+def anywhere():
+    return pl.BlockSpec(memory_space=pl.ANY)
+
+
+def comm(which, limit=48):
+    return pltpu.CompilerParams(collective_id=which, has_side_effects=True, vmem_limit_bytes=limit << 20)
+
+
+def reduce_norm_gather(nz, part, rows, bias, gain, shift):
+    share, width = rows.shape
+    half = share // 2
+    out, resid = pl.pallas_call(
+        functools.partial(forward_kernel, nz, half),
+        out_shape=[
+            jax.ShapeDtypeStruct((nz, 2, 2, share, width), BF16),
+            jax.ShapeDtypeStruct((share, width), F32),
+        ],
+        in_specs=[vmem()] * 5,
+        out_specs=[anywhere(), vmem()],
+        scratch_shapes=[pltpu.VMEM((2, half, width), BF16)]
+        + Reduce.scratch(nz, half, width)
+        + Gather.scratch(nz),
+        compiler_params=comm(2),
+    )(part.reshape(nz, 2, 2, share, width), rows, bias, gain, shift)
+    return out.reshape(4 * nz * share, width), resid
+
+
+def reduce_back_gather(nz, part, resid, gain):
+    share, width = resid.shape
+    half = share // 2
+    out, vectors = pl.pallas_call(
+        functools.partial(backward_kernel, nz, half),
+        out_shape=[
+            jax.ShapeDtypeStruct((nz, 2, 2, share, width), BF16),
+            jax.ShapeDtypeStruct((3, width), F32),
+        ],
+        in_specs=[vmem()] * 3,
+        out_specs=[anywhere(), vmem()],
+        scratch_shapes=[pltpu.VMEM((2, half, width), BF16)]
+        + Reduce.scratch(nz, half, width)
+        + Gather.scratch(nz),
+        compiler_params=comm(3),
+    )(part.reshape(nz, 2, 2, share, width), resid, gain)
+    return out.reshape(4 * nz * share, width), vectors
+
+
+def merge(a, b):
+    top = jnp.maximum(a[0], b[0])
+    return (top, a[1] * jnp.exp(a[0] - top) + b[1] * jnp.exp(b[0] - top), a[2] + b[2])
+
+
+def objective_kernel(
+    nz, seqs, seq_total, stats, hot, scored, refs, lens, wanted, coef, lse_out, scalars, held, got, ss, rs
+):
+    iz, iy, ix, ic = here()
+    peers = neighbours(nz) + [other_core()]
+    greet(peers)
+    current = tuple(stats[i] for i in range(3))
+    copies = []
+    for step, (mine, device) in enumerate(((ix, (iz, iy, 1 - ix, ic)), (iy, (iz, 1 - iy, ix, ic)))):
+        for i in range(3):
+            held[step, i] = current[i]
+        copies.append(send(held.at[step], got.at[step], ss.at[step], rs.at[step], device))
+        arrived(got.at[step], ss.at[step], rs.at[step], device)
+        theirs = tuple(got[step, i] for i in range(3))
+        low = tuple(jnp.where(mine == 0, a, b) for a, b in zip(current, theirs))
+        high = tuple(jnp.where(mine == 0, b, a) for a, b in zip(current, theirs))
+        current = merge(low, high)
+    for i in range(3):
+        held[2, i] = current[i]
+    for k in range(1, nz):
+        z = lax.rem(iz + k, nz)
+        copies.append(send(held.at[2], got.at[2 + iz], ss.at[2 + k], rs.at[2 + iz], (z, iy, ix, ic)))
+    for i in range(3):
+        got[2 + iz, i] = current[i]
+    for k in range(1, nz):
+        z = lax.rem(iz + k, nz)
+        arrived(got.at[2 + z], ss.at[2], rs.at[2 + z], (z, iy, ix, ic))
+    current = tuple(got[2, i] for i in range(3))
+    for z in range(1, nz):
+        current = merge(current, tuple(got[2 + z, i] for i in range(3)))
+    lse = current[0] + jnp.log(current[1])
+    logp = current[2] - lse
+    lse_out[...] = lse
+    held[3, 0] = logp
+    last = 2 + nz
+    copies.append(send(held.at[3, 0], got.at[last, 0], ss.at[last], rs.at[last], other_core()))
+    arrived(got.at[last, 0], ss.at[last], rs.at[last], other_core())
+    theirs = got[last, 0]
+    own = jnp.where(ic == 0, logp, theirs)
+    pair = jnp.where(ic == 0, theirs, logp)
+
+    def means(values, ref):
+        terms = (values - ref) * scored[...]
+        return [
+            jnp.sum(terms * hot[s], axis=1, keepdims=True) / lens[:, s : s + 1] for s in range(seqs)
+        ]
+
+    own_means, pair_means = means(own, refs[0]), means(pair, refs[1])
+    kl = jnp.sum(sum(pair_means), axis=0, keepdims=True) / seq_total
+    loss = jnp.zeros((1, 1), F32)
+    slopes = []
+    for s in range(seqs):
+        sign = 2.0 * wanted[:, s : s + 1] - 1.0
+        sigmoid = jax.nn.sigmoid(kto_beta * sign * (own_means[s] - kl))
+        slopes.append(-kto_beta * sign * sigmoid * (1.0 - sigmoid))
+        loss = loss + jnp.sum(1.0 - sigmoid, axis=0, keepdims=True)
+    shared = -jnp.sum(sum(slopes), axis=0, keepdims=True) / seq_total
+    total = jnp.zeros_like(logp)
+    for s in range(seqs):
+        value = jnp.where(ic == 0, slopes[s], shared) / lens[:, s : s + 1]
+        total = total + hot[s] * value
+    coef[...] = total * scored[...]
+    scalars[0] = jnp.broadcast_to(loss, scalars.shape[1:])
+    scalars[1] = jnp.broadcast_to(kl, scalars.shape[1:])
+    for copy in copies:
+        copy.wait_send()
+
+
+def objective(nz, seq_total, stats, hot, scored, refs, lens, wanted):
+    shape = scored.shape
+    dma = pltpu.SemaphoreType.DMA
+    return pl.pallas_call(
+        functools.partial(objective_kernel, nz, hot.shape[0], seq_total),
+        out_shape=[
+            jax.ShapeDtypeStruct(shape, F32),
+            jax.ShapeDtypeStruct(shape, F32),
+            jax.ShapeDtypeStruct((2, 8, 128), F32),
+        ],
+        in_specs=[vmem()] * 6,
+        out_specs=[vmem()] * 3,
+        scratch_shapes=[
+            pltpu.VMEM((4, 3) + shape, F32),
+            pltpu.VMEM((3 + nz, 3) + shape, F32),
+            dma((3 + nz,)),
+            dma((3 + nz,)),
+        ],
+        compiler_params=comm(4),
+    )(stats, hot, scored, refs, lens, wanted)
+
+
+def diagonal(nz):
+    iz, iy, ix, ic = here()
+    return [(lax.rem(iz + k, nz), 1 - iy, ix, 1 - ic) for k in range(nz)]
+
+
+def to_head(nz, k, pairs, local_sem, out_sem, in_sem):
+    iz, iy, ix, ic = here()
+    z = lax.rem(iz + k, nz)
+    device = (z, ic, ix, iy)
+
+    def remote():
+        for i, (source, target) in enumerate(pairs):
+            send(source, target, out_sem.at[i, z], in_sem.at[i, iz], device)
+
+    if k:
+        remote()
+        return
+    pl.when(iy != ic)(remote)
+
+    @pl.when(iy == ic)
+    def _():
+        for i, (source, target) in enumerate(pairs):
+            copy = pltpu.make_async_copy(source, target, local_sem.at[i])
+            copy.start()
+            copy.wait()
+
+
+def from_head(nz, k, targets, out_sem, in_sem):
+    iz, iy, ix, ic = here()
+    z = lax.rem(iz + k, nz)
+
+    def wait():
+        for i, target in enumerate(targets):
+            arrived(target, out_sem.at[i, z], in_sem.at[i, z], (z, ic, ix, iy))
+
+    if k:
+        wait()
+    else:
+        pl.when(iy != ic)(wait)
+
+
+def sent_head(nz, k, sources, out_sem, in_sem):
+    iz, iy, ix, ic = here()
+    z = lax.rem(iz + k, nz)
+
+    def wait():
+        for i, source in enumerate(sources):
+            pltpu.make_async_remote_copy(
+                src_ref=source,
+                dst_ref=source,
+                send_sem=out_sem.at[i, z],
+                recv_sem=in_sem.at[i, z],
+                device_id=(z, ic, ix, iy),
+                device_id_type=pl.DeviceIdType.MESH,
+            ).wait_send()
+
+    if k:
+        wait()
+    else:
+        pl.when(iy != ic)(wait)
+
+
+def lanes(index, size):
+    return pl.ds(pl.multiple_of(index * size, size), size)
+
+
+def front_kernel(
+    nz,
+    half,
+    residual,
+    info,
+    bias,
+    joined_in,
+    dense_in,
+    natural,
+    info_out,
+    bias_out,
+    joined_out,
+    dense_out,
+    fs,
+    fr,
+    js,
+    jr,
+    jl,
+    cs,
+    cr,
+    ms,
+    mr,
+    zs,
+    zr,
+    ps,
+    *refs,
+):
+    iz, iy, ix, ic = here()
+    core = other_core()
+    greet(neighbours(nz) + [core] + diagonal(nz))
+    depth = joined_in.shape[0]
+    cols = joined_out.shape[1]
+    heads = dense_out.shape[0]
+    copies = []
+
+    def rows_of(h, z, y, x, c):
+        return natural.at[z, y, x, c, pl.ds(h * half, half)]
+
+    def forward(h, source, z, y, x):
+        copies.append(send(source, rows_of(h, z, y, x, ic), fs.at[h, z, y, x], fr.at[h, z, y, x], core))
+
+    class Rows(Gather):
+        def block(self, h, z, y, x):
+            return rows_of(h, z, y, x, ic)
+
+    gather = Rows(nz, half, natural, refs, forward)
+    first = pl.multiple_of((ix * 2 + ic) * 2 * half, 2 * half)
+    for h in (0, 1):
+        gather.start(h, residual.at[pl.ds(first + h * half, half)])
+
+    copies.append(send(bias, bias_out, ms.at[0], mr.at[0], core))
+    info_out[iz, iy] = info[...]
+    across_y = (iz, 1 - iy, ix, ic)
+    for k in range(1, nz):
+        far = (lax.rem(iz + k, nz), iy, ix, ic)
+        copies.append(send(info, info_out.at[iz, iy], zs.at[k], zr.at[iz, iy], far))
+    copies.append(send(info, info_out.at[iz, iy], ps.at[iz], zr.at[iz, iy], across_y))
+
+    mine = iz * 2 + iy
+    for k in list(range(1, nz)) + [0]:
+        z = lax.rem(iz + k, nz)
+        to_head(
+            nz,
+            k,
+            [
+                (joined_in.at[:, lanes(z, cols)], joined_out.at[lanes(mine, depth)]),
+                (dense_in.at[lanes(z, heads)], dense_out.at[:, lanes(mine, depth)]),
+            ],
+            jl,
+            js,
+            jr,
+        )
+
+    for k in range(1, nz):
+        z = lax.rem(iz + k, nz)
+        arrived(info_out.at[z, iy], zs.at[k], zr.at[z, iy], across_y)
+        copies.append(send(info_out.at[z, iy], info_out.at[z, iy], ps.at[z], zr.at[z, iy], across_y))
+
+    gather.rest()
+
+    def head_parts(z, side):
+        d = z * 2 + side
+        return joined_out.at[lanes(d, depth)], dense_out.at[:, lanes(d, depth)]
+
+    for k in [0] + list(range(1, nz)):
+        z = lax.rem(iz + k, nz)
+        parts = head_parts(z, ic)
+        from_head(nz, k, parts, js, jr)
+        for i, part in enumerate(parts):
+            copies.append(send(part, part, cs.at[i, z], cr.at[i, z], core))
+    for k in range(nz):
+        z = lax.rem(iz + k, nz)
+        arrived(info_out.at[z, 1 - iy], ps.at[z], zr.at[z, 1 - iy], across_y)
+    for z in range(nz):
+        for y in (0, 1):
+            for x in (0, 1):
+                for h in (0, 1):
+                    arrived(rows_of(h, z, y, x, 1 - ic), fs.at[h, z, y, x], fr.at[h, z, y, x], core)
+    for z in range(nz):
+        for i, part in enumerate(head_parts(z, 1 - ic)):
+            arrived(part, cs.at[i, z], cr.at[i, z], core)
+    arrived(bias_out, ms.at[0], mr.at[0], core)
+    gather.end()
+    for k in range(nz):
+        z = lax.rem(iz + k, nz)
+        sent_head(nz, k, [joined_in.at[:, lanes(z, cols)], dense_in.at[lanes(z, heads)]], js, jr)
+    for copy in copies:
+        copy.wait_send()
+
+
+def front(nz, residual, info, bias, joined_in, dense_in):
+    held, width = residual.shape
+    half = held // 8
+    depth, cols = joined_in.shape[0], joined_in.shape[1] // nz
+    heads = dense_in.shape[0] // nz
+    dma = pltpu.SemaphoreType.DMA
+    outs = pl.pallas_call(
+        functools.partial(front_kernel, nz, half),
+        out_shape=[
+            jax.ShapeDtypeStruct((nz, 2, 2, 2, 2 * half, width), BF16),
+            jax.ShapeDtypeStruct((nz, 2) + info.shape, F32),
+            jax.ShapeDtypeStruct(bias.shape, F32),
+            jax.ShapeDtypeStruct((2 * nz * depth, cols), BF16),
+            jax.ShapeDtypeStruct((heads, 2 * nz * depth), BF16),
+        ],
+        in_specs=[anywhere(), vmem(), vmem(), anywhere(), anywhere()],
+        out_specs=[anywhere(), vmem(), vmem(), anywhere(), anywhere()],
+        scratch_shapes=[
+            dma((2, nz, 2, 2)),
+            dma((2, nz, 2, 2)),
+            dma((2, nz)),
+            dma((2, nz)),
+            dma((2,)),
+            dma((2, nz)),
+            dma((2, nz)),
+            dma((1,)),
+            dma((1,)),
+            dma((nz,)),
+            dma((nz, 2)),
+            dma((nz,)),
+        ]
+        + Gather.scratch(nz),
+        compiler_params=comm(1, 16),
+    )(residual, info, bias, joined_in, dense_in)
+    natural = outs[0].reshape(8 * nz * 2 * half, width)
+    return natural, outs[1].reshape((2 * nz,) + info.shape), outs[2], outs[3], outs[4]
+
+
+def end_kernel(
+    nz,
+    half,
+    part,
+    mine_rows,
+    other_rows,
+    rows,
+    vectors,
+    keep,
+    give,
+    joined_in,
+    dense_in,
+    rows_out,
+    vectors_out,
+    bias_out,
+    joined_out,
+    dense_out,
+    merged,
+    came,
+    rows_in,
+    vector_in,
+    vector_sum,
+    give_in,
+    joined_came,
+    joined_sum,
+    dense_came,
+    dense_sum,
+    ms,
+    mr,
+    vs,
+    vr,
+    bs,
+    br,
+    bp,
+    js,
+    jr,
+    jl,
+    cs,
+    cr,
+    os,
+    orr,
+    *refs,
+):
+    iz, iy, ix, ic = here()
+    core = other_core()
+    across_x, across_y = (iz, iy, 1 - ix, ic), (iz, 1 - iy, ix, ic)
+    greet(neighbours(nz) + [core] + diagonal(nz))
+    reduce = Reduce(nz, half, merged, refs)
+    copies = []
+    depth = joined_in.shape[0] // (2 * nz)
+    cols = joined_in.shape[1]
+    heads = dense_in.shape[0]
+    groups = [(1 - iy, 1 - ix), (iy, 1 - ix), (1 - iy, ix), (iy, ix)]
+
+    for y, x in groups:
+        for k in list(range(1, nz)) + [0]:
+            z = lax.rem(iz + k, nz)
+            copies.append(
+                send(part.at[z, y, x, 1 - ic], came.at[z, y, x], ms.at[z, y, x], mr.at[z, y, x], core)
+            )
+    copies.append(send(vectors, vector_in.at[0], vs.at[0], vr.at[0], core))
+    copies.append(send(give, give_in, bs.at[0], br.at[nz, 0], core))
+    copies.append(send(other_rows, rows_in, os.at[0], orr.at[0], core))
+    for k in range(nz):
+        z = lax.rem(iz + k, nz)
+        theirs = z * 2 + 1 - ic
+        copies.append(
+            send(joined_in.at[lanes(theirs, depth)], joined_came.at[z], cs.at[0, z], cr.at[0, z], core)
+        )
+        copies.append(
+            send(dense_in.at[:, lanes(theirs, depth)], dense_came.at[z], cs.at[1, z], cr.at[1, z], core)
+        )
+
+    def merge_group(y, x):
+        for k in list(range(1, nz)) + [0]:
+            z = lax.rem(iz + k, nz)
+            arrived(came.at[z, y, x], ms.at[z, y, x], mr.at[z, y, x], core)
+            merged[z, y, x] = (part[z, y, x, ic].astype(F32) + came[z, y, x].astype(F32)).astype(BF16)
+
+    merge_group(*groups[0])
+    reduce.start(0, True)
+    merge_group(*groups[1])
+    reduce.start(0, False)
+    merge_group(*groups[2])
+    reduce.start(1, True)
+    reduce.start(1, False)
+    merge_group(*groups[3])
+
+    arrived(vector_in.at[0], vs.at[0], vr.at[0], core)
+    vector_sum[0] = vectors[...] + vector_in[0]
+    copies.append(send(vector_sum.at[0], vector_in.at[1], vs.at[1], vr.at[1], across_x))
+    arrived(give_in, bs.at[0], br.at[nz, 0], core)
+    bias_out[iz, iy] = keep[...] + give_in[...]
+    for k in range(1, nz):
+        far = (lax.rem(iz + k, nz), iy, ix, ic)
+        copies.append(send(bias_out.at[iz, iy], bias_out.at[iz, iy], bs.at[k], br.at[iz, iy], far))
+    copies.append(send(bias_out.at[iz, iy], bias_out.at[iz, iy], bp.at[iz], br.at[iz, iy], across_y))
+
+    for k in list(range(1, nz)) + [0]:
+        z = lax.rem(iz + k, nz)
+        ours = z * 2 + ic
+        arrived(joined_came.at[z], cs.at[0, z], cr.at[0, z], core)
+        joined_sum[z] = (joined_in[lanes(ours, depth)].astype(F32) + joined_came[z].astype(F32)).astype(BF16)
+        arrived(dense_came.at[z], cs.at[1, z], cr.at[1, z], core)
+        dense_sum[z] = (dense_in[:, lanes(ours, depth)].astype(F32) + dense_came[z].astype(F32)).astype(BF16)
+        to_head(
+            nz,
+            k,
+            [
+                (joined_sum.at[z], joined_out.at[:, lanes(iz, cols)]),
+                (dense_sum.at[z], dense_out.at[lanes(iz, heads)]),
+            ],
+            jl,
+            js,
+            jr,
+        )
+
+    for h in (0, 1):
+        reduce.second(h)
+    arrived(vector_in.at[1], vs.at[1], vr.at[1], across_x)
+    vector_sum[1] = vector_sum[0] + vector_in[1]
+    copies.append(send(vector_sum.at[1], vector_in.at[2], vs.at[2], vr.at[2], across_y))
+    for k in range(1, nz):
+        z = lax.rem(iz + k, nz)
+        arrived(bias_out.at[z, iy], bs.at[k], br.at[z, iy], across_y)
+        copies.append(send(bias_out.at[z, iy], bias_out.at[z, iy], bp.at[z], br.at[z, iy], across_y))
+    kept = [reduce.third(h) for h in (0, 1)]
+    arrived(vector_in.at[2], vs.at[2], vr.at[2], across_y)
+    vector_sum[2] = vector_sum[1] + vector_in[2]
+    for k in range(1, nz):
+        far = (lax.rem(iz + k, nz), iy, ix, ic)
+        copies.append(send(vector_sum.at[2], vector_in.at[3 + iz], vs.at[2 + k], vr.at[3 + iz], far))
+    vector_in[3 + iz] = vector_sum[2]
+    arrived(rows_in, os.at[0], orr.at[0], core)
+    for h in (0, 1):
+        at = pl.ds(h * half, half)
+        hat, inverse = normed(rows[at].astype(F32))
+        back = norm_back(reduce.finish(h, kept[h]), hat, inverse)
+        block = rows_out.at[ix, ic, at]
+        rows_out[ix, ic, at] = (
+            mine_rows[at].astype(F32) + rows_in[at].astype(F32) + back
+        ).astype(BF16)
+        copies.append(send(block, block, os.at[1 + h], orr.at[1 + h], across_x))
+        copies.append(send(block, block, os.at[3 + h], orr.at[3 + h], core))
+    for h in (0, 1):
+        block = rows_out.at[1 - ix, ic, pl.ds(h * half, half)]
+        arrived(block, os.at[1 + h], orr.at[1 + h], across_x)
+        copies.append(send(block, block, os.at[5 + h], orr.at[5 + h], core))
+    for k in range(1, nz):
+        z = lax.rem(iz + k, nz)
+        arrived(vector_in.at[3 + z], vs.at[2 + k], vr.at[3 + z], (z, iy, ix, ic))
+    total = vector_in[3]
+    for z in range(1, nz):
+        total = total + vector_in[3 + z]
+    vectors_out[...] = total
+    for k in range(nz):
+        z = lax.rem(iz + k, nz)
+        arrived(bias_out.at[z, 1 - iy], bp.at[z], br.at[z, 1 - iy], across_y)
+        from_head(
+            nz, k, [joined_out.at[:, lanes(z, cols)], dense_out.at[lanes(z, heads)]], js, jr
+        )
+        sent_head(nz, k, [joined_sum.at[z], dense_sum.at[z]], js, jr)
+    for h in (0, 1):
+        at = pl.ds(h * half, half)
+        arrived(rows_out.at[ix, 1 - ic, at], os.at[3 + h], orr.at[3 + h], core)
+        arrived(rows_out.at[1 - ix, 1 - ic, at], os.at[5 + h], orr.at[5 + h], core)
+    for copy in copies + reduce.copies:
+        copy.wait_send()
+
+
+def end(nz, part, mine_rows, other_rows, rows, vectors, keep, give, joined_in, dense_in):
+    share, width = rows.shape
+    half = share // 2
+    depth, cols, heads = joined_in.shape[0] // (2 * nz), joined_in.shape[1], dense_in.shape[0]
+    dma = pltpu.SemaphoreType.DMA
+    return pl.pallas_call(
+        functools.partial(end_kernel, nz, half),
+        out_shape=[
+            jax.ShapeDtypeStruct((2, 2, share, width), BF16),
+            jax.ShapeDtypeStruct(vectors.shape, F32),
+            jax.ShapeDtypeStruct((nz, 2) + keep.shape, F32),
+            jax.ShapeDtypeStruct((depth, nz * cols), BF16),
+            jax.ShapeDtypeStruct((nz * heads, depth), BF16),
+        ],
+        in_specs=[vmem()] * 9,
+        out_specs=[vmem(), vmem(), vmem(), vmem(), vmem()],
+        scratch_shapes=[
+            pltpu.VMEM((nz, 2, 2, share, width), BF16),
+            pltpu.VMEM((nz, 2, 2, share, width), BF16),
+            pltpu.VMEM((share, width), BF16),
+            pltpu.VMEM((3 + nz,) + vectors.shape, F32),
+            pltpu.VMEM((3,) + vectors.shape, F32),
+            pltpu.VMEM(keep.shape, F32),
+            pltpu.VMEM((nz, depth, cols), BF16),
+            pltpu.VMEM((nz, depth, cols), BF16),
+            pltpu.VMEM((nz, heads, depth), BF16),
+            pltpu.VMEM((nz, heads, depth), BF16),
+            dma((nz, 2, 2)),
+            dma((nz, 2, 2)),
+            dma((2 + nz,)),
+            dma((3 + nz,)),
+            dma((nz,)),
+            dma((nz + 1, 2)),
+            dma((nz,)),
+            dma((2, nz)),
+            dma((2, nz)),
+            dma((2,)),
+            dma((2, nz)),
+            dma((2, nz)),
+            dma((7,)),
+            dma((7,)),
+        ]
+        + Reduce.scratch(nz, half, width),
+        compiler_params=comm(5),
+    )(part, mine_rows, other_rows, rows, vectors, keep, give, joined_in, dense_in)
+
+
+def fast_shards(
+    residual,
+    lengths,
+    pair_order,
+    token_ids,
+    desirable,
+    ref_match,
+    ref_pair,
+    attn_gain,
+    attn_shift,
+    mlp_gain,
+    mlp_shift,
+    w_joined,
+    b_joined,
+    w_dense,
+    b_dense,
+    w_up,
+    b_up,
+    w_down,
+    b_down,
+    final_gain,
+    final_shift,
+    w_vocab,
+):
+    nz, ny, nx = lax.axis_size("z"), lax.axis_size("y"), lax.axis_size("x")
+    n = nz * ny
+    chips = n * nx
+    iz, iy, ix, ic = (lax.axis_index(a) for a in ALL)
+    dp = iz * ny + iy
+    held, width = residual.shape
+    total = n * held
+    blocks = 2 * n
+    piece = held // 2
+    seqs = lengths.shape[1]
+    depth = width // n
+    vcols = w_vocab.shape[1] // n
+    ffs = w_up.shape[1] // n
+    hcols = 3 * HD
+    mine = ix * 2 + ic
+
+    info = jnp.stack(
+        [
+            token_ids.astype(F32),
+            ref_match,
+            ref_pair,
+            jnp.concatenate(
+                [lengths[0].astype(F32), desirable.astype(F32), jnp.zeros((held - 2 * seqs,), F32)]
+            ),
+        ]
+    )
+    bias_own = jnp.concatenate([b_joined, b_up]).astype(F32)
+    natural, info, bias_other, wj, wd = front(nz, residual, info, bias_own.reshape(-1, HD), w_joined, w_dense)
+    bias_other = bias_other.reshape(-1)
+
+    send_up = w_up.reshape(depth, n, ffs).transpose(1, 0, 2)
+    send_down = w_down.reshape(n, ffs, depth)
+    send_vocab = w_vocab.reshape(depth, n, vcols).transpose(1, 0, 2)
+    up_own = exchange(send_up).reshape(width, ffs)
+    down_own = exchange(send_down).transpose(1, 0, 2).reshape(ffs, width)
+    vocab_own = exchange(send_vocab).reshape(width, vcols)
+    up_other, down_other, vocab_other = swap(up_own), swap(down_own), swap(vocab_own)
+    wup = jnp.concatenate([up_own, up_other], axis=1)
+    wout = jnp.concatenate([wd, down_own, down_other], axis=0)
+    bias_first = jnp.where(ic == 0, bias_own, bias_other)
+    bias_second = jnp.where(ic == 0, bias_other, bias_own)
+    bj_all = jnp.where(iy == 0, bias_first, bias_second)[: nz * hcols].reshape(nz, hcols)
+    bj = lax.dynamic_index_in_dim(bj_all, iz, 0, keepdims=False)
+    bu_all = jnp.stack([bias_own[nz * hcols :], bias_other[nz * hcols :]]).reshape(2, n, ffs)
+    bu = lax.dynamic_index_in_dim(bu_all, dp, 1, keepdims=False).reshape(2 * ffs)
+
+    ids = info[:, 0].astype(jnp.int32)
+    refs = jnp.stack([info[:, 1], info[:, 2]])
+    lens = info[:, 3, :seqs].astype(jnp.int32)
+    wanted = info[:, 3, seqs : 2 * seqs]
+    slots = jnp.arange(blocks, dtype=jnp.int32)
+    anchor = jnp.sum(
+        jnp.where(pair_order[None, :] == slots[:, None], slots[None, :], 0), axis=1
+    )
+    order = jnp.where(ic == 0, slots, anchor)
+    back = jnp.where(ic == 0, slots, pair_order)
+    rows_low = take_blocks(natural, order, piece)
+    anchor_hot = (anchor[:, None] == slots[None, :])[:, :, None]
+    pair_ids = jnp.sum(jnp.where(anchor_hot, ids.reshape(1, blocks, piece), 0), axis=1).reshape(n, held)
+    all_ids = jnp.stack([ids, pair_ids])
+
+    ends = jnp.stack([jnp.sum(lens[:, : s + 1], axis=1) for s in range(seqs)], axis=1)
+    starts = ends - lens
+    places = jnp.arange(held, dtype=jnp.int32)
+    segment = jnp.sum((places[None, :, None] >= ends[:, None, :]).astype(jnp.int32), axis=2)
+    hot = (segment[:, :, None] == jnp.arange(seqs, dtype=jnp.int32)).astype(F32)
+    position = places[None, :] - jnp.sum(hot * starts[:, None, :].astype(F32), axis=2).astype(jnp.int32)
+    allowed = (segment[:, :, None] == segment[:, None, :]) & (places[None, :, None] >= places[None, None, :])
+    scored = jnp.concatenate(
+        [segment[:, 1:] == segment[:, :-1], jnp.zeros((n, 1), jnp.bool_)], axis=1
+    ).astype(F32)
+    targets = jnp.concatenate([all_ids[:, :, 1:], jnp.zeros((2, n, 1), jnp.int32)], axis=2)
+
+    rows_float = rows_low.astype(F32)
+    hat, inverse = normed(rows_float)
+    ga, sa, gm, sm, gf, sf = (
+        v.astype(F32) for v in (attn_gain, attn_shift, mlp_gain, mlp_shift, final_gain, final_shift)
+    )
+    attn_low = (hat * ga + sa).astype(BF16)
+    mlp_low = (hat * gm + sm).astype(BF16)
+    frequency = jnp.exp(jnp.arange(ROT // 2, dtype=F32) * (-2.0 * math.log(10000.0) / ROT))
+    angles = position.reshape(total)[:, None].astype(F32) * frequency[None, :]
+    cosine, sine = jnp.cos(angles), jnp.sin(angles)
+    fused = dot(attn_low, wj, (1, 0)) + bj
+    query = turn(fused[:, :HD], cosine, sine).astype(BF16)
+    keys = turn(fused[:, HD : 2 * HD], cosine, sine).astype(BF16)
+    values = fused[:, 2 * HD :].astype(BF16)
+    q3, k3, v3 = (a.reshape(n, held, HD) for a in (query, keys, values))
+    scores = jnp.einsum("grd,gcd->grc", q3, k3, preferred_element_type=F32) / math.sqrt(HD)
+    scores = jnp.where(allowed, scores, masked_score)
+    highest = jnp.max(scores, axis=-1, keepdims=True)
+    weights = jnp.exp(scores - highest)
+    probs = weights / jnp.sum(weights, axis=-1, keepdims=True)
+    probs_low = probs.astype(BF16)
+    mixed = (
+        jnp.einsum("grc,gcd->grd", probs_low, v3, preferred_element_type=F32)
+        .astype(BF16)
+        .reshape(total, HD)
+    )
+    hidden = dot(mlp_low, wup, (1, 0)) + bu
+    bell = 0.5 * (1.0 + lax.erf(hidden * math.sqrt(0.5)))
+    active = (hidden * bell).astype(BF16)
+    outs_low = jnp.concatenate([mixed, active], axis=1)
+    branch_part = dot(outs_low, wout, (1, 0)).astype(BF16)
+    share = total // chips
+    chip = dp * nx + ix
+    rows_here = lax.dynamic_slice_in_dim(rows_low, chip * share, share, 0)
+    bias_out = (b_dense.astype(F32) + b_down.astype(F32))[None]
+    final, resid = reduce_norm_gather(nz, branch_part, rows_here, bias_out, gf[None], sf[None])
+
+    my_targets = jnp.where(ic == 0, targets[0], targets[1]).reshape(total)
+    logits = [dot(final, w, (1, 0)) for w in (vocab_own, vocab_other)]
+    hits = [
+        lax.broadcasted_iota(jnp.int32, (total, vcols), 1)
+        == (my_targets - ((ix * 2 + core) * n + dp) * vcols)[:, None]
+        for core in (ic, 1 - ic)
+    ]
+    tops = [jnp.max(part, axis=1) for part in logits]
+    top = jnp.maximum(tops[0], tops[1])
+    sums = sum(jnp.sum(jnp.exp(part - top[:, None]), axis=1) for part in logits)
+    picks = sum(jnp.sum(jnp.where(h, part, 0.0), axis=1) for h, part in zip(hits, logits))
+    stats = jnp.stack([top, sums, picks]).reshape(3, n, held)
+    coef, my_lse, scalars = objective(
+        nz, n * seqs, stats, hot.transpose(2, 0, 1), scored, refs, lens.astype(F32), wanted
+    )
+    coef, my_lse = coef.reshape(total), my_lse.reshape(total)
+    kto_loss, kl_estimate = scalars[0, 0, 0], scalars[1, 0, 0]
+
+    dlogits = [
+        (coef[:, None] * (jnp.where(h, 1.0, 0.0) - jnp.exp(part - my_lse[:, None]))).astype(BF16)
+        for h, part in zip(hits, logits)
+    ]
+    gv_own = dot(final, dlogits[0], (0, 0))
+    gv_other = dot(final, dlogits[1], (0, 0)).astype(BF16)
+    dfinal_part = (dot(dlogits[0], vocab_own, (1, 1)) + dot(dlogits[1], vocab_other, (1, 1))).astype(BF16)
+    dbranch, final_vectors = reduce_back_gather(nz, dfinal_part, resid, gf[None])
+    gv = (gv_own + swap(gv_other).astype(F32)).astype(BF16)
+    grad_vocab = (
+        exchange(gv.reshape(n, depth, vcols)).transpose(1, 0, 2).reshape(depth, n * vcols).astype(F32)
+    )
+
+    gout = dot(outs_low, dbranch, (0, 0))
+    douts = dot(dbranch, wout, (1, 1))
+    dmixed = douts[:, :HD].astype(BF16).reshape(n, held, HD)
+    slope_of = bell + hidden * jnp.exp(-0.5 * hidden * hidden) * (1.0 / math.sqrt(2.0 * math.pi))
+    dhidden = (douts[:, HD:] * slope_of).astype(BF16)
+    dvalues = jnp.einsum("grc,grd->gcd", probs_low, dmixed, preferred_element_type=F32)
+    dprobs = jnp.einsum("grd,gcd->grc", dmixed, v3, preferred_element_type=F32)
+    dscores = (probs * (dprobs - jnp.sum(probs * dprobs, axis=-1, keepdims=True))).astype(BF16)
+    dquery = jnp.einsum("grc,gcd->grd", dscores, k3, preferred_element_type=F32) / math.sqrt(HD)
+    dkeys = jnp.einsum("grc,grd->gcd", dscores, q3, preferred_element_type=F32) / math.sqrt(HD)
+    dfused = jnp.concatenate(
+        [
+            turn(dquery.reshape(total, HD), cosine, -sine),
+            turn(dkeys.reshape(total, HD), cosine, -sine),
+            dvalues.reshape(total, HD),
+        ],
+        axis=1,
+    ).astype(BF16)
+    gj = dot(attn_low, dfused, (0, 0)).astype(BF16)
+    gu = dot(mlp_low, dhidden, (0, 0))
+    dattn = dot(dfused, wj, (1, 1))
+    dmlp = dot(dhidden, wup, (1, 1))
+    g_attn_gain = jnp.sum(dattn * hat, axis=0)
+    g_attn_shift = jnp.sum(dattn, axis=0)
+    g_mlp_gain = jnp.sum(dmlp * hat, axis=0)
+    g_mlp_shift = jnp.sum(dmlp, axis=0)
+    t_part = (dattn * ga + dmlp * gm).astype(BF16)
+    t_part = take_blocks(t_part, back, piece)
+
+    gout_low = gout.astype(BF16)
+    gu_low = gu.astype(BF16)
+    gdown = gout[HD : HD + ffs] + swap(gout_low[HD + ffs :]).astype(F32)
+    gup = gu[:, :ffs] + swap(gu_low[:, ffs:]).astype(F32)
+    grad_down = exchange(
+        gdown.astype(BF16).reshape(ffs, n, depth).transpose(1, 0, 2)
+    ).reshape(n * ffs, depth).astype(F32)
+    grad_up = (
+        exchange(gup.astype(BF16).reshape(n, depth, ffs)).transpose(1, 0, 2).reshape(depth, n * ffs).astype(F32)
+    )
+
+    share2 = total // (2 * chips)
+
+    def natural_rows(core):
+        first = dp * held + (ix * 2 + core) * share2
+        place = jnp.sum(jnp.where(slots == first // piece, back, 0)) * piece + first % piece
+        return lax.dynamic_slice_in_dim(dbranch, place, share2, 0)
+
+    gbj = jnp.sum(dfused.astype(F32), axis=0)
+    gbu = jnp.sum(dhidden.astype(F32), axis=0)
+    spare = jnp.zeros((8 * HD - hcols - ffs,), F32)
+    keep = jnp.concatenate([gbj, gbu[:ffs], spare]).reshape(8, HD)
+    give = jnp.concatenate([gbj, gbu[ffs:], spare]).reshape(8, HD)
+    vectors = jnp.concatenate(
+        [
+            jnp.stack([g_attn_gain, g_attn_shift, g_mlp_gain, g_mlp_shift]),
+            final_vectors,
+            jnp.zeros((1, width), F32),
+        ]
+    )
+    rows_out, vectors, biases, grad_joined, grad_dense = end(
+        nz,
+        t_part.reshape(nz, 2, 2, 2, share2, width),
+        natural_rows(ic),
+        natural_rows(1 - ic),
+        lax.dynamic_slice_in_dim(residual, mine * share2, share2, 0),
+        vectors,
+        keep,
+        give,
+        gj,
+        gout_low[:HD],
+    )
+    grad_input = rows_out.reshape(held, width).astype(F32)
+    grad_joined, grad_dense = grad_joined.astype(F32), grad_dense.astype(F32)
+    g_attn_gain, g_attn_shift, g_mlp_gain, g_mlp_shift, g_final_gain, g_final_shift, g_out = vectors[:7]
+    biases = biases.reshape(nz, 2, 8 * HD)
+    gb_joined = jnp.where(ic == 0, biases[:, 0, :hcols], biases[:, 1, :hcols]).reshape(nz * hcols)
+    gb_up = biases[:, :, hcols : hcols + ffs].reshape(n * ffs)
+    return (
+        kto_loss,
+        kl_estimate,
+        grad_input,
+        g_attn_gain,
+        g_attn_shift,
+        g_mlp_gain,
+        g_mlp_shift,
+        grad_joined,
+        gb_joined,
+        grad_dense,
+        g_out,
+        grad_up,
+        gb_up,
+        grad_down,
+        g_out,
+        g_final_gain,
+        g_final_shift,
+        grad_vocab,
+    )
+
+
+def placed(dp, mp):
+    ins = (
+        P(dp, None),
+        P(dp, None),
+        P(),
+        P(dp),
+        P(dp),
+        P(dp),
+        P(dp),
+        P(),
+        P(),
+        P(),
+        P(),
+        P(dp, mp),
+        P(mp),
+        P(mp, dp),
+        P(),
+        P(dp, mp),
+        P(mp),
+        P(mp, dp),
+        P(),
+        P(),
+        P(),
+        P(dp, mp),
+    )
+    outs = (
+        P(),
+        P(),
+        P(dp, None),
+        P(),
+        P(),
+        P(),
+        P(),
+        P(dp, mp),
+        P(mp),
+        P(mp, dp),
+        P(),
+        P(dp, mp),
+        P(mp),
+        P(mp, dp),
+        P(),
+        P(),
+        P(),
+        P(dp, mp),
+    )
+    return ins, outs
+
+
 def solution(mesh):
-    return jax.shard_map(
-        shards,
-        mesh=mesh,
-        in_specs=(
-            P("dp", None),
-            P("dp", None),
-            P(),
-            P("dp"),
-            P("dp"),
-            P("dp"),
-            P("dp"),
-            P(),
-            P(),
-            P(),
-            P(),
-            P("dp", "mp"),
-            P("mp"),
-            P("mp", "dp"),
-            P(),
-            P("dp", "mp"),
-            P("mp"),
-            P("mp", "dp"),
-            P(),
-            P(),
-            P(),
-            P("dp", "mp"),
-        ),
-        out_specs=(
-            P(),
-            P(),
-            P("dp", None),
-            P(),
-            P(),
-            P(),
-            P(),
-            P("dp", "mp"),
-            P("mp"),
-            P("mp", "dp"),
-            P(),
-            P("dp", "mp"),
-            P("mp"),
-            P("mp", "dp"),
-            P(),
-            P(),
-            P(),
-            P("dp", "mp"),
-        ),
-        check_vma=False,
-    )
+    n_dp, n_mp = mesh.shape["dp"], mesh.shape["mp"]
+    if n_dp == 8 and n_mp == 4:
+        fine = jax.sharding.Mesh(mesh.devices.reshape(n_dp // 2, 2, n_mp // 2, 2), ALL)
+        ins, outs = placed(DP, ("x", "c"))
+        return jax.shard_map(fast_shards, mesh=fine, in_specs=ins, out_specs=outs, check_vma=False)
+    ins, outs = placed("dp", "mp")
+    return jax.shard_map(shards, mesh=mesh, in_specs=ins, out_specs=outs, check_vma=False)

time: 3180 us -> 726 us (0.23)
  waiting for transfers between devices: 2630 us -> 45.4 us
  Pallas kernels: 0 us -> 435 us
  blocking collectives: 284 us -> 0 us
  matrix products: 143 us -> 97.5 us
    reduce_scatter x5 -> x0, waiting for transfers between devices: 1580 us -> none  [the longest x1 825 us: shards(): lax.psum_scatter(grad_vocab, 'dp', scatter_dimension=0, tiled=True)]
    all_gather x5 -> x0, waiting for transfers between devices: 766 us -> none  [the longest x1 499 us: gather_weights(): lax.all_gather(w_vocab, 'dp', axis=0, tiled=True)]
    pallas_call x0 -> x7, Pallas kernels: none -> 435 us  [the longest x1 119 us: front(): pl.pallas_call(functools.partial(front_kernel, nz, half), out_shape=[jax....]
    psum x3 -> x0, blocking collectives: 268 us -> none  [the longest x2 251 us: shards(): lax.psum((jnp.sum(1.0 - sigmoid_val), jnp.sum(slope)), 'dp')]
    psum x3 -> x0, waiting for transfers between devices: 125 us -> none  [the longest x1 56.6 us: shards(): dfinal = lax.psum(dfinal_part, 'mp')]
    all_to_all x3 -> x6, waiting for transfers between devices: 155 us -> 45.3 us  [exchange(): return lax.all_to_all(value, DP, split_axis=0, concat_axis=0, tiled=True)]
    dot_general x23 -> x20, matrix products: 143 us -> 95.2 us  [the longest x15 87.6 us: dot(): lax.dot_general(a, b, ((contract[:1], contract[1:]), ((), ())), preferred...]
  transfers between devices with their start and end apart: 16 -> 12, of which waited for: 13 -> 4; matrix products, arithmetic and copies ran while one was open for 4% -> 19% of each run, Pallas kernels for 0% -> 44%
where the time goes in v1:
time: 726 us; the launch traced here: 718 us
  Pallas kernels  435 us (60%)
  matrix products  97.5 us (13%)
  local copies, waits for them, and re-layouts  62 us (9%)
  waiting for transfers between devices  45.4 us (6%)
  starting transfers between devices  39.3 us (5%)
  other arithmetic  35.5 us (5%)
    pallas_call x1, Pallas kernels, front(): pl.pallas_call(functools.partial(front_kernel, nz, half), out_shape=[jax....  119 us
    pallas_call x1, Pallas kernels, reduce_norm_gather(): pl.pallas_call(functools.partial(forward_kernel, nz, half), out_shape=[ja...  95.8 us
    pallas_call x1, Pallas kernels, reduce_back_gather(): pl.pallas_call(functools.partial(backward_kernel, nz, half), out_shape=[j...  95.5 us
    dot_general x15, matrix products, dot(): lax.dot_general(a, b, ((contract[:1], contract[1:]), ((), ())), preferred...  87.6 us
    pallas_call x1, Pallas kernels, end(): pl.pallas_call(functools.partial(end_kernel, nz, half), out_shape=[jax.Sh...  81.4 us
    all_to_all x6, waiting for transfers between devices, exchange(): return lax.all_to_all(value, DP, split_axis=0, concat_axis=0, tiled=True)  45.3 us
    all_to_all x6, starting transfers between devices, exchange(): return lax.all_to_all(value, DP, split_axis=0, concat_axis=0, tiled=True)  35.8 us
    unnamed x132, local copies, waits for them, and re-layouts  25.3 us
  transfers between devices with their start and end apart: 12, of which 4 were waited for; matrix products, arithmetic and copies ran while one was open for 19% of the time, Pallas kernels for 44%

profile of v1, /device:TPU:1, one launch (start us, length us, event | category | flops | bytes accessed | tf_op | source)
XLA Modules:
  0.0 718.0 jit_solution(7514234607209129866)
XLA Ops:
  0.7 2.3 copy.209
  2.9 6.4 all-to-all-start
  9.4 5.6 copy.213
  15.0 18.9 %all-to-all-done = bf16[8,256,256]{1,2,0:T(8,128)(2,1)S(1)} async-done(((bf16[8,256,256]{1,2,0:T(8,128)(2,1)}), bf16[8,256,256]{1,2,0:T(8,128)(2,1)S(1)}, u32[]{:S(2)}, u32[]{:S(2)}) %all-to-all-start) | async-done | bytes 1048608 | tf_op jit(solution)/shard_map/all_to_all | solution.py:477
  34.9 5.1 all-to-all-start.2
  40.2 119.2 %shard_map.349 = (bf16[4,2,2,2,32,2048]{5,4,3,2,1,0:T(8,128)(2,1)S(1)}, f32[4,2,4,128]{3,2,1,0:T(4,128)S(1)}, f32[28,128]{1,0:T(8,128)S(1)}, bf16[2048,384]{1,0:T(8,128)(2,1)S(1)}, bf16[128,2048]{1,0:T(8,128)(2,1)S(1)}) custom-call(bf16[128,2048]{1,0:T(8,128)(2,1)S(1)} %copy-done.1, f32[4,128]{1,0:T(4,128)S(1)} %pad_maximum_fusion.17.info, ...), custom_call_target="tpu_custom_call" | custom-call | tf_op jit(solution)/shard_map/pallas_call | solution.py:1112
  159.4 2.0 copy-done
  163.9 10.8 %shard_map.350 = bf16[1024,2048]{1,0:T(8,128)(2,1)} custom-call(s32[16]{0:T(128)} %broadcast_select_fusion.2.order_ref, bf16[1024,2048]{1,0:T(8,128)(2,1)} %bitcast.162), custom_call_target="tpu_custom_call" | custom-call | tf_op jit(solution)/shard_map/pallas_call | solution.py:464
  175.0 3.0 convert_reduce_fusion
  178.2 1.2 fusion.13
  179.5 4.3 fusion.8
  183.8 3.0 fusion.94
  187.5 4.5 all-to-all-start.1
  192.0 1.3 fusion.63
  194.9 4.1 copy.248
  200.7 2.4 copy.210
  204.3 2.3 fusion.95
  206.6 11.1 %all-to-all-done.1 = bf16[8,256,256]{2,1,0:T(8,128)(2,1)} async-done(((bf16[8,256,256]{2,1,0:T(8,128)(2,1)}), bf16[8,256,256]{2,1,0:T(8,128)(2,1)}, u32[]{:S(2)}, u32[]{:S(2)}) %all-to-all-start.1) | async-done | bytes 1048608 | tf_op jit(solution)/shard_map/all_to_all | solution.py:477
  217.7 2.3 copy.211
  221.1 1.7 slice.200
  223.8 1.9 copy.245
  225.7 2.6 convolution_convert_fusion.4
  228.4 6.4 multiply_convert_fusion.2
  234.8 6.6 convolution_convert_fusion
  241.4 95.8 %shard_map.351 = (bf16[4,2,2,64,2048]{4,3,2,1,0:T(8,128)(2,1)S(1)}, f32[64,2048]{1,0:T(8,128)S(1)}) custom-call(bf16[4,2,2,64,2048]{4,3,2,1,0:T(8,128)(2,1)} %bitcast.188, bf16[64,2048]{1,0:T(8,128)(2,1)S(1)} %constant_dynamic-slice_fusion.3.rows, f32[1,2048]{1,0:T(1,128)S(1)} %bitcast.165, f32[1,2048]{1,0:T(1,128)S(1)} %bitcast.163, f32[1,2048]{1,0:T(1,128)S(1)} %bitcast.166), custom_call_target="tpu_custom_call" | custom-call | tf_op jit(solution)/shard_map/pallas_call | solution.py:800
  337.2 7.0 fusion.96
  344.3 6.7 fusion.97
  351.0 1.7 exponential_reduce_fusion
  352.7 21.2 %shard_map.352 = (f32[8,128]{1,0:T(8,128)S(1)}, f32[8,128]{1,0:T(8,128)S(1)}, f32[2,8,128]{2,1,0:T(8,128)S(1)}) custom-call(f32[3,8,128]{2,1,0:T(8,128)S(1)} %pad_maximum_fusion.11.stats, f32[3,8,128]{2,1,0:T(8,128)S(1)} %fusion.66.hot, f32[8,128]{1,0:T(8,128)S(1)} %pad_convert_fusion.scored, f32[2,8,128]{2,1,0:T(8,128)S(1)} %pad_maximum_fusion.12.refs, ...), custom_call_target="tpu_custom_call" | custom-call | tf_op jit(solution)/shard_map/pallas_call | solution.py:911
  373.9 6.8 fusion.85
  380.7 8.3 %add_convert_fusion.1 = bf16[1024,2048]{1,0:T(8,128)(2,1)} fusion(f32[1024,2048]{1,0:T(8,128)S(1)} %fusion.85, bf16[2048,800]{0,1:T(8,128)(2,1)} %collective-permute-done.2, f32[1024,800]{0,1:T(8,128)S(1)} %get-tuple-element.192, f32[1024]{0:T(1024)S(1)} %bitcast.180, f32[1024]{0:T(1024)S(1)} %bitcast.176, s32[1024]{0:T(1024)S(1)} %get-tuple-element.172), kind=kOutput, calls=%fused_computation.17 | convolution fusion | flops 3364552704 | bytes 19148800 | tf_op jit(solution)/shard_map/dot_general | solution.py:431
  389.1 95.5 %shard_map.353 = (bf16[4,2,2,64,2048]{4,3,2,1,0:T(8,128)(2,1)S(1)}, f32[3,2048]{1,0:T(4,128)S(1)}) custom-call(bf16[4,2,2,64,2048]{4,3,2,1,0:T(8,128)(2,1)} %bitcast.187, f32[64,2048]{1,0:T(8,128)S(1)} %get-tuple-element.44.resid, f32[1,2048]{1,0:T(1,128)S(1)} %bitcast.164), custom_call_target="tpu_custom_call" | custom-call | tf_op jit(solution)/shard_map/pallas_call | solution.py:819
  484.6 5.6 fusion.29
  490.2 1.7 convert_reduce_fusion.1
  493.7 2.5 fusion.100
  497.4 5.3 convolution_convert_fusion.1
  502.8 1.4 fusion.21
  504.2 10.0 %all-to-all-start.3 = ((bf16[8,256,256]{2,1,0:T(8,128)(2,1)}), bf16[8,256,256]{2,1,0:T(8,128)(2,1)S(1)}, u32[]{:S(2)}, u32[]{:S(2)}) async-start(bf16[8,256,256]{2,1,0:T(8,128)(2,1)} %bitcast.190), calls=%async_computation.3 | async-start | bytes 2097152 | tf_op jit(solution)/shard_map/all_to_all | solution.py:477
  514.2 7.9 %fusion.98 = (bf16[640,2048]{1,0:T(8,128)(2,1)S(1)}, f32[640,2048]{1,0:T(8,128)}) fusion(bf16[1024,2048]{1,0:T(8,128)(2,1)} %bitcast.169, bf16[1024,512]{1,0:T(8,128)(2,1)} %copy-done.62, bf16[1024,128]{1,0:T(8,128)(2,1)} %bitcast.254), kind=kOutput, calls=%fused_computation.205 | convolution fusion | flops 2688286720 | bytes 13369344 | tf_op jit(solution)/shard_map/dot_general | solution.py:431
  522.1 1.5 copy-done.32
  525.4 1.1 fusion.76
  527.9 1.8 slice.284
  530.8 2.1 fusion.20
  534.0 5.4 all-to-all-done.3
  539.4 4.4 all-to-all-start.4
  543.8 1.6 multiply_reduce_fusion
  548.9 7.8 %add_convert_fusion.2 = bf16[2048,800]{0,1:T(8,128)(2,1)S(1)} fusion(bf16[2048,800]{0,1:T(8,128)(2,1)} %collective-permute-done.5, bf16[1024,2048]{1,0:T(8,128)(2,1)} %bitcast.174, f32[1024,800]{0,1:T(8,128)} %copy-done.14, f32[1024]{0:T(1024)S(1)} %bitcast.182, f32[1024]{0:T(1024)S(1)} %bitcast.178, s32[1024]{0:T(1024)} %copy-done.38), kind=kOutput, calls=%fused_computation.18 | convolution fusion | flops 3365273600 | bytes 14036992 | tf_op jit(solution)/shard_map/dot_general | solution.py:431
  556.7 1.9 copy.257
  558.6 9.9 %all-to-all-done.4 = bf16[8,256,256]{2,1,0:T(8,128)(2,1)} async-done(((bf16[8,256,256]{2,1,0:T(8,128)(2,1)}), bf16[8,256,256]{2,1,0:T(8,128)(2,1)}, u32[]{:S(2)}, u32[]{:S(2)}) %all-to-all-start.4) | async-done | bytes 1048608 | tf_op jit(solution)/shard_map/all_to_all | solution.py:477
  568.6 5.3 all-to-all-start.5
  573.9 1.2 fusion.57
  578.5 2.5 convolution_convert_fusion.3
  581.0 3.2 concatenate.74
  584.3 2.4 fusion.99
  587.0 6.8 fusion.86
  593.8 11.0 %shard_map.354 = bf16[1024,2048]{1,0:T(8,128)(2,1)} custom-call(s32[16]{0:T(128)} %get-tuple-element.138.order_ref, bf16[1024,2048]{1,0:T(8,128)(2,1)} %get-tuple-element.139.from_ref), custom_call_target="tpu_custom_call" | custom-call | tf_op jit(solution)/shard_map/pallas_call | solution.py:464
  606.2 4.6 convolution_convert_fusion.2.joined_in
  610.8 81.4 %shard_map.355 = (bf16[2,2,32,2048]{3,2,1,0:T(8,128)(2,1)S(1)}, f32[8,2048]{1,0:T(8,128)S(1)}, f32[4,2,8,128]{3,2,1,0:T(8,128)S(1)}, bf16[256,1536]{1,0:T(8,128)(2,1)S(1)}, bf16[512,256]{1,0:T(8,128)(2,1)S(1)}) custom-call(bf16[4,2,2,2,32,2048]{5,4,3,2,1,0:T(8,128)(2,1)} %bitcast.184, bf16[32,2048]{1,0:T(8,128)(2,1)S(1)} %get-tuple-element.145.mine_rows, ...), custom_call_target="tpu_custom_call" | custom-call | tf_op jit(solution)/shard_map/pallas_call | solution.py:1319
  694.9 1.3 convert_element_type.269
  697.9 1.4 convert_bitcast_fusion
  699.3 1.6 copy.251
  700.9 2.7 bitcast_convert_fusion
  703.6 5.2 convert_element_type.293
  708.8 8.1 %copy.233 = f32[256,6400]{1,0:T(8,128)} copy(f32[256,6400]{0,1:T(8,128)} %bitcast.183) | data formatting | bytes 13107200
  (242 shorter events, 31.9 us)
Async XLA Ops:
  0.7 8.7 %copy-start.58 = (s32[3]{0:T(128)S(1)}, s32[3]{0:T(128)}, u32[]{:S(2)}) copy-start(s32[3]{0:T(128)} %param.26) | copy-start | bytes 40
  2.9 31.0 %all-to-all-start = ((bf16[8,256,256]{1,2,0:T(8,128)(2,1)}), bf16[8,256,256]{1,2,0:T(8,128)(2,1)S(1)}, u32[]{:S(2)}, u32[]{:S(2)}) async-start(bf16[8,256,256]{1,2,0:T(8,128)(2,1)} %bitcast.25), calls=%async_computation | async-start | bytes 2097152 | tf_op jit(solution)/shard_map/all_to_all | solution.py:477
  9.3 5.6 copy-start.59
  9.3 5.6 copy-start.60
  33.9 6.1 copy-start.42
  33.9 6.1 copy-start.43
  33.9 6.1 copy-start.44
  33.9 6.2 copy-start.45
  33.9 6.2 copy-start.56
  34.0 6.2 copy-start.57
  34.0 6.2 copy-start.46
  34.0 6.2 copy-start.47
  34.0 6.2 copy-start.1
  34.0 6.2 copy-start.2
  34.0 6.2 copy-start.5
  34.0 129.0 %copy-start.54 = (s32[16]{0:T(128)S(1)}, s32[16]{0:T(128)}, u32[]{:S(2)}) copy-start(s32[16]{0:T(128)} %param.24) | copy-start | bytes 196
  34.9 152.6 %all-to-all-start.2 = ((bf16[8,256,800]{1,2,0:T(8,128)(2,1)}), bf16[8,256,800]{1,2,0:T(8,128)(2,1)}, u32[]{:S(2)}, u32[]{:S(2)}) async-start(bf16[8,256,800]{1,2,0:T(8,128)(2,1)} %bitcast.186), calls=%async_computation.2 | async-start | bytes 6553600 | tf_op jit(solution)/shard_map/all_to_all | solution.py:477
  174.8 3.5 copy-start.8
  174.8 17.2 %copy-start.52 = (f32[16]{0:T(128)}, f32[16]{0:T(128)S(1)}, u32[]{:S(2)}) copy-start(f32[16]{0:T(128)S(1)} %multiply_exponential_fusion) | copy-start | bytes 196
  186.7 6.6 copy-start.34
  187.5 30.2 %all-to-all-start.1 = ((bf16[8,256,256]{2,1,0:T(8,128)(2,1)}), bf16[8,256,256]{2,1,0:T(8,128)(2,1)}, u32[]{:S(2)}, u32[]{:S(2)}) async-start(bf16[8,256,256]{2,1,0:T(8,128)(2,1)} %bitcast.28), calls=%async_computation.1 | async-start | bytes 2097152 | tf_op jit(solution)/shard_map/all_to_all | solution.py:477
  193.9 31.8 %copy-start.37 = (pred[128,128]{0,1:T(8,128)(4,1)}, pred[128,128]{0,1:T(8,128)(4,1)S(1)}, u32[]{:S(2)}) copy-start(pred[128,128]{0,1:T(8,128)(4,1)S(1)} %iota_compare_fusion.2) | copy-start | bytes 49156
  194.9 5.6 copy-start.33
  194.9 5.8 copy-start.50
  194.9 5.8 copy-start.51
  199.1 145.2 %collective-permute-start.2 = (bf16[2048,800]{0,1:T(8,128)(2,1)}, bf16[2048,800]{0,1:T(8,128)(2,1)}, u32[]{:S(2)}, u32[]{:S(2)}) collective-permute-start(bf16[2048,800]{0,1:T(8,128)(2,1)} %bitcast.87), channel_id=1, source_target_pairs={{0,1},{1,0},{2,3},{3,2},{4,5},{5,4},{6,7},{7,6},{8,9},{9,8},{10,11... | collective-permute-start | bytes 9830408 | tf_op jit(solution)/shard_map/ppermute | solution.py:435
  199.6 20.3 %copy-start.26 = (bf16[1024,16]{1,0:T(8,128)(2,1)}, bf16[1024,16]{1,0:T(8,128)(2,1)S(1)}, u32[]{:S(2)}) copy-start(bf16[1024,16]{1,0:T(8,128)(2,1)S(1)} %copy.241) | copy-start | bytes 98308
  200.7 19.3 %copy-start.23 = (bf16[1024,96]{1,0:T(8,128)(2,1)}, bf16[1024,96]{1,0:T(8,128)(2,1)S(1)}, u32[]{:S(2)}) copy-start(bf16[1024,96]{1,0:T(8,128)(2,1)S(1)} %copy.243) | copy-start | bytes 589828
  200.7 22.1 %copy-start.48 = (bf16[2048]{0:T(1024)(128)(2,1)S(1)}, bf16[2048]{0:T(1024)(128)(2,1)}, u32[]{:S(2)}) copy-start(bf16[2048]{0:T(1024)(128)(2,1)} %param.41) | copy-start | bytes 12292
  200.7 22.1 %copy-start.49 = (bf16[2048]{0:T(1024)(128)(2,1)S(1)}, bf16[2048]{0:T(1024)(128)(2,1)}, u32[]{:S(2)}) copy-start(bf16[2048]{0:T(1024)(128)(2,1)} %param.42) | copy-start | bytes 12292
  200.7 22.1 %copy-start.4 = (bf16[128,2048]{1,0:T(8,128)(2,1)S(1)}, bf16[128,2048]{1,0:T(8,128)(2,1)}, u32[]{:S(2)}) copy-start(bf16[128,2048]{1,0:T(8,128)(2,1)} %copy-done.3) | copy-start | bytes 1572868
  203.1 25.2 %collective-permute-start = (bf16[2048,256]{1,0:T(8,128)(2,1)}, bf16[2048,256]{1,0:T(8,128)(2,1)}, u32[]{:S(2)}, u32[]{:S(2)}) collective-permute-start(bf16[2048,256]{1,0:T(8,128)(2,1)} %bitcast.198), channel_id=1, source_target_pairs={{0,1},{1,0},{2,3},{3,2},{4,5},{5,4},{6,7},{7,6},{8,9},{9,8},{10,11... | collective-permute-start | bytes 3145736 | tf_op jit(solution)/shard_map/ppermute | solution.py:435
  206.6 338.8 %copy-start.40 = (f32[8,128]{1,0:T(8,128)}, f32[8,128]{1,0:T(8,128)S(1)}, u32[]{:S(2)}) copy-start(f32[8,128]{1,0:T(8,128)S(1)} %get-tuple-element.187) | copy-start | bytes 12292
  219.9 14.8 %collective-permute-start.1 = (bf16[256,2048]{0,1:T(8,128)(2,1)}, bf16[256,2048]{0,1:T(8,128)(2,1)}, u32[]{:S(2)}, u32[]{:S(2)}) collective-permute-start(bf16[256,2048]{0,1:T(8,128)(2,1)} %bitcast.201), channel_id=1, source_target_pairs={{0,1},{1,0},{2,3},{3,2},{4,5},{5,4},{6,7},{7,6},{8,9},{9,8},{10,11... | collective-permute-start | bytes 3145736 | tf_op jit(solution)/shard_map/ppermute | solution.py:435
  223.8 4.5 copy-start.20
  225.7 148.2 %copy-start.38 = (s32[1024]{0:T(1024)}, s32[1024]{0:T(1024)S(1)}, u32[]{:S(2)}) copy-start(s32[1024]{0:T(1024)S(1)} %get-tuple-element.171) | copy-start | bytes 12292
  228.3 6.4 copy-start.22
  228.4 6.4 copy-start.35
  228.4 6.4 copy-start.61
  234.8 6.6 copy-start.62
  337.2 160.2 %copy-start.7 = (bf16[4,2,2,64,2048]{4,3,2,1,0:T(8,128)(2,1)}, bf16[4,2,2,64,2048]{4,3,2,1,0:T(8,128)(2,1)S(1)}, u32[]{:S(2)}) copy-start(bf16[4,2,2,64,2048]{4,3,2,1,0:T(8,128)(2,1)S(1)} %get-tuple-element.40) | copy-start | bytes 12582916
  344.2 29.7 %copy-start.14 = (f32[1024,800]{0,1:T(8,128)}, f32[1024,800]{0,1:T(8,128)S(1)}, u32[]{:S(2)}) copy-start(f32[1024,800]{0,1:T(8,128)S(1)} %get-tuple-element.190) | copy-start | bytes 9830404
  351.0 29.8 %copy-start.15 = (f32[1024,800]{0,1:T(8,128)}, f32[1024,800]{0,1:T(8,128)S(1)}, u32[]{:S(2)}) copy-start(f32[1024,800]{0,1:T(8,128)S(1)} %get-tuple-element.192) | copy-start | bytes 9830404
  484.6 5.6 copy-start.6
  484.6 5.6 copy-start.18
  490.2 6.0 copy-start.17
  490.2 3.5 copy-start.13
  493.7 3.7 copy-start.16
  496.3 6.5 collective-permute-start.3
  502.7 46.2 %collective-permute-start.5 = (bf16[2048,800]{0,1:T(8,128)(2,1)}, bf16[2048,800]{0,1:T(8,128)(2,1)}, u32[]{:S(2)}, u32[]{:S(2)}) collective-permute-start(bf16[2048,800]{0,1:T(8,128)(2,1)} %convolution_convert_fusion.1), channel_id=1, source_target_pairs={{0,1},{1,0},{2,3},{3,2},{4,5},{5,4},{6,7},{7,6},{8,9},{9,8},{10,11... | collective-permute-start | bytes 9830408 | tf_op jit(solution)/shard_map/ppermute | solution.py:435
  504.2 35.2 %all-to-all-start.3 = ((bf16[8,256,256]{2,1,0:T(8,128)(2,1)}), bf16[8,256,256]{2,1,0:T(8,128)(2,1)S(1)}, u32[]{:S(2)}, u32[]{:S(2)}) async-start(bf16[8,256,256]{2,1,0:T(8,128)(2,1)} %bitcast.190), calls=%async_computation.3 | async-start | bytes 2097152 | tf_op jit(solution)/shard_map/all_to_all | solution.py:477
  514.2 11.2 %copy-start.55 = (s32[16]{0:T(128)S(1)}, s32[16]{0:T(128)}, u32[]{:S(2)}) copy-start(s32[16]{0:T(128)} %param.24) | copy-start | bytes 196
  524.6 6.1 collective-permute-start.4
  539.4 7.6 %copy-start.10 = (bf16[8,256,256]{2,1,0:T(8,128)(2,1)}, bf16[8,256,256]{2,1,0:T(8,128)(2,1)S(1)}, u32[]{:S(2)}) copy-start(bf16[8,256,256]{2,1,0:T(8,128)(2,1)S(1)} %all-to-all-done.3) | copy-start | bytes 3145732
  539.4 29.2 %all-to-all-start.4 = ((bf16[8,256,256]{2,1,0:T(8,128)(2,1)}), bf16[8,256,256]{2,1,0:T(8,128)(2,1)}, u32[]{:S(2)}, u32[]{:S(2)}) async-start(bf16[8,256,256]{2,1,0:T(8,128)(2,1)} %bitcast.189), calls=%async_computation.4 | async-start | bytes 2097152 | tf_op jit(solution)/shard_map/all_to_all | solution.py:477
  543.8 3.2 copy-start.24
  543.8 3.2 copy-start.27
  543.8 3.2 copy-start.28
  568.6 5.3 copy-start.53
  568.6 9.9 %copy-start.25 = (bf16[1024,96]{1,0:T(8,128)(2,1)S(1)}, bf16[1024,96]{1,0:T(8,128)(2,1)}, u32[]{:S(2)}) copy-start(bf16[1024,96]{1,0:T(8,128)(2,1)} %copy-done.23) | copy-start | bytes 589828
  568.6 9.9 %copy-start.41 = (f32[8,128]{1,0:T(8,128)S(1)}, f32[8,128]{1,0:T(8,128)}, u32[]{:S(2)}) copy-start(f32[8,128]{1,0:T(8,128)} %copy-done.40) | copy-start | bytes 12292
  568.6 135.0 %all-to-all-start.5 = ((bf16[8,256,800]{1,2,0:T(8,128)(2,1)}), bf16[8,256,800]{1,2,0:T(8,128)(2,1)}, u32[]{:S(2)}, u32[]{:S(2)}) async-start(bf16[8,256,800]{1,2,0:T(8,128)(2,1)} %bitcast.185), calls=%async_computation.5 | async-start | bytes 6553600 | tf_op jit(solution)/shard_map/all_to_all | solution.py:477
  593.8 11.2 %copy-start.39 = (f32[512]{0:T(512)S(1)}, f32[512]{0:T(512)}, u32[]{:S(2)}) copy-start(f32[512]{0:T(512)} %get-tuple-element.136) | copy-start | bytes 6148
  694.1 22.8 %copy-start.36 = (f32[1,2048]{1,0:T(1,128)}, f32[1,2048]{1,0:T(1,128)S(1)}, u32[]{:S(2)}) copy-start(f32[1,2048]{1,0:T(1,128)S(1)} %get-tuple-element.158) | copy-start | bytes 24580
  (11 other events, 20.4 us)

commit v2 on v1

--- a/solution.py
+++ b/solution.py
@@ -425,6 +425,8 @@
 ALL = ("z", "y", "x", "c")
 SWAP = ((0, 1), (1, 0))
 F32, BF16 = jnp.float32, jnp.bfloat16
+BY_X = (0, 2)
+END_BY_X = (0,)
 
 
 def dot(a, b, contract):
@@ -445,32 +447,6 @@
     return inverse * (
         t - jnp.mean(t, axis=-1, keepdims=True) - hat * jnp.mean(t * hat, axis=-1, keepdims=True)
     )
-
-
-def turn(values, cosine, sine):
-    half_rot = ROT // 2
-    first, second = values[:, :half_rot], values[:, half_rot:ROT]
-    return jnp.concatenate(
-        [first * cosine - second * sine, second * cosine + first * sine, values[:, ROT:]], axis=1
-    )
-
-
-def copy_block(order_ref, from_ref, to_ref):
-    to_ref[...] = from_ref[...]
-
-
-def take_blocks(values, order, piece):
-    count, width = values.shape[0] // piece, values.shape[1]
-    return pl.pallas_call(
-        copy_block,
-        out_shape=jax.ShapeDtypeStruct(values.shape, values.dtype),
-        grid_spec=pltpu.PrefetchScalarGridSpec(
-            num_scalar_prefetch=1,
-            grid=(count,),
-            in_specs=[pl.BlockSpec((piece, width), lambda i, order: (order[i], 0))],
-            out_specs=pl.BlockSpec((piece, width), lambda i, order: (i, 0)),
-        ),
-    )(order, values)
 
 
 def exchange(value):
@@ -505,6 +481,17 @@
     ).wait_recv()
 
 
+def left(source, out_sem, in_sem, device):
+    pltpu.make_async_remote_copy(
+        src_ref=source,
+        dst_ref=source,
+        send_sem=out_sem,
+        recv_sem=in_sem,
+        device_id=device,
+        device_id_type=pl.DeviceIdType.MESH,
+    ).wait_send()
+
+
 def greet(devices):
     barrier = pltpu.get_barrier_semaphore()
     for device in devices:
@@ -527,54 +514,59 @@
 
 class Reduce:
     @staticmethod
-    def scratch(nz, half, width):
+    def scratch(parts, nz, half, width):
         dma = pltpu.SemaphoreType.DMA
         return [
-            pltpu.VMEM((2, nz, 2, half, width), BF16),
-            pltpu.VMEM((2, nz, half, width), BF16),
-            pltpu.VMEM((2, nz, half, width), BF16),
-            pltpu.VMEM((2, nz, half, width), BF16),
-            pltpu.VMEM((2, nz, half, width), BF16),
-            dma((2, nz, 2)),
-            dma((2, nz, 2)),
-            dma((2, nz)),
-            dma((2, nz)),
-            dma((2, nz)),
-            dma((2, nz)),
+            pltpu.VMEM((parts, nz, 2, half, width), BF16),
+            pltpu.VMEM((parts, nz, half, width), BF16),
+            pltpu.VMEM((parts, nz, half, width), BF16),
+            pltpu.VMEM((parts, nz, half, width), BF16),
+            pltpu.VMEM((parts, nz, half, width), BF16),
+            pltpu.VMEM((parts, nz, half, width), BF16),
+            dma((parts, nz, 2)),
+            dma((parts, nz, 2)),
+            dma((parts, nz)),
+            dma((parts, nz)),
+            dma((parts, nz)),
+            dma((parts, nz)),
+            dma((parts, nz)),
         ]
 
-    def __init__(self, nz, half, part, refs):
+    def __init__(self, nz, half, part, refs, by_x=(0,)):
+        self.by_x = by_x
         self.nz, self.half, self.part = nz, half, part
         (
             self.in1,
             self.out2,
             self.in2,
             self.out3,
-            self.in3,
+            self.below,
+            self.above,
             self.s1,
             self.r1,
             self.s2,
             self.r2,
             self.s3,
-            self.r3,
+            self.rb,
+            self.ra,
         ) = refs
         self.copies = []
 
     def along(self, h):
         iz, iy, ix, ic = here()
         across_x, across_y = (iz, iy, 1 - ix, ic), (iz, 1 - iy, ix, ic)
-        return (across_x, across_y) if h == 0 else (across_y, across_x)
+        return (across_x, across_y) if h in self.by_x else (across_y, across_x)
 
     def block(self, h, z, first_mine, second):
         _, iy, ix, _ = here()
         rows = pl.ds(h * self.half, self.half)
-        if h == 0:
+        if h in self.by_x:
             return self.part.at[z, second, ix if first_mine else 1 - ix, rows]
         return self.part.at[z, iy if first_mine else 1 - iy, second, rows]
 
     def mine(self, h):
         _, iy, ix, _ = here()
-        return iy if h == 0 else ix
+        return iy if h in self.by_x else ix
 
     def plane(self, k):
         return lax.rem(here()[0] + k, self.nz)
@@ -608,7 +600,6 @@
             )
 
     def third(self, h):
-        iz, iy, ix, ic = here()
         first, across = self.along(h)
         near = self.mine(h)
         for k in list(range(1, self.nz)) + [0]:
@@ -622,33 +613,63 @@
             )
             if k == 0:
                 return total
-            self.out3[h, k] = total.astype(BF16)
-            self.copies.append(
-                send(
-                    self.out3.at[h, k],
-                    self.in3.at[h, k],
-                    self.s3.at[h, k],
-                    self.r3.at[h, k],
-                    (z, iy, ix, ic),
-                )
-            )
+            self.out3[h, z] = total.astype(BF16)
+
+    def hops(self, m):
+        up = [(z, m + 1, self.below, self.rb, m > 0) for z in range(self.nz - 1, m, -1)]
+        down = [(z, m - 1, self.above, self.ra, m < self.nz - 1) for z in range(m)]
+        return up + down
+
+    def chain(self, h):
+        iz, iy, ix, ic = here()
+        for m in range(self.nz):
+
+            @pl.when(iz == m)
+            def _():
+                for z, to, buffer, sems, waits in self.hops(m):
+                    device = (to, iy, ix, ic)
+                    if waits:
+                        arrived(buffer.at[h, z], self.s3.at[h, z], sems.at[h, z], device)
+                        self.out3[h, z] = (
+                            self.out3[h, z].astype(F32) + buffer[h, z].astype(F32)
+                        ).astype(BF16)
+                    send(self.out3.at[h, z], buffer.at[h, z], self.s3.at[h, z], sems.at[h, z], device)
+                if m == 0:
+                    self.below[h, m] = jnp.zeros(self.below.shape[2:], BF16)
+                if m == self.nz - 1:
+                    self.above[h, m] = jnp.zeros(self.above.shape[2:], BF16)
 
     def finish(self, h, total):
-        _, iy, ix, ic = here()
-        for k in range(1, self.nz):
-            z = self.plane(self.nz - k)
-            arrived(self.in3.at[h, k], self.s3.at[h, k], self.r3.at[h, k], (z, iy, ix, ic))
-            total = total + self.in3[h, k].astype(F32)
-        return total
+        iz, iy, ix, ic = here()
+        for at_end, buffer, sems in (
+            (iz == 0, self.below, self.rb),
+            (iz == self.nz - 1, self.above, self.ra),
+        ):
+
+            @pl.when(jnp.logical_not(at_end))
+            def _():
+                arrived(buffer.at[h, iz], self.s3.at[h, iz], sems.at[h, iz], (1 - iz, iy, ix, ic))
+
+        return total + self.below[h, iz].astype(F32) + self.above[h, iz].astype(F32)
+
+    def end(self, parts):
+        iz, iy, ix, ic = here()
+        for copy in self.copies:
+            copy.wait_send()
+        for h in parts:
+            for k in range(1, self.nz):
+                z = self.plane(k)
+                left(self.out3.at[h, z], self.s3.at[h, z], self.rb.at[h, z], (z, iy, ix, ic))
 
 
 class Gather:
     @staticmethod
-    def scratch(nz):
+    def scratch(parts, nz):
         dma = pltpu.SemaphoreType.DMA
-        return [dma((2, nz)), dma((2, nz)), dma((2, nz, 2)), dma((2, nz, 2, 2)), dma((2,))]
-
-    def __init__(self, nz, half, out, refs, forward=None):
+        return [dma((parts, nz + 1)), dma((parts, nz)), dma((parts, nz, 2)), dma((parts, nz, 2, 2)), dma((parts,))]
+
+    def __init__(self, nz, half, out, refs, forward=None, by_x=(0,)):
+        self.by_x = by_x
         self.nz, self.half, self.out = nz, half, out
         self.sz, self.sp, self.sq, self.r, self.local = refs
         self.copies, self.locals, self.forward = [], [], forward
@@ -656,47 +677,56 @@
     def axes(self, h):
         iz, iy, ix, ic = here()
         across_x, across_y = (iz, iy, 1 - ix, ic), (iz, 1 - iy, ix, ic)
-        return (across_y, across_x) if h == 0 else (across_x, across_y)
+        return (across_y, across_x) if h in self.by_x else (across_x, across_y)
 
     def block(self, h, z, y, x):
         return self.out.at[z, y, x, pl.ds(h * self.half, self.half)]
 
     def on(self, h, source, z, y, x, which):
-        iz, iy, ix, ic = here()
         p, q = self.axes(h)
         there, got = self.block(h, z, y, x), self.r.at[h, z, y, x]
-        if "z" in which:
-            for k in range(1, self.nz):
-                far = (lax.rem(iz + k, self.nz), iy, ix, ic)
-                self.copies.append(send(source, there, self.sz.at[h, k], got, far))
         if "p" in which:
-            self.copies.append(send(source, there, self.sp.at[h, z], got, p))
+            send(source, there, self.sp.at[h, z], got, p)
         if "q" in which:
-            side = x if h == 1 else y
-            self.copies.append(send(source, there, self.sq.at[h, z, side], got, q))
+            send(source, there, self.sq.at[h, z, x if h not in self.by_x else y], got, q)
         if self.forward is not None:
             self.forward(h, source, z, y, x)
+
+    def along_z(self, h, source, z, step, sem):
+        iz, iy, ix, ic = here()
+        there = iz + step
+
+        @pl.when((there >= 0) & (there < self.nz))
+        def _():
+            send(source, self.block(h, z, iy, ix), self.sz.at[h, sem], self.r.at[h, z, iy, ix], (there, iy, ix, ic))
 
     def start(self, h, source):
         iz, iy, ix, _ = here()
         copy = pltpu.make_async_copy(source, self.block(h, iz, iy, ix), self.local.at[h])
         copy.start()
         self.locals.append(copy)
-        self.on(h, source, iz, iy, ix, "zpq")
+        self.along_z(h, source, iz, 1, iz)
+        self.along_z(h, source, iz, -1, self.nz)
+        self.on(h, source, iz, iy, ix, "pq")
 
     def got(self, h, z, y, x):
         arrived(self.block(h, z, y, x), self.sz.at[h, 0], self.r.at[h, z, y, x], self.axes(h)[0])
 
-    def first(self, h, k):
+    def first(self, h, distance, step):
         iz, iy, ix, _ = here()
-        z = lax.rem(iz + k, self.nz)
-        self.got(h, z, iy, ix)
-        self.on(h, self.block(h, z, iy, ix), z, iy, ix, "pq")
+        z = iz - distance * step
+
+        @pl.when((z >= 0) & (z < self.nz))
+        def _():
+            self.got(h, z, iy, ix)
+            block = self.block(h, z, iy, ix)
+            self.along_z(h, block, z, step, z)
+            self.on(h, block, z, iy, ix, "pq")
 
     def second(self, h, k):
         iz, iy, ix, _ = here()
         z = lax.rem(iz + k, self.nz)
-        y, x = (1 - iy, ix) if h == 0 else (iy, 1 - ix)
+        y, x = (1 - iy, ix) if h in self.by_x else (iy, 1 - ix)
         self.got(h, z, y, x)
         self.on(h, self.block(h, z, y, x), z, y, x, "q")
 
@@ -704,7 +734,7 @@
         iz, iy, ix, _ = here()
         z = lax.rem(iz + k, self.nz)
         for side in (0, 1):
-            if h == 0:
+            if h in self.by_x:
                 y, x = (iy if side == 0 else 1 - iy), 1 - ix
             else:
                 y, x = 1 - iy, (ix if side == 0 else 1 - ix)
@@ -712,74 +742,120 @@
             if self.forward is not None:
                 self.forward(h, self.block(h, z, y, x), z, y, x)
 
+    def turns(self):
+        return [1, self.nz - 1] + [k for k in range(2, self.nz - 1)]
+
+    def firsts(self, parts):
+        for h in parts:
+            self.second(h, 0)
+        for distance in range(1, self.nz):
+            for step in (1, -1):
+                for h in parts:
+                    self.first(h, distance, step)
+
+    def seconds(self, parts):
+        for k in self.turns():
+            for h in parts:
+                self.second(h, k)
+
+    def thirds(self, parts):
+        for k in [0] + self.turns():
+            for h in parts:
+                self.third(h, k)
+
     def rest(self):
-        turns = [1, self.nz - 1] + [k for k in range(2, self.nz - 1)]
-        for h in (0, 1):
-            self.second(h, 0)
-        for k in turns:
-            for h in (0, 1):
-                self.first(h, k)
-        for k in turns:
-            for h in (0, 1):
-                self.second(h, k)
-        for k in [0] + turns:
-            for h in (0, 1):
-                self.third(h, k)
-
-    def end(self):
+        self.firsts((0, 1))
+        self.seconds((0, 1))
+        self.thirds((0, 1))
+
+    def end(self, parts):
+        iz, iy, ix, ic = here()
         for copy in self.locals:
             copy.wait()
-        for copy in self.copies:
-            copy.wait_send()
-
-
-def run_reduce(reduce):
-    for far in (True, False):
-        for h in (0, 1):
-            reduce.start(h, far)
-    for h in (0, 1):
+        for h in parts:
+            p, q = self.axes(h)
+            for k in range(self.nz):
+                z = lax.rem(iz + k, self.nz)
+                block, got = self.block(h, z, iy, ix), self.r.at[h, z, iy, ix]
+                left(block, self.sp.at[h, z], got, p)
+                for side in (0, 1):
+                    left(block, self.sq.at[h, z, side], got, q)
+                up = (z <= iz) & (iz < self.nz - 1)
+                down = (z > iz) & (iz > 0)
+
+                @pl.when(up | down)
+                def _():
+                    left(block, self.sz.at[h, z], got, p)
+
+            @pl.when(iz > 0)
+            def _():
+                left(self.block(h, iz, iy, ix), self.sz.at[h, self.nz], self.r.at[h, iz, iy, ix], p)
+
+
+def reduce_gather(nz, half, part, out, refs, finished):
+    reduce = Reduce(nz, half, part, refs[:13], BY_X)
+    gather = Gather(nz, half, out, refs[13:], None, BY_X)
+    greet(neighbours(nz))
+    early, late = (0, 1), (2, 3)
+
+    def begin(parts):
+        for far in (True, False):
+            for h in parts:
+                reduce.start(h, far)
+
+    def finish(parts, kept):
+        for h in parts:
+            gather.start(h, finished(h, reduce.finish(h, kept[h])))
+
+    begin(early)
+    for h in early:
         reduce.second(h)
+    begin(late)
+    kept = {h: reduce.third(h) for h in early}
+    for h in early:
+        reduce.chain(h)
+    for h in late:
+        reduce.second(h)
+    finish(early, kept)
+    kept = {h: reduce.third(h) for h in late}
+    for h in late:
+        reduce.chain(h)
+    gather.firsts(early)
+    finish(late, kept)
+    gather.seconds(early)
+    gather.firsts(late)
+    gather.thirds(early)
+    gather.seconds(late)
+    gather.thirds(late)
+    gather.end(early + late)
+    reduce.end(early + late)
 
 
 def forward_kernel(nz, half, part, rows, bias, gain, shift, out, resid, fin, *refs):
-    reduce = Reduce(nz, half, part, refs[:11])
-    gather = Gather(nz, half, out, refs[11:])
-    greet(neighbours(nz))
-    run_reduce(reduce)
-    kept = [reduce.third(h) for h in (0, 1)]
-    for h in (0, 1):
+    def finished(h, total):
         at = pl.ds(h * half, half)
-        total = rows[at].astype(F32) + reduce.finish(h, kept[h]) + bias[...]
+        total = rows[at].astype(F32) + total + bias[...]
         resid[at] = total
         hat, _ = normed(total)
         fin[h] = (hat * gain[...] + shift[...]).astype(BF16)
-        gather.start(h, fin.at[h])
-    gather.rest()
-    gather.end()
-    for copy in reduce.copies:
-        copy.wait_send()
+        return fin.at[h]
+
+    reduce_gather(nz, half, part, out, refs, finished)
 
 
 def backward_kernel(nz, half, part, resid, gain, out, vectors, fin, *refs):
-    reduce = Reduce(nz, half, part, refs[:11])
-    gather = Gather(nz, half, out, refs[11:])
-    greet(neighbours(nz))
-    run_reduce(reduce)
-    kept = [reduce.third(h) for h in (0, 1)]
     sums = []
-    for h in (0, 1):
-        total = reduce.finish(h, kept[h])
+
+    def finished(h, total):
         hat, inverse = normed(resid[pl.ds(h * half, half)])
         dresid = norm_back(total * gain[...], hat, inverse)
         fin[h] = dresid.astype(BF16)
-        gather.start(h, fin.at[h])
         sums.append([jnp.sum(v, axis=0, keepdims=True) for v in (total * hat, total, dresid)])
+        return fin.at[h]
+
+    reduce_gather(nz, half, part, out, refs, finished)
     for i in range(3):
-        vectors[pl.ds(i, 1)] = sums[0][i] + sums[1][i]
-    gather.rest()
-    gather.end()
-    for copy in reduce.copies:
-        copy.wait_send()
+        vectors[pl.ds(i, 1)] = sum(part_sums[i] for part_sums in sums)
 
 
 def vmem():
@@ -790,13 +866,17 @@
     return pl.BlockSpec(memory_space=pl.ANY)
 
 
+def busy(us):
+    return pl.CostEstimate(flops=0, bytes_accessed=us * 3_000_000, transcendentals=0)
+
+
 def comm(which, limit=48):
     return pltpu.CompilerParams(collective_id=which, has_side_effects=True, vmem_limit_bytes=limit << 20)
 
 
 def reduce_norm_gather(nz, part, rows, bias, gain, shift):
     share, width = rows.shape
-    half = share // 2
+    half = share // 4
     out, resid = pl.pallas_call(
         functools.partial(forward_kernel, nz, half),
         out_shape=[
@@ -805,9 +885,10 @@
         ],
         in_specs=[vmem()] * 5,
         out_specs=[anywhere(), vmem()],
-        scratch_shapes=[pltpu.VMEM((2, half, width), BF16)]
-        + Reduce.scratch(nz, half, width)
-        + Gather.scratch(nz),
+        scratch_shapes=[pltpu.VMEM((4, half, width), BF16)]
+        + Reduce.scratch(4, nz, half, width)
+        + Gather.scratch(4, nz),
+        cost_estimate=busy(90),
         compiler_params=comm(2),
     )(part.reshape(nz, 2, 2, share, width), rows, bias, gain, shift)
     return out.reshape(4 * nz * share, width), resid
@@ -815,7 +896,7 @@
 
 def reduce_back_gather(nz, part, resid, gain):
     share, width = resid.shape
-    half = share // 2
+    half = share // 4
     out, vectors = pl.pallas_call(
         functools.partial(backward_kernel, nz, half),
         out_shape=[
@@ -824,9 +905,10 @@
         ],
         in_specs=[vmem()] * 3,
         out_specs=[anywhere(), vmem()],
-        scratch_shapes=[pltpu.VMEM((2, half, width), BF16)]
-        + Reduce.scratch(nz, half, width)
-        + Gather.scratch(nz),
+        scratch_shapes=[pltpu.VMEM((4, half, width), BF16)]
+        + Reduce.scratch(4, nz, half, width)
+        + Gather.scratch(4, nz),
+        cost_estimate=busy(90),
         compiler_params=comm(3),
     )(part.reshape(nz, 2, 2, share, width), resid, gain)
     return out.reshape(4 * nz * share, width), vectors
@@ -838,45 +920,37 @@
 
 
 def objective_kernel(
-    nz, seqs, seq_total, stats, hot, scored, refs, lens, wanted, coef, lse_out, scalars, held, got, ss, rs
+    nz, seqs, seq_total, stats, hot, scored, refs, lens, wanted, coef, lse_out, scalars, held, near, far, s1, r1, s2, r2
 ):
     iz, iy, ix, ic = here()
-    peers = neighbours(nz) + [other_core()]
-    greet(peers)
-    current = tuple(stats[i] for i in range(3))
+    plane = [(iz, iy, 1 - ix, ic), (iz, 1 - iy, ix, ic), (iz, 1 - iy, 1 - ix, ic)]
+    line = [(lax.rem(iz + k, nz), iy, ix, c) for c in (ic, 1 - ic) for k in range(nz)][1:]
+    greet(plane + line)
     copies = []
-    for step, (mine, device) in enumerate(((ix, (iz, iy, 1 - ix, ic)), (iy, (iz, 1 - iy, ix, ic)))):
-        for i in range(3):
-            held[step, i] = current[i]
-        copies.append(send(held.at[step], got.at[step], ss.at[step], rs.at[step], device))
-        arrived(got.at[step], ss.at[step], rs.at[step], device)
-        theirs = tuple(got[step, i] for i in range(3))
-        low = tuple(jnp.where(mine == 0, a, b) for a, b in zip(current, theirs))
-        high = tuple(jnp.where(mine == 0, b, a) for a, b in zip(current, theirs))
-        current = merge(low, high)
+    for i, device in enumerate(plane):
+        copies.append(send(stats, near.at[iy, ix], s1.at[i], r1.at[iy, ix], device))
+    near[iy, ix] = stats[...]
+    for _, y, x, _ in plane:
+        arrived(near.at[y, x], s1.at[0], r1.at[y, x], plane[0])
+    sides = [tuple(near[y, x, i] for i in range(3)) for y in (0, 1) for x in (0, 1)]
+    current = merge(merge(sides[0], sides[1]), merge(sides[2], sides[3]))
     for i in range(3):
-        held[2, i] = current[i]
-    for k in range(1, nz):
-        z = lax.rem(iz + k, nz)
-        copies.append(send(held.at[2], got.at[2 + iz], ss.at[2 + k], rs.at[2 + iz], (z, iy, ix, ic)))
-    for i in range(3):
-        got[2 + iz, i] = current[i]
-    for k in range(1, nz):
-        z = lax.rem(iz + k, nz)
-        arrived(got.at[2 + z], ss.at[2], rs.at[2 + z], (z, iy, ix, ic))
-    current = tuple(got[2, i] for i in range(3))
-    for z in range(1, nz):
-        current = merge(current, tuple(got[2 + z, i] for i in range(3)))
-    lse = current[0] + jnp.log(current[1])
-    logp = current[2] - lse
-    lse_out[...] = lse
-    held[3, 0] = logp
-    last = 2 + nz
-    copies.append(send(held.at[3, 0], got.at[last, 0], ss.at[last], rs.at[last], other_core()))
-    arrived(got.at[last, 0], ss.at[last], rs.at[last], other_core())
-    theirs = got[last, 0]
-    own = jnp.where(ic == 0, logp, theirs)
-    pair = jnp.where(ic == 0, theirs, logp)
+        held[i] = current[i]
+        far[iz, ic, i] = current[i]
+    for i, device in enumerate(line):
+        copies.append(send(held, far.at[iz, ic], s2.at[i], r2.at[iz, ic], device))
+    for z, _, _, c in line:
+        arrived(far.at[z, c], s2.at[0], r2.at[z, c], line[0])
+
+    def whole(c):
+        total = tuple(far[0, c, i] for i in range(3))
+        for z in range(1, nz):
+            total = merge(total, tuple(far[z, c, i] for i in range(3)))
+        lse = total[0] + jnp.log(total[1])
+        return lse, total[2] - lse
+
+    (own_lse, own), (pair_lse, pair) = whole(0), whole(1)
+    lse_out[...] = jnp.where(ic == 0, own_lse, pair_lse)
 
     def means(values, ref):
         terms = (values - ref) * scored[...]
@@ -894,7 +968,7 @@
         slopes.append(-kto_beta * sign * sigmoid * (1.0 - sigmoid))
         loss = loss + jnp.sum(1.0 - sigmoid, axis=0, keepdims=True)
     shared = -jnp.sum(sum(slopes), axis=0, keepdims=True) / seq_total
-    total = jnp.zeros_like(logp)
+    total = jnp.zeros_like(own)
     for s in range(seqs):
         value = jnp.where(ic == 0, slopes[s], shared) / lens[:, s : s + 1]
         total = total + hot[s] * value
@@ -918,11 +992,15 @@
         in_specs=[vmem()] * 6,
         out_specs=[vmem()] * 3,
         scratch_shapes=[
-            pltpu.VMEM((4, 3) + shape, F32),
-            pltpu.VMEM((3 + nz, 3) + shape, F32),
-            dma((3 + nz,)),
-            dma((3 + nz,)),
+            pltpu.VMEM((3,) + shape, F32),
+            pltpu.VMEM((2, 2, 3) + shape, F32),
+            pltpu.VMEM((nz, 2, 3) + shape, F32),
+            dma((3,)),
+            dma((2, 2)),
+            dma((2 * nz - 1,)),
+            dma((nz, 2)),
         ],
+        cost_estimate=busy(15),
         compiler_params=comm(4),
     )(stats, hot, scored, refs, lens, wanted)
 
@@ -1001,11 +1079,12 @@
     bias,
     joined_in,
     dense_in,
+    down_in,
     natural,
     info_out,
     bias_out,
     joined_out,
-    dense_out,
+    out_all,
     fs,
     fr,
     js,
@@ -1018,21 +1097,30 @@
     zs,
     zr,
     ps,
+    ds,
+    dr,
+    dl,
+    es,
+    er,
     *refs,
 ):
     iz, iy, ix, ic = here()
     core = other_core()
-    greet(neighbours(nz) + [core] + diagonal(nz))
+    across = [(lax.rem(iz + k, nz), 1 - iy, ix, ic) for k in range(nz)]
+    greet(neighbours(nz) + [core] + diagonal(nz) + across[1:])
     depth = joined_in.shape[0]
     cols = joined_out.shape[1]
-    heads = dense_out.shape[0]
+    heads = dense_in.shape[0] // nz
+    units = down_in.shape[0] // (2 * nz)
+    dense_out = out_all.at[pl.ds(0, heads)]
+    down_out, down_other = (out_all.at[pl.ds(heads + i * units, units)] for i in (0, 1))
     copies = []
 
     def rows_of(h, z, y, x, c):
         return natural.at[z, y, x, c, pl.ds(h * half, half)]
 
     def forward(h, source, z, y, x):
-        copies.append(send(source, rows_of(h, z, y, x, ic), fs.at[h, z, y, x], fr.at[h, z, y, x], core))
+        send(source, rows_of(h, z, y, x, ic), fs.at[h, z, y, x], fr.at[h, z, y, x], core)
 
     class Rows(Gather):
         def block(self, h, z, y, x):
@@ -1071,7 +1159,18 @@
         arrived(info_out.at[z, iy], zs.at[k], zr.at[z, iy], across_y)
         copies.append(send(info_out.at[z, iy], info_out.at[z, iy], ps.at[z], zr.at[z, iy], across_y))
 
-    gather.rest()
+    gather.firsts((0, 1))
+
+    line = [(lax.rem(iz + k, nz), iy, ix, ic) for k in range(1, nz)]
+    local = pltpu.make_async_copy(down_in.at[lanes(mine, units)], down_out.at[:, lanes(mine, depth)], dl.at[0])
+    local.start()
+    for device in line + across:
+        d = device[0] * 2 + device[1]
+        copies.append(
+            send(down_in.at[lanes(d, units)], down_out.at[:, lanes(mine, depth)], ds.at[d], dr.at[mine], device)
+        )
+    gather.seconds((0, 1))
+    gather.thirds((0, 1))
 
     def head_parts(z, side):
         d = z * 2 + side
@@ -1083,6 +1182,15 @@
         from_head(nz, k, parts, js, jr)
         for i, part in enumerate(parts):
             copies.append(send(part, part, cs.at[i, z], cr.at[i, z], core))
+    local.wait()
+    for device in [(iz, iy, ix, ic)] + line + across:
+        d = device[0] * 2 + device[1]
+        block = down_out.at[:, lanes(d, depth)]
+        if device[0] is not iz or device[1] is not iy:
+            arrived(block, ds.at[d], dr.at[d], device)
+        copies.append(send(block, down_other.at[:, lanes(d, depth)], es.at[d], er.at[d], core))
+    for d in range(2 * nz):
+        arrived(down_other.at[:, lanes(d, depth)], es.at[d], er.at[d], core)
     for k in range(nz):
         z = lax.rem(iz + k, nz)
         arrived(info_out.at[z, 1 - iy], ps.at[z], zr.at[z, 1 - iy], across_y)
@@ -1091,11 +1199,12 @@
             for x in (0, 1):
                 for h in (0, 1):
                     arrived(rows_of(h, z, y, x, 1 - ic), fs.at[h, z, y, x], fr.at[h, z, y, x], core)
+                    left(rows_of(h, z, y, x, ic), fs.at[h, z, y, x], fr.at[h, z, y, x], core)
     for z in range(nz):
         for i, part in enumerate(head_parts(z, 1 - ic)):
             arrived(part, cs.at[i, z], cr.at[i, z], core)
     arrived(bias_out, ms.at[0], mr.at[0], core)
-    gather.end()
+    gather.end((0, 1))
     for k in range(nz):
         z = lax.rem(iz + k, nz)
         sent_head(nz, k, [joined_in.at[:, lanes(z, cols)], dense_in.at[lanes(z, heads)]], js, jr)
@@ -1103,11 +1212,12 @@
         copy.wait_send()
 
 
-def front(nz, residual, info, bias, joined_in, dense_in):
+def front(nz, residual, info, bias, joined_in, dense_in, down_in):
     held, width = residual.shape
     half = held // 8
     depth, cols = joined_in.shape[0], joined_in.shape[1] // nz
     heads = dense_in.shape[0] // nz
+    units = down_in.shape[0] // (2 * nz)
     dma = pltpu.SemaphoreType.DMA
     outs = pl.pallas_call(
         functools.partial(front_kernel, nz, half),
@@ -1116,9 +1226,9 @@
             jax.ShapeDtypeStruct((nz, 2) + info.shape, F32),
             jax.ShapeDtypeStruct(bias.shape, F32),
             jax.ShapeDtypeStruct((2 * nz * depth, cols), BF16),
-            jax.ShapeDtypeStruct((heads, 2 * nz * depth), BF16),
+            jax.ShapeDtypeStruct((heads + 2 * units, 2 * nz * depth), BF16),
         ],
-        in_specs=[anywhere(), vmem(), vmem(), anywhere(), anywhere()],
+        in_specs=[anywhere(), vmem(), vmem(), anywhere(), anywhere(), anywhere()],
         out_specs=[anywhere(), vmem(), vmem(), anywhere(), anywhere()],
         scratch_shapes=[
             dma((2, nz, 2, 2)),
@@ -1133,10 +1243,16 @@
             dma((nz,)),
             dma((nz, 2)),
             dma((nz,)),
+            dma((2 * nz,)),
+            dma((2 * nz,)),
+            dma((1,)),
+            dma((2 * nz,)),
+            dma((2 * nz,)),
         ]
-        + Gather.scratch(nz),
+        + Gather.scratch(2, nz),
+        cost_estimate=busy(45),
         compiler_params=comm(1, 16),
-    )(residual, info, bias, joined_in, dense_in)
+    )(residual, info, bias, joined_in, dense_in, down_in)
     natural = outs[0].reshape(8 * nz * 2 * half, width)
     return natural, outs[1].reshape((2 * nz,) + info.shape), outs[2], outs[3], outs[4]
 
@@ -1188,7 +1304,7 @@
     core = other_core()
     across_x, across_y = (iz, iy, 1 - ix, ic), (iz, 1 - iy, ix, ic)
     greet(neighbours(nz) + [core] + diagonal(nz))
-    reduce = Reduce(nz, half, merged, refs)
+    reduce = Reduce(nz, half, merged, refs, END_BY_X)
     copies = []
     depth = joined_in.shape[0] // (2 * nz)
     cols = joined_in.shape[1]
@@ -1268,6 +1384,8 @@
         arrived(bias_out.at[z, iy], bs.at[k], br.at[z, iy], across_y)
         copies.append(send(bias_out.at[z, iy], bias_out.at[z, iy], bp.at[z], br.at[z, iy], across_y))
     kept = [reduce.third(h) for h in (0, 1)]
+    for h in (0, 1):
+        reduce.chain(h)
     arrived(vector_in.at[2], vs.at[2], vr.at[2], across_y)
     vector_sum[2] = vector_sum[1] + vector_in[2]
     for k in range(1, nz):
@@ -1307,7 +1425,8 @@
         at = pl.ds(h * half, half)
         arrived(rows_out.at[ix, 1 - ic, at], os.at[3 + h], orr.at[3 + h], core)
         arrived(rows_out.at[1 - ix, 1 - ic, at], os.at[5 + h], orr.at[5 + h], core)
-    for copy in copies + reduce.copies:
+    reduce.end((0, 1))
+    for copy in copies:
         copy.wait_send()
 
 
@@ -1353,9 +1472,121 @@
             dma((7,)),
             dma((7,)),
         ]
-        + Reduce.scratch(nz, half, width),
+        + Reduce.scratch(2, nz, half, width),
+        cost_estimate=busy(70),
         compiler_params=comm(5),
     )(part, mine_rows, other_rows, rows, vectors, keep, give, joined_in, dense_in)
+
+
+def turned(values, cosine, low, high):
+    half_rot = ROT // 2
+    return (
+        values * cosine
+        + pltpu.roll(values, values.shape[1] - half_rot, 1) * low
+        + pltpu.roll(values, half_rot, 1) * high
+    )
+
+
+def block_rows(order, ref, piece, first, count):
+    return jnp.concatenate(
+        [ref[pl.ds(pl.multiple_of(order[first + i] * piece, piece), piece), :] for i in range(count)], axis=0
+    )
+
+
+def attention_kernel(piece, order, fused, tables, allowed, qkv, probs_out, mixed):
+    groups, held = allowed.shape[0], allowed.shape[1]
+    per = held // piece
+    for g in range(groups):
+        at = pl.ds(g * held, held)
+        rows = block_rows(order, fused, piece, g * per, per)
+        turn_by = [tables[i, at] for i in range(3)]
+        query = turned(rows[:, :HD], *turn_by).astype(BF16)
+        keys = turned(rows[:, HD : 2 * HD], *turn_by).astype(BF16)
+        values = rows[:, 2 * HD :].astype(BF16)
+        qkv[at, :HD] = query
+        qkv[at, HD : 2 * HD] = keys
+        qkv[at, 2 * HD :] = values
+        scores = jnp.where(allowed[g] > 0.5, dot(query, keys, (1, 1)) / math.sqrt(HD), masked_score)
+        weights = jnp.exp(scores - jnp.max(scores, axis=-1, keepdims=True))
+        probs = weights / jnp.sum(weights, axis=-1, keepdims=True)
+        probs_out[g] = probs
+        mixed[at] = dot(probs.astype(BF16), values, (1, 0)).astype(BF16)
+
+
+def attention(order, fused, tables, allowed, piece):
+    total = fused.shape[0]
+    return pl.pallas_call(
+        functools.partial(attention_kernel, piece),
+        out_shape=[
+            jax.ShapeDtypeStruct((total, 3 * HD), BF16),
+            jax.ShapeDtypeStruct(allowed.shape, F32),
+            jax.ShapeDtypeStruct((total, HD), BF16),
+        ],
+        in_specs=[pl.BlockSpec(memory_space=pltpu.SMEM)] + [vmem()] * 3,
+        out_specs=[vmem()] * 3,
+        compiler_params=pltpu.CompilerParams(vmem_limit_bytes=32 << 20),
+    )(order, fused, tables, allowed)
+
+
+def place_kernel(piece, order, mixed, active, out):
+    per = 2
+    out[:, :HD] = mixed[...]
+    for g in range(mixed.shape[0] // (per * piece)):
+        out[pl.ds(g * per * piece, per * piece), HD:] = block_rows(order, active, piece, g * per, per)
+
+
+def place(order, mixed, active, piece):
+    total = mixed.shape[0]
+    return pl.pallas_call(
+        functools.partial(place_kernel, piece),
+        out_shape=jax.ShapeDtypeStruct((total, HD + active.shape[1]), BF16),
+        in_specs=[pl.BlockSpec(memory_space=pltpu.SMEM)] + [vmem()] * 2,
+        out_specs=vmem(),
+        compiler_params=pltpu.CompilerParams(vmem_limit_bytes=32 << 20),
+    )(order, mixed, active)
+
+
+def attention_back_kernel(piece, order, douts, slope, qkv, probs_in, tables, dfused, dhidden, sums):
+    groups, held = probs_in.shape[0], probs_in.shape[1]
+    per = held // piece
+    joined_sum = jnp.zeros((1, 3 * HD), F32)
+    hidden_sum = jnp.zeros((1, slope.shape[1]), F32)
+    for g in range(groups):
+        at = pl.ds(g * held, held)
+        query, keys, values = qkv[at, :HD], qkv[at, HD : 2 * HD], qkv[at, 2 * HD :]
+        dmixed = douts[at, :HD].astype(BF16)
+        probs = probs_in[g]
+        dvalues = dot(probs.astype(BF16), dmixed, (0, 0))
+        dprobs = dot(dmixed, values, (1, 1))
+        dscores = (probs * (dprobs - jnp.sum(probs * dprobs, axis=-1, keepdims=True))).astype(BF16)
+        turn_by = [tables[0, at], -tables[1, at], -tables[2, at]]
+        dquery = turned(dot(dscores, keys, (1, 0)) / math.sqrt(HD), *turn_by)
+        dkeys = turned(dot(dscores, query, (0, 0)) / math.sqrt(HD), *turn_by)
+        whole = jnp.concatenate([dquery, dkeys, dvalues], axis=1).astype(BF16)
+        joined_sum = joined_sum + jnp.sum(whole.astype(F32), axis=0, keepdims=True)
+        for i in range(per):
+            to = pl.ds(pl.multiple_of(order[g * per + i] * piece, piece), piece)
+            dfused[to, :] = whole[i * piece : (i + 1) * piece]
+            grown = (douts[pl.ds(g * held + i * piece, piece), HD:] * slope[to, :]).astype(BF16)
+            dhidden[to, :] = grown
+            hidden_sum = hidden_sum + jnp.sum(grown.astype(F32), axis=0, keepdims=True)
+    sums[:, : 3 * HD] = joined_sum
+    sums[:, 3 * HD :] = hidden_sum
+
+
+def attention_back(order, douts, slope, qkv, probs, tables, piece):
+    total, units = slope.shape
+    return pl.pallas_call(
+        functools.partial(attention_back_kernel, piece),
+        out_shape=[
+            jax.ShapeDtypeStruct((total, 3 * HD), BF16),
+            jax.ShapeDtypeStruct((total, units), BF16),
+            jax.ShapeDtypeStruct((1, 3 * HD + units), F32),
+        ],
+        in_specs=[pl.BlockSpec(memory_space=pltpu.SMEM)] + [vmem()] * 5,
+        out_specs=[vmem()] * 3,
+        compiler_params=pltpu.CompilerParams(vmem_limit_bytes=40 << 20),
+    )(order, douts, slope, qkv, probs, tables)
 
 
 def fast_shards(
@@ -1409,18 +1640,15 @@
         ]
     )
     bias_own = jnp.concatenate([b_joined, b_up]).astype(F32)
-    natural, info, bias_other, wj, wd = front(nz, residual, info, bias_own.reshape(-1, HD), w_joined, w_dense)
+    natural, info, bias_other, wj, wout = front(
+        nz, residual, info, bias_own.reshape(-1, HD), w_joined, w_dense, w_down
+    )
     bias_other = bias_other.reshape(-1)
 
     send_up = w_up.reshape(depth, n, ffs).transpose(1, 0, 2)
-    send_down = w_down.reshape(n, ffs, depth)
     send_vocab = w_vocab.reshape(depth, n, vcols).transpose(1, 0, 2)
-    up_own = exchange(send_up).reshape(width, ffs)
-    down_own = exchange(send_down).transpose(1, 0, 2).reshape(ffs, width)
-    vocab_own = exchange(send_vocab).reshape(width, vcols)
-    up_other, down_other, vocab_other = swap(up_own), swap(down_own), swap(vocab_own)
-    wup = jnp.concatenate([up_own, up_other], axis=1)
-    wout = jnp.concatenate([wd, down_own, down_other], axis=0)
+    send_up, bias_other = lax.optimization_barrier((send_up, bias_other))
+    up_own = exchange(send_up)
     bias_first = jnp.where(ic == 0, bias_own, bias_other)
     bias_second = jnp.where(ic == 0, bias_other, bias_own)
     bj_all = jnp.where(iy == 0, bias_first, bias_second)[: nz * hcols].reshape(nz, hcols)
@@ -1438,7 +1666,6 @@
     )
     order = jnp.where(ic == 0, slots, anchor)
     back = jnp.where(ic == 0, slots, pair_order)
-    rows_low = take_blocks(natural, order, piece)
     anchor_hot = (anchor[:, None] == slots[None, :])[:, :, None]
     pair_ids = jnp.sum(jnp.where(anchor_hot, ids.reshape(1, blocks, piece), 0), axis=1).reshape(n, held)
     all_ids = jnp.stack([ids, pair_ids])
@@ -1455,43 +1682,46 @@
     ).astype(F32)
     targets = jnp.concatenate([all_ids[:, :, 1:], jnp.zeros((2, n, 1), jnp.int32)], axis=2)
 
-    rows_float = rows_low.astype(F32)
-    hat, inverse = normed(rows_float)
+    hat, inverse = normed(natural.astype(F32))
     ga, sa, gm, sm, gf, sf = (
         v.astype(F32) for v in (attn_gain, attn_shift, mlp_gain, mlp_shift, final_gain, final_shift)
     )
     attn_low = (hat * ga + sa).astype(BF16)
     mlp_low = (hat * gm + sm).astype(BF16)
-    frequency = jnp.exp(jnp.arange(ROT // 2, dtype=F32) * (-2.0 * math.log(10000.0) / ROT))
+    lane = jnp.arange(HD, dtype=jnp.int32)
+    frequency = jnp.exp((lane % (ROT // 2)).astype(F32) * (-2.0 * math.log(10000.0) / ROT))
     angles = position.reshape(total)[:, None].astype(F32) * frequency[None, :]
-    cosine, sine = jnp.cos(angles), jnp.sin(angles)
+    cosine = jnp.where(lane < ROT, jnp.cos(angles), 1.0)
+    sine = jnp.sin(angles)
+    tables = jnp.stack(
+        [
+            cosine,
+            jnp.where(lane < ROT // 2, -sine, 0.0),
+            jnp.where((lane >= ROT // 2) & (lane < ROT), sine, 0.0),
+        ]
+    )
     fused = dot(attn_low, wj, (1, 0)) + bj
-    query = turn(fused[:, :HD], cosine, sine).astype(BF16)
-    keys = turn(fused[:, HD : 2 * HD], cosine, sine).astype(BF16)
-    values = fused[:, 2 * HD :].astype(BF16)
-    q3, k3, v3 = (a.reshape(n, held, HD) for a in (query, keys, values))
-    scores = jnp.einsum("grd,gcd->grc", q3, k3, preferred_element_type=F32) / math.sqrt(HD)
-    scores = jnp.where(allowed, scores, masked_score)
-    highest = jnp.max(scores, axis=-1, keepdims=True)
-    weights = jnp.exp(scores - highest)
-    probs = weights / jnp.sum(weights, axis=-1, keepdims=True)
-    probs_low = probs.astype(BF16)
-    mixed = (
-        jnp.einsum("grc,gcd->grd", probs_low, v3, preferred_element_type=F32)
-        .astype(BF16)
-        .reshape(total, HD)
-    )
+    qkv, probs, mixed = attention(order, fused, tables, allowed.astype(F32), piece)
+    up_own, mixed, send_vocab = lax.optimization_barrier((up_own, mixed, send_vocab))
+    up_other = swap(up_own)
+    vocab_got = exchange(send_vocab)
+    wup = jnp.concatenate([w.reshape(width, ffs) for w in (up_own, up_other)], axis=1)
     hidden = dot(mlp_low, wup, (1, 0)) + bu
     bell = 0.5 * (1.0 + lax.erf(hidden * math.sqrt(0.5)))
     active = (hidden * bell).astype(BF16)
-    outs_low = jnp.concatenate([mixed, active], axis=1)
+    gelu_slope = bell + hidden * jnp.exp(-0.5 * hidden * hidden) * (1.0 / math.sqrt(2.0 * math.pi))
+    outs_low = place(order, mixed, active, piece)
     branch_part = dot(outs_low, wout, (1, 0)).astype(BF16)
     share = total // chips
     chip = dp * nx + ix
-    rows_here = lax.dynamic_slice_in_dim(rows_low, chip * share, share, 0)
+    first_row = jnp.sum(jnp.where(slots == chip * share // piece, order, 0)) * piece + chip * share % piece
+    rows_here = lax.dynamic_slice_in_dim(natural, first_row, share, 0)
     bias_out = (b_dense.astype(F32) + b_down.astype(F32))[None]
     final, resid = reduce_norm_gather(nz, branch_part, rows_here, bias_out, gf[None], sf[None])
 
+    vocab_got, final = lax.optimization_barrier((vocab_got, final))
+    vocab_own = vocab_got.reshape(width, vcols)
+    vocab_other = swap(vocab_own)
     my_targets = jnp.where(ic == 0, targets[0], targets[1]).reshape(total)
     logits = [dot(final, w, (1, 0)) for w in (vocab_own, vocab_other)]
     hits = [
@@ -1517,30 +1747,20 @@
     gv_own = dot(final, dlogits[0], (0, 0))
     gv_other = dot(final, dlogits[1], (0, 0)).astype(BF16)
     dfinal_part = (dot(dlogits[0], vocab_own, (1, 1)) + dot(dlogits[1], vocab_other, (1, 1))).astype(BF16)
+    gv = (gv_own + swap(gv_other).astype(F32)).astype(BF16)
+    gv, dfinal_part = lax.optimization_barrier((gv, dfinal_part))
+    early_cols = vcols * 272 // 800
+    gv = gv.reshape(n, depth, vcols)
+    grad_early = exchange(gv[:, :, :early_cols])
     dbranch, final_vectors = reduce_back_gather(nz, dfinal_part, resid, gf[None])
-    gv = (gv_own + swap(gv_other).astype(F32)).astype(BF16)
-    grad_vocab = (
-        exchange(gv.reshape(n, depth, vcols)).transpose(1, 0, 2).reshape(depth, n * vcols).astype(F32)
-    )
+    gv_late, dbranch, grad_early = lax.optimization_barrier((gv[:, :, early_cols:], dbranch, grad_early))
+    grad_late = exchange(gv_late)
+    grad_vocab = jnp.concatenate([grad_early, grad_late], axis=2).transpose(1, 0, 2).reshape(depth, n * vcols)
+    grad_vocab = lax.optimization_barrier(grad_vocab).astype(F32)
 
     gout = dot(outs_low, dbranch, (0, 0))
     douts = dot(dbranch, wout, (1, 1))
-    dmixed = douts[:, :HD].astype(BF16).reshape(n, held, HD)
-    slope_of = bell + hidden * jnp.exp(-0.5 * hidden * hidden) * (1.0 / math.sqrt(2.0 * math.pi))
-    dhidden = (douts[:, HD:] * slope_of).astype(BF16)
-    dvalues = jnp.einsum("grc,grd->gcd", probs_low, dmixed, preferred_element_type=F32)
-    dprobs = jnp.einsum("grd,gcd->grc", dmixed, v3, preferred_element_type=F32)
-    dscores = (probs * (dprobs - jnp.sum(probs * dprobs, axis=-1, keepdims=True))).astype(BF16)
-    dquery = jnp.einsum("grc,gcd->grd", dscores, k3, preferred_element_type=F32) / math.sqrt(HD)
-    dkeys = jnp.einsum("grc,grd->gcd", dscores, q3, preferred_element_type=F32) / math.sqrt(HD)
-    dfused = jnp.concatenate(
-        [
-            turn(dquery.reshape(total, HD), cosine, -sine),
-            turn(dkeys.reshape(total, HD), cosine, -sine),
-            dvalues.reshape(total, HD),
-        ],
-        axis=1,
-    ).astype(BF16)
+    dfused, dhidden, bias_sums = attention_back(order, douts, gelu_slope, qkv, probs, tables, piece)
     gj = dot(attn_low, dfused, (0, 0)).astype(BF16)
     gu = dot(mlp_low, dhidden, (0, 0))
     dattn = dot(dfused, wj, (1, 1))
@@ -1550,18 +1770,17 @@
     g_mlp_gain = jnp.sum(dmlp * hat, axis=0)
     g_mlp_shift = jnp.sum(dmlp, axis=0)
     t_part = (dattn * ga + dmlp * gm).astype(BF16)
-    t_part = take_blocks(t_part, back, piece)
-
-    gout_low = gout.astype(BF16)
-    gu_low = gu.astype(BF16)
-    gdown = gout[HD : HD + ffs] + swap(gout_low[HD + ffs :]).astype(F32)
-    gup = gu[:, :ffs] + swap(gu_low[:, ffs:]).astype(F32)
-    grad_down = exchange(
-        gdown.astype(BF16).reshape(ffs, n, depth).transpose(1, 0, 2)
-    ).reshape(n * ffs, depth).astype(F32)
-    grad_up = (
-        exchange(gup.astype(BF16).reshape(n, depth, ffs)).transpose(1, 0, 2).reshape(depth, n * ffs).astype(F32)
-    )
+
+    def to_send(up, down):
+        return jnp.concatenate(
+            [up.reshape(n, depth, ffs), down.reshape(ffs, n, depth).transpose(1, 0, 2)], axis=1
+        )
+
+    give_grads = to_send(gu[:, ffs:].astype(BF16), gout[HD + ffs :].astype(BF16))
+    layer_grads = to_send(gu[:, :ffs], gout[HD : HD + ffs]) + swap(give_grads).astype(F32)
+    layer_grads = exchange(layer_grads.astype(BF16))
+    grad_up = layer_grads[:, :depth].transpose(1, 0, 2).reshape(depth, n * ffs).astype(F32)
+    grad_down = layer_grads[:, depth:].reshape(n * ffs, depth).astype(F32)
 
     share2 = total // (2 * chips)
 
@@ -1570,8 +1789,7 @@
         place = jnp.sum(jnp.where(slots == first // piece, back, 0)) * piece + first % piece
         return lax.dynamic_slice_in_dim(dbranch, place, share2, 0)
 
-    gbj = jnp.sum(dfused.astype(F32), axis=0)
-    gbu = jnp.sum(dhidden.astype(F32), axis=0)
+    gbj, gbu = bias_sums[0, :hcols], bias_sums[0, hcols:]
     spare = jnp.zeros((8 * HD - hcols - ffs,), F32)
     keep = jnp.concatenate([gbj, gbu[:ffs], spare]).reshape(8, HD)
     give = jnp.concatenate([gbj, gbu[ffs:], spare]).reshape(8, HD)
@@ -1592,7 +1810,7 @@
         keep,
         give,
         gj,
-        gout_low[:HD],
+        gout[:HD].astype(BF16),
     )
     grad_input = rows_out.reshape(held, width).astype(F32)
     grad_joined, grad_dense = grad_joined.astype(F32), grad_dense.astype(F32)

time: 726 us -> 609 us (0.84)
  Pallas kernels: 435 us -> 362 us
  waiting for transfers between devices: 45.4 us -> 0.02 us
  starting transfers between devices: 39.3 us -> 49.4 us
  matrix products: 97.5 us -> 88.5 us
    pallas_call x1, Pallas kernels: 119 us -> 64.8 us  [front(): pl.pallas_call(functools.partial(front_kernel, nz, half), out_shape=[jax....]
    all_to_all x6 -> x5, waiting for transfers between devices: 45.3 us -> 0.01 us  [exchange(): return lax.all_to_all(value, DP, split_axis=0, concat_axis=0, tiled=True)]
    ppermute x6 -> x4, starting transfers between devices: 3.52 us -> 24.4 us  [swap(): return lax.ppermute(value, 'c', SWAP)]
    pallas_call x2 -> x3, Pallas kernels: 21.8 us -> 7.7 us  [the longest x1 3.55 us: attention(): pl.pallas_call(functools.partial(attention_kernel, piece), out_shape=[jax...]
    pallas_call x1, Pallas kernels: 95.8 us -> 110 us  [reduce_norm_gather(): pl.pallas_call(functools.partial(forward_kernel, nz, half), out_shape=[ja...]
    unnamed x132 -> x88, local copies, waits for them, and re-layouts: 25.3 us -> 37.8 us
    all_to_all x6 -> x5, starting transfers between devices: 35.8 us -> 25 us  [exchange(): return lax.all_to_all(value, DP, split_axis=0, concat_axis=0, tiled=True)]
    pallas_call x1, Pallas kernels: 21.2 us -> 11.7 us  [objective(): pl.pallas_call(functools.partial(objective_kernel, nz, hot.shape[0], seq_...]
  transfers between devices with their start and end apart: 12 -> 9, of which waited for: 4 -> 0; matrix products, arithmetic and copies ran while one was open for 19% -> 20% of each run, Pallas kernels for 44% -> 48%
where the time goes in v2:
time: 609 us; the launch traced here: 599 us
  Pallas kernels  362 us (59%)
  matrix products  88.5 us (15%)
  local copies, waits for them, and re-layouts  62.5 us (10%)
  starting transfers between devices  49.4 us (8%)
  other arithmetic  32.1 us (5%)
    pallas_call x1, Pallas kernels, reduce_norm_gather(): pl.pallas_call(functools.partial(forward_kernel, nz, half), out_shape=[ja...  110 us
    pallas_call x1, Pallas kernels, reduce_back_gather(): pl.pallas_call(functools.partial(backward_kernel, nz, half), out_shape=[j...  88.6 us
    dot_general x15, matrix products, dot(): lax.dot_general(a, b, ((contract[:1], contract[1:]), ((), ())), preferred...  88.5 us
    pallas_call x1, Pallas kernels, end(): pl.pallas_call(functools.partial(end_kernel, nz, half), out_shape=[jax.Sh...  79.7 us
    pallas_call x1, Pallas kernels, front(): pl.pallas_call(functools.partial(front_kernel, nz, half), out_shape=[jax....  64.8 us
    unnamed x88, local copies, waits for them, and re-layouts  37.8 us
    all_to_all x5, starting transfers between devices, exchange(): return lax.all_to_all(value, DP, split_axis=0, concat_axis=0, tiled=True)  25 us
    ppermute x4, starting transfers between devices, swap(): return lax.ppermute(value, 'c', SWAP)  24.4 us
  transfers between devices with their start and end apart: 9, of which 0 were waited for; matrix products, arithmetic and copies ran while one was open for 20% of the time, Pallas kernels for 48%

profile of v2, /device:TPU:1, one launch (start us, length us, event | category | flops | bytes accessed | tf_op | source)
XLA Modules:
  0.0 598.8 jit_solution(3155251093918510546)
XLA Ops:
  0.7 2.3 copy.142
  6.4 1.2 copy-done.6
  8.6 1.1 copy-done.10
  10.7 64.8 %shard_map.349 = (bf16[4,2,2,2,32,2048]{5,4,3,2,1,0:T(8,128)(2,1)S(1)}, f32[4,2,4,128]{3,2,1,0:T(4,128)S(1)}, f32[28,128]{1,0:T(8,128)S(1)}, bf16[2048,384]{1,0:T(8,128)(2,1)S(1)}, bf16[640,2048]{1,0:T(8,128)(2,1)S(1)}) custom-call(bf16[128,2048]{1,0:T(8,128)(2,1)S(1)} %copy-done.7, f32[4,128]{1,0:T(4,128)S(1)} %pad_maximum_fusion.12.info, ...), custom_call_target="tpu_custom_call" | custom-call | bytes 135000000 | tf_op jit(solution)/shard_map/pallas_call | solution.py:1222
  75.5 1.9 copy-done
  77.4 1.5 copy-done.18
  78.9 4.2 all-to-all-start
  83.6 3.0 convert_reduce_fusion
  87.0 1.3 fusion.1
  88.9 2.0 fusion.12
  91.4 5.6 copy.149
  97.8 5.9 add_convert_fusion.2
  103.7 2.3 convolution_add_fusion.fused
  106.1 3.5 shard_map.350
  111.4 5.7 all-to-all-start.1
  119.5 1.5 copy.150
  121.0 2.6 copy.151
  123.6 6.9 %fusion.6 = (f32[1024,512]{1,0:T(8,128)}, bf16[1024,512]{1,0:T(8,128)(2,1)S(1)}) fusion(f32[512]{0:T(512)S(1)} %bitcast.214, bf16[1024,2048]{1,0:T(8,128)(2,1)} %get-tuple-element.195, bf16[2048,256]{1,0:T(8,128)(2,1)} %bitcast.186, bf16[2048,256]{1,0:T(8,128)(2,1)S(1)} %bitcast.184), kind=kOutput, calls=%fused_computation.30 | convolution fusion | flops 2157445120 | bytes 9439232 | tf_op jit(solution)/shard_map/dot_general | solution.py:433
  131.2 4.9 convolution_convert_fusion
  136.2 109.9 %shard_map.352 = (bf16[4,2,2,64,2048]{4,3,2,1,0:T(8,128)(2,1)S(1)}, f32[64,2048]{1,0:T(8,128)S(1)}) custom-call(bf16[4,2,2,64,2048]{4,3,2,1,0:T(8,128)(2,1)} %bitcast.179, bf16[64,2048]{1,0:T(8,128)(2,1)S(1)} %constant_dynamic-slice_fusion.3.rows, f32[1,2048]{1,0:T(1,128)S(1)} %bitcast.154, f32[1,2048]{1,0:T(1,128)S(1)} %bitcast.151, f32[1,2048]{1,0:T(1,128)S(1)} %bitcast.153), custom_call_target="tpu_custom_call" | custom-call | bytes 270000000 | tf_op jit(solution)/shard_map/pallas_call | solution.py:880
  246.9 2.0 copy-done.16
  248.9 4.1 copy.169
  252.9 10.2 %collective-permute-start.1 = (bf16[2048,800]{0,1:T(8,128)(2,1)}, bf16[2048,800]{0,1:T(8,128)(2,1)}, u32[]{:S(2)}, u32[]{:S(2)}) collective-permute-start(bf16[2048,800]{0,1:T(8,128)(2,1)} %bitcast.81), channel_id=1, source_target_pairs={{0,1},{1,0},{2,3},{3,2},{4,5},{5,4},{6,7},{7,6},{8,9},{9,8},{10,11... | collective-permute-start | bytes 9830408 | tf_op jit(solution)/shard_map/ppermute | solution.py:437
  263.7 6.5 %fusion.41 = (f32[1024]{0:T(1024)S(1)}, f32[1024,800]{0,1:T(8,128)S(1)}) fusion(bf16[1024,2048]{1,0:T(8,128)(2,1)} %bitcast.157, bf16[2048,800]{0,1:T(8,128)(2,1)} %bitcast.81), kind=kOutput, calls=%fused_computation.142 | convolution fusion | flops 3356261376 | bytes 10752000 | tf_op jit(solution)/shard_map/dot_general | solution.py:433
  270.3 5.7 fusion.42
  276.0 1.7 exponential_reduce_fusion
  277.7 11.7 %shard_map.353 = (f32[8,128]{1,0:T(8,128)S(1)}, f32[8,128]{1,0:T(8,128)S(1)}, f32[2,8,128]{2,1,0:T(8,128)S(1)}) custom-call(f32[3,8,128]{2,1,0:T(8,128)S(1)} %pad_maximum_fusion.6.stats, f32[3,8,128]{2,1,0:T(8,128)S(1)} %fusion.13.hot, f32[8,128]{1,0:T(8,128)S(1)} %pad_convert_fusion.scored, f32[2,8,128]{2,1,0:T(8,128)S(1)} %pad_maximum_fusion.7.refs, ...), custom_call_target="tpu_custom_call" | custom-call | bytes 45000000 | tf_op jit(solution)/shard_map/pallas_call | solution.py:985
  289.4 4.0 convolution_convert_fusion.1
  293.6 9.0 %fusion.32 = f32[1024,2048]{1,0:T(8,128)} fusion(bf16[2048,800]{0,1:T(8,128)(2,1)} %bitcast.81, f32[1024,800]{0,1:T(8,128)S(1)} %get-tuple-element.232, f32[1024]{0:T(1024)S(1)} %bitcast.166, f32[1024]{0:T(1024)S(1)} %bitcast.162, s32[1024]{0:T(1024)S(1)} %get-tuple-element.218), kind=kOutput, calls=%fused_computation.133 | convolution fusion | flops 3360358400 | bytes 14954496 | tf_op jit(solution)/shard_map/dot_general | solution.py:433
  302.6 9.7 %add_convert_fusion.1 = bf16[1024,2048]{1,0:T(8,128)(2,1)} fusion(f32[1024,2048]{1,0:T(8,128)} %fusion.32, bf16[2048,800]{0,1:T(8,128)(2,1)} %collective-permute-done.1, f32[1024,800]{0,1:T(8,128)S(1)} %get-tuple-element.234, f32[1024]{0:T(1024)S(1)} %bitcast.167, f32[1024]{0:T(1024)S(1)} %bitcast.163, s32[1024]{0:T(1024)S(1)} %get-tuple-element.219), kind=kOutput, calls=%fused_computation.7 | convolution fusion | flops 3364552704 | bytes 19148800 | tf_op jit(solution)/shard_map/dot_general | solution.py:433
  312.3 3.9 add_convert_fusion.4
  316.3 1.1 copy.170
  317.4 1.7 copy-done.21
  319.2 1.2 copy.165
  320.4 4.4 all-to-all-start.2
  324.8 1.8 slice.158
  326.6 1.8 copy.164
  328.5 88.6 %shard_map.354 = (bf16[4,2,2,64,2048]{4,3,2,1,0:T(8,128)(2,1)S(1)}, f32[3,2048]{1,0:T(4,128)S(1)}) custom-call(bf16[4,2,2,64,2048]{4,3,2,1,0:T(8,128)(2,1)} %bitcast.178, f32[64,2048]{1,0:T(8,128)S(1)} %copy-done.12, f32[1,2048]{1,0:T(1,128)S(1)} %bitcast.152), custom_call_target="tpu_custom_call" | custom-call | bytes 270000000 | tf_op jit(solution)/shard_map/pallas_call | solution.py:900
  417.1 2.0 copy-done.2
  419.1 7.5 %fusion.43 = (bf16[640,2048]{1,0:T(8,128)(2,1)S(1)}, f32[640,2048]{1,0:T(8,128)}) fusion(bf16[1024,640]{1,0:T(8,128)(2,1)S(1)} %shard_map.351, bf16[1024,2048]{1,0:T(8,128)(2,1)} %bitcast.148), kind=kOutput, calls=%fused_computation.144 | convolution fusion | flops 2685665280 | bytes 13369344 | tf_op jit(solution)/shard_map/dot_general | solution.py:433
  426.6 1.5 copy-done.23
  429.2 4.6 all-to-all-start.4
  433.9 6.2 %fusion.44.douts = f32[1024,640]{1,0:T(8,128)S(1)} fusion(bf16[1024,2048]{1,0:T(8,128)(2,1)} %bitcast.149, bf16[640,2048]{1,0:T(8,128)(2,1)} %copy-done.18), kind=kOutput, calls=%fused_computation.145 | convolution fusion | flops 2684354560 | bytes 9437184 | tf_op jit(solution)/shard_map/dot_general | solution.py:433
  440.1 3.5 shard_map.355
  443.6 2.4 fusion.46
  446.2 1.9 copy-done.22
  448.1 1.5 pad_maximum_fusion.2
  449.6 13.5 %collective-permute-start.3 = (bf16[8,512,256]{2,1,0:T(8,128)(2,1)}, bf16[8,512,256]{2,1,0:T(8,128)(2,1)}, u32[]{:S(2)}, u32[]{:S(2)}) collective-permute-start(bf16[8,512,256]{2,1,0:T(8,128)(2,1)} %pad_maximum_fusion.2), channel_id=1, source_target_pairs={{0,1},{1,0},{2,3},{3,2},{4,5},{5,4},{6,7},{7,6},{8,9},{9,8},{10,11... | collective-permute-start | bytes 6291464 | tf_op jit(solution)/shard_map/ppermute | solution.py:437
  466.5 1.1 slice.160.dense_in
  467.6 1.8 slice.164
  469.6 5.6 fusion.45
  475.3 3.6 fusion.2
  478.9 6.0 %all-to-all-start.3 = ((bf16[8,512,256]{2,1,0:T(8,128)(2,1)}), bf16[8,512,256]{2,1,0:T(8,128)(2,1)}, u32[]{:S(2)}, u32[]{:S(2)}) async-start(bf16[8,512,256]{2,1,0:T(8,128)(2,1)} %fusion.2), calls=%async_computation.3 | async-start | bytes 4194304 | tf_op jit(solution)/shard_map/all_to_all | solution.py:453
  484.9 9.3 %fusion.34 = (f32[2048]{0:T(1024)S(1)}, f32[2048]{0:T(1024)S(1)}, bf16[1024,2048]{1,0:T(8,128)(2,1)}, f32[2048]{0:T(1024)S(1)}, f32[2048]{0:T(1024)S(1)}) fusion(f32[1024]{0:T(1024)S(1)} %rsqrt.12, f32[1024]{0:T(1024)S(1)} %div.31, bf16[4,2,2,2,32,2048]{5,4,3,2,1,0:T(8,128)(2,1)} %copy-done, f32[2048]{0:T(1024)S(1)} %convert_element_type.219, ...), kind=kOutput, calls=%fused_computation.135 | convolution fusion | flops 2178932736 | bytes 19980288 | tf_op jit(solution)/shard_map/dot_general | solution.py:433
  494.3 1.1 constant_dynamic-slice_fusion.1
  495.4 4.6 convolution_convert_fusion.2.joined_in
  500.0 79.7 %shard_map.356 = (bf16[2,2,32,2048]{3,2,1,0:T(8,128)(2,1)S(1)}, f32[8,2048]{1,0:T(8,128)S(1)}, f32[4,2,8,128]{3,2,1,0:T(8,128)S(1)}, bf16[256,1536]{1,0:T(8,128)(2,1)S(1)}, bf16[512,256]{1,0:T(8,128)(2,1)S(1)}) custom-call(bf16[4,2,2,2,32,2048]{5,4,3,2,1,0:T(8,128)(2,1)} %bitcast.177, bf16[32,2048]{1,0:T(8,128)(2,1)S(1)} %get-tuple-element.198.mine_rows, ...), custom_call_target="tpu_custom_call" | custom-call | bytes 210000000 | tf_op jit(solution)/shard_map/pallas_call | solution.py:1438
  579.7 1.3 convert_element_type.242
  583.7 1.1 bitcast_convert_fusion.1
  584.8 2.1 pad_maximum_fusion
  587.0 4.0 copy.162
  591.0 2.7 fusion.36
  594.4 1.8 copy.161
  596.2 1.5 bitcast_convert_fusion
  (174 shorter events, 21.6 us)
Async XLA Ops:
  6.4 1.2 copy-start.6
  7.6 1.0 copy-start.7
  8.6 1.1 copy-start.10
  9.8 0.9 copy-start.15
  75.5 2.0 copy-start
  77.4 1.5 copy-start.18
  78.9 24.8 %copy-start.4 = (bf16[2048,384]{1,0:T(8,128)(2,1)}, bf16[2048,384]{1,0:T(8,128)(2,1)S(1)}, u32[]{:S(2)}) copy-start(bf16[2048,384]{1,0:T(8,128)(2,1)S(1)} %get-tuple-element.56) | copy-start | bytes 4718596
  78.9 32.4 %all-to-all-start = ((bf16[8,256,256]{1,2,0:T(8,128)(2,1)}), bf16[8,256,256]{1,2,0:T(8,128)(2,1)}, u32[]{:S(2)}, u32[]{:S(2)}) async-start(bf16[8,256,256]{1,2,0:T(8,128)(2,1)} %bitcast.1), calls=%async_computation | async-start | bytes 2097152 | tf_op jit(solution)/shard_map/all_to_all | solution.py:453
  83.6 3.5 copy-start.1
  88.3 2.8 copy-start.38
  88.3 3.0 copy-start.30
  88.3 3.0 copy-start.31
  88.3 3.1 copy-start.32
  88.3 3.1 copy-start.33
  103.7 2.4 copy-start.26
  109.6 0.9 copy-start.8
  110.5 0.8 copy-start.13
  111.3 7.0 %copy-start.34 = (bf16[2048]{0:T(1024)(128)(2,1)S(1)}, bf16[2048]{0:T(1024)(128)(2,1)}, u32[]{:S(2)}) copy-start(bf16[2048]{0:T(1024)(128)(2,1)} %param.41) | copy-start | bytes 12292
  111.3 7.0 %copy-start.35 = (bf16[2048]{0:T(1024)(128)(2,1)S(1)}, bf16[2048]{0:T(1024)(128)(2,1)}, u32[]{:S(2)}) copy-start(bf16[2048]{0:T(1024)(128)(2,1)} %param.42) | copy-start | bytes 12292
  111.3 7.1 %copy-start.36 = (bf16[2048]{0:T(1024)(128)(2,1)S(1)}, bf16[2048]{0:T(1024)(128)(2,1)}, u32[]{:S(2)}) copy-start(bf16[2048]{0:T(1024)(128)(2,1)} %param.40) | copy-start | bytes 12292
  111.4 7.1 %copy-start.37 = (bf16[2048]{0:T(1024)(128)(2,1)S(1)}, bf16[2048]{0:T(1024)(128)(2,1)}, u32[]{:S(2)}) copy-start(bf16[2048]{0:T(1024)(128)(2,1)} %param.36) | copy-start | bytes 12292
  111.4 137.5 %all-to-all-start.1 = ((bf16[8,256,800]{1,2,0:T(8,128)(2,1)}), bf16[8,256,800]{1,2,0:T(8,128)(2,1)}, u32[]{:S(2)}, u32[]{:S(2)}) async-start(bf16[8,256,800]{1,2,0:T(8,128)(2,1)} %bitcast.169), calls=%async_computation.1 | async-start | bytes 6553600 | tf_op jit(solution)/shard_map/all_to_all | solution.py:453
  117.1 3.9 collective-permute-start
  121.0 9.6 %copy-start.28 = (bf16[8,256,256]{2,1,0:T(8,128)(2,1)}, bf16[8,256,256]{2,1,0:T(8,128)(2,1)S(1)}, u32[]{:S(2)}) copy-start(bf16[8,256,256]{2,1,0:T(8,128)(2,1)S(1)} %copy.150) | copy-start | bytes 3145732
  123.6 7.6 %copy-start.19 = (bf16[640,2048]{1,0:T(8,128)(2,1)S(1)}, bf16[640,2048]{1,0:T(8,128)(2,1)}, u32[]{:S(2)}) copy-start(bf16[640,2048]{1,0:T(8,128)(2,1)} %copy-done.18) | copy-start | bytes 7864324
  246.1 0.8 copy-start.11
  246.8 2.0 copy-start.16
  252.9 17.3 %collective-permute-start.1 = (bf16[2048,800]{0,1:T(8,128)(2,1)}, bf16[2048,800]{0,1:T(8,128)(2,1)}, u32[]{:S(2)}, u32[]{:S(2)}) collective-permute-start(bf16[2048,800]{0,1:T(8,128)(2,1)} %bitcast.81), channel_id=1, source_target_pairs={{0,1},{1,0},{2,3},{3,2},{4,5},{5,4},{6,7},{7,6},{8,9},{9,8},{10,11... | collective-permute-start | bytes 9830408 | tf_op jit(solution)/shard_map/ppermute | solution.py:437
  263.7 6.6 %copy-start.17 = (bf16[4,2,2,64,2048]{4,3,2,1,0:T(8,128)(2,1)S(1)}, bf16[4,2,2,64,2048]{4,3,2,1,0:T(8,128)(2,1)}, u32[]{:S(2)}) copy-start(bf16[4,2,2,64,2048]{4,3,2,1,0:T(8,128)(2,1)} %copy-done.16) | copy-start | bytes 12582916
  293.4 18.9 %collective-permute-start.2 = (bf16[2048,800]{0,1:T(8,128)(2,1)S(1)}, bf16[2048,800]{0,1:T(8,128)(2,1)S(1)}, u32[]{:S(2)}, u32[]{:S(2)}) collective-permute-start(bf16[2048,800]{0,1:T(8,128)(2,1)S(1)} %convolution_convert_fusion.1), channel_id=1, source_target_pairs={{0,1},{1,0},{2,3},{3,2},{4,5},{5,4},{6,7},{7,6},{8,9},{9,8},{10,11... | collective-permute-start | bytes 9830408 | tf_op jit(solution)/shard_map/ppermute | solution.py:437
  317.4 1.7 copy-start.21
  320.4 98.7 %all-to-all-start.2 = ((bf16[8,256,272]{1,2,0:T(8,128)(2,1)}), bf16[8,256,272]{1,2,0:T(8,128)(2,1)}, u32[]{:S(2)}, u32[]{:S(2)}) async-start(bf16[8,256,272]{1,2,0:T(8,128)(2,1)} %copy.165), calls=%async_computation.2 | async-start | bytes 2228224 | tf_op jit(solution)/shard_map/all_to_all | solution.py:453
  324.8 3.6 copy-start.12
  417.1 2.0 copy-start.2
  426.6 1.5 copy-start.23
  429.2 49.6 %all-to-all-start.4 = ((bf16[8,256,528]{1,2,0:T(8,128)(2,1)}), bf16[8,256,528]{1,2,0:T(8,128)(2,1)}, u32[]{:S(2)}, u32[]{:S(2)}) async-start(bf16[8,256,528]{1,2,0:T(8,128)(2,1)} %copy.164), calls=%async_computation.4 | async-start | bytes 4325376 | tf_op jit(solution)/shard_map/all_to_all | solution.py:453
  433.8 6.3 %copy-start.3 = (f32[1024,512]{1,0:T(8,128)S(1)}, f32[1024,512]{1,0:T(8,128)}, u32[]{:S(2)}) copy-start(f32[1024,512]{1,0:T(8,128)} %get-tuple-element.199.slope) | copy-start | bytes 6291460
  433.8 6.3 %copy-start.9 = (bf16[1024,384]{1,0:T(8,128)(2,1)S(1)}, bf16[1024,384]{1,0:T(8,128)(2,1)}, u32[]{:S(2)}) copy-start(bf16[1024,384]{1,0:T(8,128)(2,1)} %copy-done.8) | copy-start | bytes 2359300
  433.8 6.3 %copy-start.14 = (f32[8,128,128]{2,1,0:T(8,128)S(1)}, f32[8,128,128]{2,1,0:T(8,128)}, u32[]{:S(2)}) copy-start(f32[8,128,128]{2,1,0:T(8,128)} %copy-done.13) | copy-start | bytes 1572868
  440.1 3.5 copy-start.27
  443.6 2.4 copy-start.20
  443.6 4.5 copy-start.25
  446.0 2.1 copy-start.22
  449.6 25.7 %collective-permute-start.3 = (bf16[8,512,256]{2,1,0:T(8,128)(2,1)}, bf16[8,512,256]{2,1,0:T(8,128)(2,1)}, u32[]{:S(2)}, u32[]{:S(2)}) collective-permute-start(bf16[8,512,256]{2,1,0:T(8,128)(2,1)} %pad_maximum_fusion.2), channel_id=1, source_target_pairs={{0,1},{1,0},{2,3},{3,2},{4,5},{5,4},{6,7},{7,6},{8,9},{9,8},{10,11... | collective-permute-start | bytes 6291464 | tf_op jit(solution)/shard_map/ppermute | solution.py:437
  467.6 2.1 copy-start.5
  469.6 5.6 slice-start
  478.9 112.1 %all-to-all-start.3 = ((bf16[8,512,256]{2,1,0:T(8,128)(2,1)}), bf16[8,512,256]{2,1,0:T(8,128)(2,1)}, u32[]{:S(2)}, u32[]{:S(2)}) async-start(bf16[8,512,256]{2,1,0:T(8,128)(2,1)} %fusion.2), calls=%async_computation.3 | async-start | bytes 4194304 | tf_op jit(solution)/shard_map/all_to_all | solution.py:453
  583.7 14.0 %copy-start.29 = (f32[1,2048]{1,0:T(1,128)}, f32[1,2048]{1,0:T(1,128)S(1)}, u32[]{:S(2)}) copy-start(f32[1,2048]{1,0:T(1,128)S(1)} %get-tuple-element.205) | copy-start | bytes 24580
  594.4 1.8 copy-start.24

commit v3 on v2

--- a/solution.py
+++ b/solution.py
@@ -5,6 +5,7 @@
 import jax.numpy as jnp
 from jax import lax
 from jax.experimental import pallas as pl
+from jax.experimental.layout import Layout, with_layout_constraint
 from jax.experimental.pallas import tpu as pltpu
 from jax.sharding import PartitionSpec as P
 
@@ -492,6 +493,16 @@
     ).wait_send()
 
 
+PIECES = 1
+
+
+def in_pieces(source, target, out_sem, in_sem, device):
+    size = source.shape[1] // PIECES
+    for i in range(PIECES):
+        at = (slice(None), pl.ds(i * size, size))
+        send(source.at[at], target.at[at], out_sem, in_sem, device)
+
+
 def greet(devices):
     barrier = pltpu.get_barrier_semaphore()
     for device in devices:
@@ -522,10 +533,8 @@
             pltpu.VMEM((parts, nz, half, width), BF16),
             pltpu.VMEM((parts, nz, half, width), BF16),
             pltpu.VMEM((parts, nz, half, width), BF16),
-            pltpu.VMEM((parts, nz, half, width), BF16),
             dma((parts, nz, 2)),
             dma((parts, nz, 2)),
-            dma((parts, nz)),
             dma((parts, nz)),
             dma((parts, nz)),
             dma((parts, nz)),
@@ -540,15 +549,13 @@
             self.out2,
             self.in2,
             self.out3,
-            self.below,
-            self.above,
+            self.in3,
             self.s1,
             self.r1,
             self.s2,
             self.r2,
             self.s3,
-            self.rb,
-            self.ra,
+            self.r3,
         ) = refs
         self.copies = []
 
@@ -600,6 +607,7 @@
             )
 
     def third(self, h):
+        iz, iy, ix, ic = here()
         first, across = self.along(h)
         near = self.mine(h)
         for k in list(range(1, self.nz)) + [0]:
@@ -613,44 +621,17 @@
             )
             if k == 0:
                 return total
-            self.out3[h, z] = total.astype(BF16)
-
-    def hops(self, m):
-        up = [(z, m + 1, self.below, self.rb, m > 0) for z in range(self.nz - 1, m, -1)]
-        down = [(z, m - 1, self.above, self.ra, m < self.nz - 1) for z in range(m)]
-        return up + down
-
-    def chain(self, h):
-        iz, iy, ix, ic = here()
-        for m in range(self.nz):
-
-            @pl.when(iz == m)
-            def _():
-                for z, to, buffer, sems, waits in self.hops(m):
-                    device = (to, iy, ix, ic)
-                    if waits:
-                        arrived(buffer.at[h, z], self.s3.at[h, z], sems.at[h, z], device)
-                        self.out3[h, z] = (
-                            self.out3[h, z].astype(F32) + buffer[h, z].astype(F32)
-                        ).astype(BF16)
-                    send(self.out3.at[h, z], buffer.at[h, z], self.s3.at[h, z], sems.at[h, z], device)
-                if m == 0:
-                    self.below[h, m] = jnp.zeros(self.below.shape[2:], BF16)
-                if m == self.nz - 1:
-                    self.above[h, m] = jnp.zeros(self.above.shape[2:], BF16)
+            self.out3[h, k] = total.astype(BF16)
+            far = (z, iy, ix, ic)
+            in_pieces(self.out3.at[h, k], self.in3.at[h, k], self.s3.at[h, k], self.r3.at[h, k], far)
 
     def finish(self, h, total):
-        iz, iy, ix, ic = here()
-        for at_end, buffer, sems in (
-            (iz == 0, self.below, self.rb),
-            (iz == self.nz - 1, self.above, self.ra),
-        ):
-
-            @pl.when(jnp.logical_not(at_end))
-            def _():
-                arrived(buffer.at[h, iz], self.s3.at[h, iz], sems.at[h, iz], (1 - iz, iy, ix, ic))
-
-        return total + self.below[h, iz].astype(F32) + self.above[h, iz].astype(F32)
+        _, iy, ix, ic = here()
+        for k in range(1, self.nz):
+            z = self.plane(self.nz - k)
+            arrived(self.in3.at[h, k], self.s3.at[h, k], self.r3.at[h, k], (z, iy, ix, ic))
+            total = total + self.in3[h, k].astype(F32)
+        return total
 
     def end(self, parts):
         iz, iy, ix, ic = here()
@@ -658,15 +639,15 @@
             copy.wait_send()
         for h in parts:
             for k in range(1, self.nz):
-                z = self.plane(k)
-                left(self.out3.at[h, z], self.s3.at[h, z], self.rb.at[h, z], (z, iy, ix, ic))
+                far = (self.plane(k), iy, ix, ic)
+                left(self.out3.at[h, k], self.s3.at[h, k], self.r3.at[h, k], far)
 
 
 class Gather:
     @staticmethod
     def scratch(parts, nz):
         dma = pltpu.SemaphoreType.DMA
-        return [dma((parts, nz + 1)), dma((parts, nz)), dma((parts, nz, 2)), dma((parts, nz, 2, 2)), dma((parts,))]
+        return [dma((parts, nz)), dma((parts, nz)), dma((parts, nz, 2)), dma((parts, nz, 2, 2)), dma((parts,))]
 
     def __init__(self, nz, half, out, refs, forward=None, by_x=(0,)):
         self.by_x = by_x
@@ -683,45 +664,36 @@
         return self.out.at[z, y, x, pl.ds(h * self.half, self.half)]
 
     def on(self, h, source, z, y, x, which):
+        iz, iy, ix, ic = here()
         p, q = self.axes(h)
         there, got = self.block(h, z, y, x), self.r.at[h, z, y, x]
+        if "z" in which:
+            for k in range(1, self.nz):
+                far = (lax.rem(iz + k, self.nz), iy, ix, ic)
+                in_pieces(source, there, self.sz.at[h, k], got, far)
         if "p" in which:
-            send(source, there, self.sp.at[h, z], got, p)
+            self.copies.append(send(source, there, self.sp.at[h, z], got, p))
         if "q" in which:
-            send(source, there, self.sq.at[h, z, x if h not in self.by_x else y], got, q)
+            side = x if h not in self.by_x else y
+            self.copies.append(send(source, there, self.sq.at[h, z, side], got, q))
         if self.forward is not None:
             self.forward(h, source, z, y, x)
-
-    def along_z(self, h, source, z, step, sem):
-        iz, iy, ix, ic = here()
-        there = iz + step
-
-        @pl.when((there >= 0) & (there < self.nz))
-        def _():
-            send(source, self.block(h, z, iy, ix), self.sz.at[h, sem], self.r.at[h, z, iy, ix], (there, iy, ix, ic))
 
     def start(self, h, source):
         iz, iy, ix, _ = here()
         copy = pltpu.make_async_copy(source, self.block(h, iz, iy, ix), self.local.at[h])
         copy.start()
         self.locals.append(copy)
-        self.along_z(h, source, iz, 1, iz)
-        self.along_z(h, source, iz, -1, self.nz)
-        self.on(h, source, iz, iy, ix, "pq")
+        self.on(h, source, iz, iy, ix, "zpq")
 
     def got(self, h, z, y, x):
         arrived(self.block(h, z, y, x), self.sz.at[h, 0], self.r.at[h, z, y, x], self.axes(h)[0])
 
-    def first(self, h, distance, step):
+    def first(self, h, k):
         iz, iy, ix, _ = here()
-        z = iz - distance * step
-
-        @pl.when((z >= 0) & (z < self.nz))
-        def _():
-            self.got(h, z, iy, ix)
-            block = self.block(h, z, iy, ix)
-            self.along_z(h, block, z, step, z)
-            self.on(h, block, z, iy, ix, "pq")
+        z = lax.rem(iz + k, self.nz)
+        self.got(h, z, iy, ix)
+        self.on(h, self.block(h, z, iy, ix), z, iy, ix, "pq")
 
     def second(self, h, k):
         iz, iy, ix, _ = here()
@@ -748,10 +720,9 @@
     def firsts(self, parts):
         for h in parts:
             self.second(h, 0)
-        for distance in range(1, self.nz):
-            for step in (1, -1):
-                for h in parts:
-                    self.first(h, distance, step)
+        for k in self.turns():
+            for h in parts:
+                self.first(h, k)
 
     def seconds(self, parts):
         for k in self.turns():
@@ -772,29 +743,17 @@
         iz, iy, ix, ic = here()
         for copy in self.locals:
             copy.wait()
+        for copy in self.copies:
+            copy.wait_send()
         for h in parts:
-            p, q = self.axes(h)
-            for k in range(self.nz):
-                z = lax.rem(iz + k, self.nz)
-                block, got = self.block(h, z, iy, ix), self.r.at[h, z, iy, ix]
-                left(block, self.sp.at[h, z], got, p)
-                for side in (0, 1):
-                    left(block, self.sq.at[h, z, side], got, q)
-                up = (z <= iz) & (iz < self.nz - 1)
-                down = (z > iz) & (iz > 0)
-
-                @pl.when(up | down)
-                def _():
-                    left(block, self.sz.at[h, z], got, p)
-
-            @pl.when(iz > 0)
-            def _():
-                left(self.block(h, iz, iy, ix), self.sz.at[h, self.nz], self.r.at[h, iz, iy, ix], p)
+            for k in range(1, self.nz):
+                far = (lax.rem(iz + k, self.nz), iy, ix, ic)
+                left(self.block(h, iz, iy, ix), self.sz.at[h, k], self.r.at[h, iz, iy, ix], far)
 
 
 def reduce_gather(nz, half, part, out, refs, finished):
-    reduce = Reduce(nz, half, part, refs[:13], BY_X)
-    gather = Gather(nz, half, out, refs[13:], None, BY_X)
+    reduce = Reduce(nz, half, part, refs[:11], BY_X)
+    gather = Gather(nz, half, out, refs[11:], None, BY_X)
     greet(neighbours(nz))
     early, late = (0, 1), (2, 3)
 
@@ -812,14 +771,10 @@
         reduce.second(h)
     begin(late)
     kept = {h: reduce.third(h) for h in early}
-    for h in early:
-        reduce.chain(h)
     for h in late:
         reduce.second(h)
     finish(early, kept)
     kept = {h: reduce.third(h) for h in late}
-    for h in late:
-        reduce.chain(h)
     gather.firsts(early)
     finish(late, kept)
     gather.seconds(early)
@@ -863,7 +818,7 @@
 
 
 def anywhere():
-    return pl.BlockSpec(memory_space=pl.ANY)
+    return pl.BlockSpec(memory_space=pltpu.HBM)
 
 
 def busy(us):
@@ -889,7 +844,7 @@
         + Reduce.scratch(4, nz, half, width)
         + Gather.scratch(4, nz),
         cost_estimate=busy(90),
-        compiler_params=comm(2),
+        compiler_params=comm(2, 62),
     )(part.reshape(nz, 2, 2, share, width), rows, bias, gain, shift)
     return out.reshape(4 * nz * share, width), resid
 
@@ -909,7 +864,7 @@
         + Reduce.scratch(4, nz, half, width)
         + Gather.scratch(4, nz),
         cost_estimate=busy(90),
-        compiler_params=comm(3),
+        compiler_params=comm(3, 62),
     )(part.reshape(nz, 2, 2, share, width), resid, gain)
     return out.reshape(4 * nz * share, width), vectors
 
@@ -1080,11 +1035,17 @@
     joined_in,
     dense_in,
     down_in,
+    up_in,
+    vocab_in,
     natural,
     info_out,
     bias_out,
     joined_out,
     out_all,
+    up_all,
+    vocab_out,
+    vocab_here,
+    vs,
     fs,
     fr,
     js,
@@ -1126,6 +1087,8 @@
         def block(self, h, z, y, x):
             return rows_of(h, z, y, x, ic)
 
+    fetch = pltpu.make_async_copy(vocab_in, vocab_here, vs.at[0])
+    fetch.start()
     gather = Rows(nz, half, natural, refs, forward)
     first = pl.multiple_of((ix * 2 + ic) * 2 * half, 2 * half)
     for h in (0, 1):
@@ -1161,16 +1124,35 @@
 
     gather.firsts((0, 1))
 
+    def own_units(d):
+        rows, own, other = lanes(d, depth), pl.ds(0, units), pl.ds(units, units)
+        return [
+            (up_all.at[rows, own], up_all.at[rows, other]),
+            (down_out.at[:, rows], down_other.at[:, rows]),
+        ]
+
     line = [(lax.rem(iz + k, nz), iy, ix, ic) for k in range(1, nz)]
-    local = pltpu.make_async_copy(down_in.at[lanes(mine, units)], down_out.at[:, lanes(mine, depth)], dl.at[0])
-    local.start()
-    for device in line + across:
-        d = device[0] * 2 + device[1]
-        copies.append(
-            send(down_in.at[lanes(d, units)], down_out.at[:, lanes(mine, depth)], ds.at[d], dr.at[mine], device)
-        )
+    keep = []
+    for i, source in enumerate((up_in.at[:, lanes(mine, units)], down_in.at[lanes(mine, units)])):
+        copy = pltpu.make_async_copy(source, own_units(mine)[i][0], dl.at[i])
+        copy.start()
+        keep.append(copy)
+    for i in (0, 1):
+        for device in line + across:
+            d = device[0] * 2 + device[1]
+            source = up_in.at[:, lanes(d, units)] if i == 0 else down_in.at[lanes(d, units)]
+            copies.append(send(source, own_units(mine)[i][0], ds.at[i, d], dr.at[i, mine], device))
     gather.seconds((0, 1))
     gather.thirds((0, 1))
+
+    fetch.wait()
+
+    def across_block(i, carry):
+        at = lanes(i, depth)
+        vocab_out[at] = vocab_here[:, at].T
+        return carry
+
+    lax.fori_loop(0, vocab_in.shape[1] // depth, across_block, 0)
 
     def head_parts(z, side):
         d = z * 2 + side
@@ -1182,15 +1164,17 @@
         from_head(nz, k, parts, js, jr)
         for i, part in enumerate(parts):
             copies.append(send(part, part, cs.at[i, z], cr.at[i, z], core))
-    local.wait()
-    for device in [(iz, iy, ix, ic)] + line + across:
-        d = device[0] * 2 + device[1]
-        block = down_out.at[:, lanes(d, depth)]
-        if device[0] is not iz or device[1] is not iy:
-            arrived(block, ds.at[d], dr.at[d], device)
-        copies.append(send(block, down_other.at[:, lanes(d, depth)], es.at[d], er.at[d], core))
-    for d in range(2 * nz):
-        arrived(down_other.at[:, lanes(d, depth)], es.at[d], er.at[d], core)
+    for copy in keep:
+        copy.wait()
+    for i in (0, 1):
+        for device in [None] + line + across:
+            d = mine if device is None else device[0] * 2 + device[1]
+            block, other = own_units(d)[i]
+            if device is not None:
+                arrived(block, ds.at[i, d], dr.at[i, d], device)
+            copies.append(send(block, other, es.at[i, d], er.at[i, d], core))
+        for d in range(2 * nz):
+            arrived(own_units(d)[i][1], es.at[i, d], er.at[i, d], core)
     for k in range(nz):
         z = lax.rem(iz + k, nz)
         arrived(info_out.at[z, 1 - iy], ps.at[z], zr.at[z, 1 - iy], across_y)
@@ -1212,7 +1196,7 @@
         copy.wait_send()
 
 
-def front(nz, residual, info, bias, joined_in, dense_in, down_in):
+def front(nz, residual, info, bias, joined_in, dense_in, down_in, up_in, vocab_in):
     held, width = residual.shape
     half = held // 8
     depth, cols = joined_in.shape[0], joined_in.shape[1] // nz
@@ -1227,10 +1211,14 @@
             jax.ShapeDtypeStruct(bias.shape, F32),
             jax.ShapeDtypeStruct((2 * nz * depth, cols), BF16),
             jax.ShapeDtypeStruct((heads + 2 * units, 2 * nz * depth), BF16),
+            jax.ShapeDtypeStruct((2 * nz * depth, 2 * units), BF16),
+            jax.ShapeDtypeStruct(vocab_in.shape[::-1], BF16),
         ],
-        in_specs=[anywhere(), vmem(), vmem(), anywhere(), anywhere(), anywhere()],
-        out_specs=[anywhere(), vmem(), vmem(), anywhere(), anywhere()],
+        in_specs=[anywhere(), vmem(), vmem(), anywhere(), anywhere(), anywhere(), anywhere(), anywhere()],
+        out_specs=[anywhere(), vmem(), vmem(), anywhere(), anywhere(), anywhere(), vmem()],
         scratch_shapes=[
+            pltpu.VMEM(vocab_in.shape, BF16),
+            dma((1,)),
             dma((2, nz, 2, 2)),
             dma((2, nz, 2, 2)),
             dma((2, nz)),
@@ -1243,18 +1231,18 @@
             dma((nz,)),
             dma((nz, 2)),
             dma((nz,)),
-            dma((2 * nz,)),
-            dma((2 * nz,)),
-            dma((1,)),
-            dma((2 * nz,)),
-            dma((2 * nz,)),
+            dma((2, 2 * nz)),
+            dma((2, 2 * nz)),
+            dma((2,)),
+            dma((2, 2 * nz)),
+            dma((2, 2 * nz)),
         ]
         + Gather.scratch(2, nz),
         cost_estimate=busy(45),
-        compiler_params=comm(1, 16),
-    )(residual, info, bias, joined_in, dense_in, down_in)
+        compiler_params=comm(1, 62),
+    )(residual, info, bias, joined_in, dense_in, down_in, up_in, vocab_in)
     natural = outs[0].reshape(8 * nz * 2 * half, width)
-    return natural, outs[1].reshape((2 * nz,) + info.shape), outs[2], outs[3], outs[4]
+    return natural, outs[1].reshape((2 * nz,) + info.shape), outs[2], outs[3], outs[4], outs[5], outs[6]
 
 
 def end_kernel(
@@ -1384,8 +1372,6 @@
         arrived(bias_out.at[z, iy], bs.at[k], br.at[z, iy], across_y)
         copies.append(send(bias_out.at[z, iy], bias_out.at[z, iy], bp.at[z], br.at[z, iy], across_y))
     kept = [reduce.third(h) for h in (0, 1)]
-    for h in (0, 1):
-        reduce.chain(h)
     arrived(vector_in.at[2], vs.at[2], vr.at[2], across_y)
     vector_sum[2] = vector_sum[1] + vector_in[2]
     for k in range(1, nz):
@@ -1546,7 +1532,17 @@
     )(order, mixed, active)
 
 
-def attention_back_kernel(piece, order, douts, slope, qkv, probs_in, tables, dfused, dhidden, sums):
+def attention_back_kernel(
+    piece, order, dbranch, wout, slope, qkv, probs_in, tables, dfused, dhidden, sums, douts
+):
+    tile = 4 * piece
+
+    def back(i, carry):
+        at = pl.ds(pl.multiple_of(i * tile, tile), tile)
+        douts[at] = dot(dbranch[at], wout[...], (1, 1))
+        return carry
+
+    lax.fori_loop(0, dbranch.shape[0] // tile, back, 0)
     groups, held = probs_in.shape[0], probs_in.shape[1]
     per = held // piece
     joined_sum = jnp.zeros((1, 3 * HD), F32)
@@ -1574,7 +1570,7 @@
     sums[:, 3 * HD :] = hidden_sum
 
 
-def attention_back(order, douts, slope, qkv, probs, tables, piece):
+def attention_back(order, dbranch, wout, slope, qkv, probs, tables, piece):
     total, units = slope.shape
     return pl.pallas_call(
         functools.partial(attention_back_kernel, piece),
@@ -1583,10 +1579,12 @@
             jax.ShapeDtypeStruct((total, units), BF16),
             jax.ShapeDtypeStruct((1, 3 * HD + units), F32),
         ],
-        in_specs=[pl.BlockSpec(memory_space=pltpu.SMEM)] + [vmem()] * 5,
+        in_specs=[pl.BlockSpec(memory_space=pltpu.SMEM)] + [vmem()] * 6,
         out_specs=[vmem()] * 3,
-        compiler_params=pltpu.CompilerParams(vmem_limit_bytes=40 << 20),
-    )(order, douts, slope, qkv, probs, tables)
+        scratch_shapes=[pltpu.VMEM((total, wout.shape[0]), F32)],
+        cost_estimate=pl.CostEstimate(flops=0, bytes_accessed=1000, transcendentals=0),
+        compiler_params=pltpu.CompilerParams(vmem_limit_bytes=48 << 20),
+    )(order, dbranch, wout, slope, qkv, probs, tables)
 
 
 def fast_shards(
@@ -1640,15 +1638,13 @@
         ]
     )
     bias_own = jnp.concatenate([b_joined, b_up]).astype(F32)
-    natural, info, bias_other, wj, wout = front(
-        nz, residual, info, bias_own.reshape(-1, HD), w_joined, w_dense, w_down
+    natural, info, bias_other, wj, wout, wup, vocab_across = front(
+        nz, residual, info, bias_own.reshape(-1, HD), w_joined, w_dense, w_down, w_up, w_vocab
     )
     bias_other = bias_other.reshape(-1)
 
-    send_up = w_up.reshape(depth, n, ffs).transpose(1, 0, 2)
-    send_vocab = w_vocab.reshape(depth, n, vcols).transpose(1, 0, 2)
-    send_up, bias_other = lax.optimization_barrier((send_up, bias_other))
-    up_own = exchange(send_up)
+    send_vocab = vocab_across.reshape(n, vcols, depth)
+    vocab_got = exchange(send_vocab)
     bias_first = jnp.where(ic == 0, bias_own, bias_other)
     bias_second = jnp.where(ic == 0, bias_other, bias_own)
     bj_all = jnp.where(iy == 0, bias_first, bias_second)[: nz * hcols].reshape(nz, hcols)
@@ -1702,10 +1698,6 @@
     )
     fused = dot(attn_low, wj, (1, 0)) + bj
     qkv, probs, mixed = attention(order, fused, tables, allowed.astype(F32), piece)
-    up_own, mixed, send_vocab = lax.optimization_barrier((up_own, mixed, send_vocab))
-    up_other = swap(up_own)
-    vocab_got = exchange(send_vocab)
-    wup = jnp.concatenate([w.reshape(width, ffs) for w in (up_own, up_other)], axis=1)
     hidden = dot(mlp_low, wup, (1, 0)) + bu
     bell = 0.5 * (1.0 + lax.erf(hidden * math.sqrt(0.5)))
     active = (hidden * bell).astype(BF16)
@@ -1720,10 +1712,10 @@
     final, resid = reduce_norm_gather(nz, branch_part, rows_here, bias_out, gf[None], sf[None])
 
     vocab_got, final = lax.optimization_barrier((vocab_got, final))
-    vocab_own = vocab_got.reshape(width, vcols)
-    vocab_other = swap(vocab_own)
+    vocab_own = vocab_got.transpose(1, 0, 2).reshape(vcols, width)
+    vocab_other = swap(vocab_got).transpose(1, 0, 2).reshape(vcols, width)
     my_targets = jnp.where(ic == 0, targets[0], targets[1]).reshape(total)
-    logits = [dot(final, w, (1, 0)) for w in (vocab_own, vocab_other)]
+    logits = [dot(final, w, (1, 1)) for w in (vocab_own, vocab_other)]
     hits = [
         lax.broadcasted_iota(jnp.int32, (total, vcols), 1)
         == (my_targets - ((ix * 2 + core) * n + dp) * vcols)[:, None]
@@ -1744,25 +1736,38 @@
         (coef[:, None] * (jnp.where(h, 1.0, 0.0) - jnp.exp(part - my_lse[:, None]))).astype(BF16)
         for h, part in zip(hits, logits)
     ]
-    gv_own = dot(final, dlogits[0], (0, 0))
-    gv_other = dot(final, dlogits[1], (0, 0)).astype(BF16)
-    dfinal_part = (dot(dlogits[0], vocab_own, (1, 1)) + dot(dlogits[1], vocab_other, (1, 1))).astype(BF16)
+    gv_other = dot(dlogits[1], final, (0, 0)).astype(BF16)
+    dfinal_other = dot(dlogits[1], vocab_other, (1, 0)).astype(F32)
+    gv_own = dot(dlogits[0], final, (0, 0))
     gv = (gv_own + swap(gv_other).astype(F32)).astype(BF16)
-    gv, dfinal_part = lax.optimization_barrier((gv, dfinal_part))
-    early_cols = vcols * 272 // 800
-    gv = gv.reshape(n, depth, vcols)
-    grad_early = exchange(gv[:, :, :early_cols])
+    gv, dlogits_own = lax.optimization_barrier((gv, dlogits[0]))
+    dfinal_part = (dot(dlogits_own, vocab_own, (1, 0)) + dfinal_other).astype(BF16)
+    gv = gv.reshape(vcols, n, depth).transpose(1, 0, 2)
+    early_cols = vcols * 368 // 800
+    grad_early = exchange(gv[:, :early_cols])
     dbranch, final_vectors = reduce_back_gather(nz, dfinal_part, resid, gf[None])
-    gv_late, dbranch, grad_early = lax.optimization_barrier((gv[:, :, early_cols:], dbranch, grad_early))
+    gv_late, dbranch, grad_early = lax.optimization_barrier((gv[:, early_cols:], dbranch, grad_early))
     grad_late = exchange(gv_late)
-    grad_vocab = jnp.concatenate([grad_early, grad_late], axis=2).transpose(1, 0, 2).reshape(depth, n * vcols)
-    grad_vocab = lax.optimization_barrier(grad_vocab).astype(F32)
-
+    grad_vocab = jnp.concatenate([grad_early, grad_late], axis=1).reshape(n * vcols, depth).T
+    grad_vocab = with_layout_constraint(lax.optimization_barrier(grad_vocab).astype(F32), Layout((0, 1)))
+
+    dfused, dhidden, bias_sums = attention_back(
+        order, dbranch, wout, gelu_slope, qkv, probs, tables, piece
+    )
+    dhidden, outs_low = lax.optimization_barrier((dhidden, outs_low))
     gout = dot(outs_low, dbranch, (0, 0))
-    douts = dot(dbranch, wout, (1, 1))
-    dfused, dhidden, bias_sums = attention_back(order, douts, gelu_slope, qkv, probs, tables, piece)
+    gu = dot(mlp_low, dhidden, (0, 0))
+
+    def to_send(up, down):
+        return jnp.concatenate(
+            [up.reshape(n, depth, ffs), down.reshape(ffs, n, depth).transpose(1, 0, 2)], axis=1
+        )
+
+    give_grads = to_send(gu[:, ffs:].astype(BF16), gout[HD + ffs :].astype(BF16))
+    layer_grads = to_send(gu[:, :ffs], gout[HD : HD + ffs]) + swap(give_grads).astype(F32)
+    layer_grads, dfused, dhidden = lax.optimization_barrier((layer_grads.astype(BF16), dfused, dhidden))
+    layer_grads = exchange(layer_grads)
     gj = dot(attn_low, dfused, (0, 0)).astype(BF16)
-    gu = dot(mlp_low, dhidden, (0, 0))
     dattn = dot(dfused, wj, (1, 1))
     dmlp = dot(dhidden, wup, (1, 1))
     g_attn_gain = jnp.sum(dattn * hat, axis=0)
@@ -1770,15 +1775,6 @@
     g_mlp_gain = jnp.sum(dmlp * hat, axis=0)
     g_mlp_shift = jnp.sum(dmlp, axis=0)
     t_part = (dattn * ga + dmlp * gm).astype(BF16)
-
-    def to_send(up, down):
-        return jnp.concatenate(
-            [up.reshape(n, depth, ffs), down.reshape(ffs, n, depth).transpose(1, 0, 2)], axis=1
-        )
-
-    give_grads = to_send(gu[:, ffs:].astype(BF16), gout[HD + ffs :].astype(BF16))
-    layer_grads = to_send(gu[:, :ffs], gout[HD : HD + ffs]) + swap(give_grads).astype(F32)
-    layer_grads = exchange(layer_grads.astype(BF16))
     grad_up = layer_grads[:, :depth].transpose(1, 0, 2).reshape(depth, n * ffs).astype(F32)
     grad_down = layer_grads[:, depth:].reshape(n * ffs, depth).astype(F32)
 
@@ -1800,6 +1796,7 @@
             jnp.zeros((1, width), F32),
         ]
     )
+    grad_vocab, t_part = lax.optimization_barrier((grad_vocab, t_part))
     rows_out, vectors, biases, grad_joined, grad_dense = end(
         nz,
         t_part.reshape(nz, 2, 2, 2, share2, width),

time: 609 us -> 552 us (0.906)
  matrix products: 88.5 us -> 65.4 us
  local copies, waits for them, and re-layouts: 62.5 us -> 40.6 us
  starting transfers between devices: 49.4 us -> 33.2 us
  other arithmetic: 32.1 us -> 39.9 us
    pallas_call x1, Pallas kernels: 64.8 us -> 91.8 us  [front(): pl.pallas_call(functools.partial(front_kernel, nz, half), out_shape=[jax....]
    unnamed x88 -> x99, local copies, waits for them, and re-layouts: 37.8 us -> 14.5 us
    dot_general x15 -> x14, matrix products: 88.5 us -> 65.4 us  [dot(): lax.dot_general(a, b, ((contract[:1], contract[1:]), ((), ())), preferred...]
    pallas_call x1, Pallas kernels: 79.7 us -> 62.9 us  [end(): pl.pallas_call(functools.partial(end_kernel, nz, half), out_shape=[jax.Sh...]
    pallas_call x1, Pallas kernels: 110 us -> 94.8 us  [reduce_norm_gather(): pl.pallas_call(functools.partial(forward_kernel, nz, half), out_shape=[ja...]
    ppermute x4 -> x3, starting transfers between devices: 24.4 us -> 9.92 us  [swap(): return lax.ppermute(value, 'c', SWAP)]
    pallas_call x1, Pallas kernels: 88.6 us -> 79.8 us  [reduce_back_gather(): pl.pallas_call(functools.partial(backward_kernel, nz, half), out_shape=[j...]
    pallas_call x1, Pallas kernels: 3.5 us -> 10.7 us  [attention_back(): pl.pallas_call(functools.partial(attention_back_kernel, piece), out_shape...]
  transfers between devices with their start and end apart: 9 -> 7, of which waited for: 0 -> 1; matrix products, arithmetic and copies ran while one was open for 20% -> 19% of each run, Pallas kernels for 48% -> 46%
where the time goes in v3:
time: 552 us; the launch traced here: 544 us
  Pallas kernels  356 us (64%)
  matrix products  65.4 us (12%)
  local copies, waits for them, and re-layouts  40.6 us (7%)
  other arithmetic  39.9 us (7%)
  starting transfers between devices  33.2 us (6%)
    pallas_call x1, Pallas kernels, reduce_norm_gather(): pl.pallas_call(functools.partial(forward_kernel, nz, half), out_shape=[ja...  94.8 us
    pallas_call x1, Pallas kernels, front(): pl.pallas_call(functools.partial(front_kernel, nz, half), out_shape=[jax....  91.8 us
    pallas_call x1, Pallas kernels, reduce_back_gather(): pl.pallas_call(functools.partial(backward_kernel, nz, half), out_shape=[j...  79.8 us
    dot_general x14, matrix products, dot(): lax.dot_general(a, b, ((contract[:1], contract[1:]), ((), ())), preferred...  65.4 us
    pallas_call x1, Pallas kernels, end(): pl.pallas_call(functools.partial(end_kernel, nz, half), out_shape=[jax.Sh...  62.9 us
    all_to_all x4, starting transfers between devices, exchange(): return lax.all_to_all(value, DP, split_axis=0, concat_axis=0, tiled=True)  23.3 us
    unnamed x99, local copies, waits for them, and re-layouts  14.5 us
    pallas_call x1, Pallas kernels, objective(): pl.pallas_call(functools.partial(objective_kernel, nz, hot.shape[0], seq_...  12.2 us
  transfers between devices with their start and end apart: 7, of which 1 were waited for; matrix products, arithmetic and copies ran while one was open for 19% of the time, Pallas kernels for 46%

profile of v3, /device:TPU:1, one launch (start us, length us, event | category | flops | bytes accessed | tf_op | source)
XLA Modules:
  0.0 544.5 jit_solution(9969320325740893965)
XLA Ops:
  2.6 1.3 maximum_convert_fusion
  4.0 1.3 pad_maximum_fusion.9.info
  5.3 91.8 %shard_map.349 = (bf16[4,2,2,2,32,2048]{5,4,3,2,1,0:T(8,128)(2,1)}, f32[4,2,4,128]{3,2,1,0:T(4,128)}, f32[28,128]{1,0:T(8,128)}, bf16[2048,384]{1,0:T(8,128)(2,1...) custom-call(bf16[128,2048]{1,0:T(8,128)(2,1)} %residual.1, ...), custom_call_target="tpu_custom_call" | custom-call | bytes 135000000 | tf_op jit(solution)/shard_map/pallas_call | solution.py:1206
  97.1 5.4 %all-to-all-start = ((bf16[8,800,256]{2,1,0:T(8,128)(2,1)}), bf16[8,800,256]{2,1,0:T(8,128)(2,1)}, u32[]{:S(2)}, u32[]{:S(2)}) async-start(bf16[8,800,256]{2,1,0:T(8,128)(2,1)} %bitcast.172), calls=%async_computation | async-start | bytes 6553600 | tf_op jit(solution)/shard_map/all_to_all | solution.py:454
  102.8 3.0 convert_reduce_fusion
  106.2 1.3 fusion.1
  108.5 0.7 fusion.23
  111.3 2.0 fusion.10
  113.7 3.5 add_convert_fusion.2
  117.2 2.3 convolution_add_fusion.fused
  119.6 3.6 shard_map.350
  123.2 4.3 fusion.6
  128.2 0.7 convert_add_fusion
  128.9 1.7 constant_dynamic-slice_fusion.3.rows
  130.6 7.0 %convolution_convert_fusion = bf16[1024,2048]{1,0:T(8,128)(2,1)} fusion(bf16[1024,640]{1,0:T(8,128)(2,1)S(1)} %shard_map.351, bf16[640,2048]{1,0:T(8,128)(2,1)} %get-tuple-element.64.wout), kind=kOutput, calls=%fused_computation.14 | convolution fusion | flops 2686451712 | bytes 8126464 | tf_op jit(solution)/shard_map/dot_general | solution.py:434
  137.7 94.8 %shard_map.352 = (bf16[4,2,2,64,2048]{4,3,2,1,0:T(8,128)(2,1)}, f32[64,2048]{1,0:T(8,128)}) custom-call(bf16[4,2,2,64,2048]{4,3,2,1,0:T(8,128)(2,1)} %bitcast.168, bf16[64,2048]{1,0:T(8,128)(2,1)} %constant_dynamic-slice_fusion.3.rows, f32[1,2048]{1,0:T(1,128)} %bitcast.186, f32[1,2048]{1,0:T(1,128)} %bitcast.182, f32[1,2048]{1,0:T(1,128)} %bitcast.185), custom_call_target="tpu_custom_call" | custom-call | bytes 270000000 | tf_op jit(solution)/shard_map/pallas_call | solution.py:835
  232.5 3.8 collective-permute-start
  236.9 2.5 copy.132
  240.1 3.6 fusion.36
  243.7 2.4 copy.133
  246.1 3.6 fusion.37
  249.7 1.7 exponential_reduce_fusion
  251.5 12.2 %shard_map.353 = (f32[8,128]{1,0:T(8,128)S(1)}, f32[8,128]{1,0:T(8,128)S(1)}, f32[2,8,128]{2,1,0:T(8,128)S(1)}) custom-call(f32[3,8,128]{2,1,0:T(8,128)S(1)} %pad_maximum_fusion.3.stats, f32[3,8,128]{2,1,0:T(8,128)S(1)} %fusion.11.hot, f32[8,128]{1,0:T(8,128)S(1)} %pad_convert_fusion.scored, f32[2,8,128]{2,1,0:T(8,128)S(1)} %pad_maximum_fusion.4.refs, ...), custom_call_target="tpu_custom_call" | custom-call | bytes 45000000 | tf_op jit(solution)/shard_map/pallas_call | solution.py:940
  263.7 6.3 %convolution_convert_fusion.1 = bf16[800,2048]{1,0:T(8,128)(2,1)S(1)} fusion(bf16[1024,2048]{1,0:T(8,128)(2,1)} %bitcast.214, f32[1024,800]{0,1:T(8,128)S(1)} %get-tuple-element.188, f32[1024]{0:T(1024)S(1)} %bitcast.151, f32[1024]{0:T(1024)S(1)} %bitcast.148, s32[1024]{0:T(1024)S(1)} %get-tuple-element.173), kind=kOutput, calls=%fused_computation.15 | convolution fusion | flops 3361996800 | bytes 10760192 | tf_op jit(solution)/shard_map/dot_general | solution.py:434
  270.4 0.9 multiply_convert_fusion.1
  271.3 4.6 collective-permute-done.1
  275.9 3.8 add_convert_fusion.4
  280.0 1.7 copy-done.14
  281.7 1.2 slice.160
  282.9 4.3 all-to-all-start.1
  287.3 7.8 %fusion.28 = f32[1024,2048]{1,0:T(8,128)S(1)} fusion(bf16[800,2048]{1,0:T(8,128)(2,1)} %bitcast.176, f32[1024,800]{0,1:T(8,128)} %copy-done.25, f32[1024]{0:T(1024)S(1)} %bitcast.153, f32[1024]{0:T(1024)S(1)} %bitcast.150, s32[1024]{0:T(1024)S(1)} %get-tuple-element.173), kind=kOutput, calls=%fused_computation.129 | convolution fusion | flops 3360358400 | bytes 14954496 | tf_op jit(solution)/shard_map/dot_general | solution.py:434
  295.1 1.3 slice.159
  296.4 1.2 copy-done.23
  297.7 6.4 %add_convert_fusion.1 = bf16[1024,2048]{1,0:T(8,128)(2,1)} fusion(f32[1024,2048]{1,0:T(8,128)S(1)} %fusion.28, bf16[1024,800]{0,1:T(8,128)(2,1)S(1)} %copy-done.27, bf16[800,2048]{1,0:T(8,128)(2,1)S(1)} %bitcast.174), kind=kOutput, calls=%fused_computation.7 | convolution fusion | flops 3359637504 | bytes 17498112 | tf_op jit(solution)/shard_map/dot_general | solution.py:434
  304.1 79.8 %shard_map.354 = (bf16[4,2,2,64,2048]{4,3,2,1,0:T(8,128)(2,1)}, f32[3,2048]{1,0:T(4,128)}) custom-call(bf16[4,2,2,64,2048]{4,3,2,1,0:T(8,128)(2,1)} %bitcast.167, f32[64,2048]{1,0:T(8,128)} %get-tuple-element.73.resid, f32[1,2048]{1,0:T(1,128)} %bitcast.183), custom_call_target="tpu_custom_call" | custom-call | bytes 270000000 | tf_op jit(solution)/shard_map/pallas_call | solution.py:855
  383.9 7.4 %all-to-all-start.2 = ((bf16[8,432,256]{2,1,0:T(8,128)(2,1)}), bf16[8,432,256]{2,1,0:T(8,128)(2,1)}, u32[]{:S(2)}, u32[]{:S(2)}) async-start(bf16[8,432,256]{2,1,0:T(8,128)(2,1)} %slice.159), calls=%async_computation.2 | async-start | bytes 3538944 | tf_op jit(solution)/shard_map/all_to_all | solution.py:454
  391.3 1.1 copy-done.5
  392.5 10.7 %shard_map.355 = (bf16[1024,384]{1,0:T(8,128)(2,1)S(1)}, bf16[1024,512]{1,0:T(8,128)(2,1)S(1)}, f32[1,896]{1,0:T(1,128)S(1)}) custom-call(s32[16]{0:T(128)S(1)} %get-tuple-element.145.order, bf16[1024,2048]{1,0:T(8,128)(2,1)} %bitcast.155, bf16[640,2048]{1,0:T(8,128)(2,1)} %get-tuple-element.64.wout, f32[1024,512]{1,0:T(8,128)} %get-tuple-element.153.slope, ...), custom_call_target="tpu_custom_call" | custom-call | bytes 1000 | tf_op jit(solution)/shard_map/pallas_call | solution.py:1575
  403.2 4.6 fusion.38
  408.0 3.0 copy-done.21
  411.0 2.5 fusion.39
  413.5 2.0 copy-done.16
  415.6 1.5 pad_maximum_fusion.1
  417.0 5.7 %collective-permute-start.2 = (bf16[8,512,256]{2,1,0:T(8,128)(2,1)}, bf16[8,512,256]{2,1,0:T(8,128)(2,1)}, u32[]{:S(2)}, u32[]{:S(2)}) collective-permute-start(bf16[8,512,256]{2,1,0:T(8,128)(2,1)} %pad_maximum_fusion.1), channel_id=1, source_target_pairs={{0,1},{1,0},{2,3},{3,2},{4,5},{5,4},{6,7},{7,6},{8,9},{9,8},{10,11... | collective-permute-start | bytes 6291464 | tf_op jit(solution)/shard_map/ppermute | solution.py:438
  424.1 0.9 constant_dynamic-slice_fusion.rows
  425.5 1.1 slice.165.dense_in
  426.6 1.7 slice.162
  428.6 1.2 constant_dynamic-slice_fusion.1
  430.1 3.6 fusion.2
  433.7 6.2 %all-to-all-start.3 = ((bf16[8,512,256]{2,1,0:T(8,128)(2,1)}), bf16[8,512,256]{2,1,0:T(8,128)(2,1)}, u32[]{:S(2)}, u32[]{:S(2)}) async-start(bf16[8,512,256]{2,1,0:T(8,128)(2,1)} %fusion.2), calls=%async_computation.3 | async-start | bytes 4194304 | tf_op jit(solution)/shard_map/all_to_all | solution.py:454
  439.9 2.4 fusion.40
  442.4 0.7 copy-done.46
  443.1 6.1 %fusion.29 = (f32[2048]{0:T(1024)S(1)}, f32[2048]{0:T(1024)S(1)}, bf16[1024,2048]{1,0:T(8,128)(2,1)}, f32[2048]{0:T(1024)S(1)}, f32[2048]{0:T(1024)S(1)}) fusion(f32[1024]{0:T(1024)S(1)} %rsqrt.12, f32[1024]{0:T(1024)S(1)} %div.31, bf16[4,2,2,2,32,2048]{5,4,3,2,1,0:T(8,128)(2,1)S(1)} %copy-done.12, f32[2048]{0:T(1024)S(1)} %convert_element_type.219, ...), kind=kOutput, calls=%fused_computation.130 | convolution fusion | flops 2174738432 | bytes 19980288 | tf_op jit(solution)/shard_map/dot_general | solution.py:434
  449.3 4.6 convolution_convert_fusion.2.joined_in
  453.9 3.8 pad_maximum_fusion
  457.8 5.7 %copy.122 = bf16[6400,256]{0,1:T(8,128)(2,1)} copy(bf16[6400,256]{1,0:T(8,128)(2,1)} %bitcast.160) | data formatting | bytes 6553600 | tf_op jit(solution)/shard_map/reshape | solution.py:1751
  463.4 5.1 convert_element_type.238
  468.6 62.9 %shard_map.356 = (bf16[2,2,32,2048]{3,2,1,0:T(8,128)(2,1)S(1)}, f32[8,2048]{1,0:T(8,128)S(1)}, f32[4,2,8,128]{3,2,1,0:T(8,128)S(1)}, bf16[256,1536]{1,0:T(8,128)(2,1)S(1)}, bf16[512,256]{1,0:T(8,128)(2,1)S(1)}) custom-call(bf16[4,2,2,2,32,2048]{5,4,3,2,1,0:T(8,128)(2,1)} %bitcast.166, bf16[32,2048]{1,0:T(8,128)(2,1)S(1)} %get-tuple-element.152.mine_rows, ...), custom_call_target="tpu_custom_call" | custom-call | bytes 210000000 | tf_op jit(solution)/shard_map/pallas_call | solution.py:1424
  531.5 1.3 convert_element_type.245
  533.4 0.8 convert_element_type.246
  535.5 1.1 bitcast_convert_fusion.1
  536.6 2.7 fusion.31
  540.1 1.8 copy.126
  541.9 1.5 bitcast_convert_fusion
  (181 shorter events, 12.6 us)
Async XLA Ops:
  97.1 5.5 %copy-start.33 = (f32[4,2,4,128]{3,2,1,0:T(4,128)S(1)}, f32[4,2,4,128]{3,2,1,0:T(4,128)}, u32[]{:S(2)}) copy-start(f32[4,2,4,128]{3,2,1,0:T(4,128)} %get-tuple-element.61) | copy-start | bytes 49156
  97.1 135.4 %all-to-all-start = ((bf16[8,800,256]{2,1,0:T(8,128)(2,1)}), bf16[8,800,256]{2,1,0:T(8,128)(2,1)}, u32[]{:S(2)}, u32[]{:S(2)}) async-start(bf16[8,800,256]{2,1,0:T(8,128)(2,1)} %bitcast.172), calls=%async_computation | async-start | bytes 6553600 | tf_op jit(solution)/shard_map/all_to_all | solution.py:454
  102.8 3.5 copy-start.10
  102.8 4.8 copy-start.32
  105.8 2.0 copy-start.34
  105.8 2.0 copy-start.35
  105.8 2.1 copy-start.36
  105.8 2.1 copy-start.37
  105.8 2.6 copy-start.42
  105.8 4.0 copy-start.38
  105.8 4.6 copy-start.39
  111.1 2.5 copy-start.11
  113.6 3.5 copy-start.28
  117.2 2.4 copy-start.19
  117.2 6.0 %copy-start.20 = (bf16[1024,2048]{1,0:T(8,128)(2,1)}, bf16[1024,2048]{1,0:T(8,128)(2,1)S(1)}, u32[]{:S(2)}) copy-start(bf16[1024,2048]{1,0:T(8,128)(2,1)S(1)} %get-tuple-element.149) | copy-start | bytes 12582916
  119.6 3.6 copy-start.45
  123.1 4.4 copy-start.4
  123.1 4.4 copy-start.6
  123.2 5.0 copy-start.40
  123.2 5.0 copy-start.41
  128.2 9.5 %copy-start = (bf16[1024,640]{1,0:T(8,128)(2,1)}, bf16[1024,640]{1,0:T(8,128)(2,1)S(1)}, u32[]{:S(2)}) copy-start(bf16[1024,640]{1,0:T(8,128)(2,1)S(1)} %shard_map.351) | copy-start | bytes 3932164
  232.5 11.2 %collective-permute-start = (bf16[8,800,256]{2,1,0:T(8,128)(2,1)}, bf16[8,800,256]{2,1,0:T(8,128)(2,1)}, u32[]{:S(2)}, u32[]{:S(2)}) collective-permute-start(bf16[8,800,256]{2,1,0:T(8,128)(2,1)} %all-to-all-done), channel_id=1, source_target_pairs={{0,1},{1,0},{2,3},{3,2},{4,5},{5,4},{6,7},{7,6},{8,9},{9,8},{10,11... | collective-permute-start | bytes 9830408 | tf_op jit(solution)/shard_map/ppermute | solution.py:438
  236.9 3.2 copy-start.43
  239.5 4.2 copy-start.22
  246.1 3.6 copy-start.24
  249.7 14.0 %copy-start.25 = (f32[1024,800]{0,1:T(8,128)}, f32[1024,800]{0,1:T(8,128)S(1)}, u32[]{:S(2)}) copy-start(f32[1024,800]{0,1:T(8,128)S(1)} %get-tuple-element.188) | copy-start | bytes 9830404
  270.0 5.9 %copy-start.44 = (bf16[4,2,2,64,2048]{4,3,2,1,0:T(8,128)(2,1)S(1)}, bf16[4,2,2,64,2048]{4,3,2,1,0:T(8,128)(2,1)}, u32[]{:S(2)}) copy-start(bf16[4,2,2,64,2048]{4,3,2,1,0:T(8,128)(2,1)} %get-tuple-element.65) | copy-start | bytes 12582916
  270.0 5.9 %collective-permute-start.1 = (bf16[800,2048]{1,0:T(8,128)(2,1)S(1)}, bf16[800,2048]{1,0:T(8,128)(2,1)S(1)}, u32[]{:S(2)}, u32[]{:S(2)}) collective-permute-start(bf16[800,2048]{1,0:T(8,128)(2,1)S(1)} %convolution_convert_fusion.1), channel_id=1, source_target_pairs={{0,1},{1,0},{2,3},{3,2},{4,5},{5,4},{6,7},{7,6},{8,9},{9,8},{10,11... | collective-permute-start | bytes 9830408 | tf_op jit(solution)/shard_map/ppermute | solution.py:438
  271.3 8.5 %copy-start.26 = (bf16[1024,800]{0,1:T(8,128)(2,1)}, bf16[1024,800]{0,1:T(8,128)(2,1)S(1)}, u32[]{:S(2)}) copy-start(bf16[1024,800]{0,1:T(8,128)(2,1)S(1)} %multiply_convert_fusion.1) | copy-start | bytes 4915204
  280.0 1.7 copy-start.14
  282.9 101.0 %all-to-all-start.1 = ((bf16[8,368,256]{2,1,0:T(8,128)(2,1)}), bf16[8,368,256]{2,1,0:T(8,128)(2,1)}, u32[]{:S(2)}, u32[]{:S(2)}) async-start(bf16[8,368,256]{2,1,0:T(8,128)(2,1)} %slice.160), calls=%async_computation.1 | async-start | bytes 3014656 | tf_op jit(solution)/shard_map/all_to_all | solution.py:454
  287.2 7.8 %copy-start.15 = (bf16[100,8,8,256]{3,2,0,1:T(8,128)(2,1)S(1)}, bf16[100,8,8,256]{3,2,0,1:T(8,128)(2,1)}, u32[]{:S(2)}) copy-start(bf16[100,8,8,256]{3,2,0,1:T(8,128)(2,1)} %copy-done.14) | copy-start | bytes 9830404
  287.2 9.2 %copy-start.27 = (bf16[1024,800]{0,1:T(8,128)(2,1)S(1)}, bf16[1024,800]{0,1:T(8,128)(2,1)}, u32[]{:S(2)}) copy-start(bf16[1024,800]{0,1:T(8,128)(2,1)} %copy-done.26) | copy-start | bytes 4915204
  295.1 2.6 copy-start.23
  383.9 7.4 %copy-start.7 = (f32[8,128,128]{2,1,0:T(8,128)S(1)}, f32[8,128,128]{2,1,0:T(8,128)}, u32[]{:S(2)}) copy-start(f32[8,128,128]{2,1,0:T(8,128)} %copy-done.6) | copy-start | bytes 1572868
  383.9 49.8 %all-to-all-start.2 = ((bf16[8,432,256]{2,1,0:T(8,128)(2,1)}), bf16[8,432,256]{2,1,0:T(8,128)(2,1)}, u32[]{:S(2)}, u32[]{:S(2)}) async-start(bf16[8,432,256]{2,1,0:T(8,128)(2,1)} %slice.159), calls=%async_computation.2 | async-start | bytes 3538944 | tf_op jit(solution)/shard_map/all_to_all | solution.py:454
  391.3 1.1 copy-start.5
  392.5 10.7 %copy-start.1 = (bf16[1024,640]{1,0:T(8,128)(2,1)S(1)}, bf16[1024,640]{1,0:T(8,128)(2,1)}, u32[]{:S(2)}) copy-start(bf16[1024,640]{1,0:T(8,128)(2,1)} %copy-done) | copy-start | bytes 3932164
  392.5 10.7 %copy-start.13 = (bf16[4,2,2,64,2048]{4,3,2,1,0:T(8,128)(2,1)S(1)}, bf16[4,2,2,64,2048]{4,3,2,1,0:T(8,128)(2,1)}, u32[]{:S(2)}) copy-start(bf16[4,2,2,64,2048]{4,3,2,1,0:T(8,128)(2,1)} %get-tuple-element.74) | copy-start | bytes 12582916
  403.2 4.8 copy-start.8
  403.2 36.7 %copy-start.2 = (bf16[1024,384]{1,0:T(8,128)(2,1)}, bf16[1024,384]{1,0:T(8,128)(2,1)S(1)}, u32[]{:S(2)}) copy-start(bf16[1024,384]{1,0:T(8,128)(2,1)S(1)} %get-tuple-element.84) | copy-start | bytes 2359300
  407.8 5.6 %copy-start.17 = (bf16[640,2048]{1,0:T(8,128)(2,1)}, bf16[640,2048]{1,0:T(8,128)(2,1)S(1)}, u32[]{:S(2)}) copy-start(bf16[640,2048]{1,0:T(8,128)(2,1)S(1)} %get-tuple-element.189) | copy-start | bytes 7864324
  407.8 3.1 copy-start.21
  413.5 2.0 copy-start.16
  417.0 12.8 %collective-permute-start.2 = (bf16[8,512,256]{2,1,0:T(8,128)(2,1)}, bf16[8,512,256]{2,1,0:T(8,128)(2,1)}, u32[]{:S(2)}, u32[]{:S(2)}) collective-permute-start(bf16[8,512,256]{2,1,0:T(8,128)(2,1)} %pad_maximum_fusion.1), channel_id=1, source_target_pairs={{0,1},{1,0},{2,3},{3,2},{4,5},{5,4},{6,7},{7,6},{8,9},{9,8},{10,11... | collective-permute-start | bytes 6291464 | tf_op jit(solution)/shard_map/ppermute | solution.py:438
  428.4 1.7 slice-start
  433.7 6.2 %copy-start.29 = (bf16[2048,384]{1,0:T(8,128)(2,1)S(1)}, bf16[2048,384]{1,0:T(8,128)(2,1)}, u32[]{:S(2)}) copy-start(bf16[2048,384]{1,0:T(8,128)(2,1)} %get-tuple-element.59) | copy-start | bytes 4718596
  433.7 102.9 %all-to-all-start.3 = ((bf16[8,512,256]{2,1,0:T(8,128)(2,1)}), bf16[8,512,256]{2,1,0:T(8,128)(2,1)}, u32[]{:S(2)}, u32[]{:S(2)}) async-start(bf16[8,512,256]{2,1,0:T(8,128)(2,1)} %fusion.2), calls=%async_computation.3 | async-start | bytes 4194304 | tf_op jit(solution)/shard_map/all_to_all | solution.py:454
  439.9 2.4 copy-start.9
  439.9 2.5 copy-start.12
  439.9 3.2 copy-start.46
  443.1 6.1 %copy-start.31 = (f32[3,2048]{1,0:T(4,128)S(1)}, f32[3,2048]{1,0:T(4,128)}, u32[]{:S(2)}) copy-start(f32[3,2048]{1,0:T(4,128)} %get-tuple-element.87) | copy-start | bytes 73732
  443.1 6.2 %copy-start.3 = (bf16[1024,384]{1,0:T(8,128)(2,1)S(1)}, bf16[1024,384]{1,0:T(8,128)(2,1)}, u32[]{:S(2)}) copy-start(bf16[1024,384]{1,0:T(8,128)(2,1)} %copy-done.2) | copy-start | bytes 2359300
  535.5 7.9 %copy-start.30 = (f32[1,2048]{1,0:T(1,128)}, f32[1,2048]{1,0:T(1,128)S(1)}, u32[]{:S(2)}) copy-start(f32[1,2048]{1,0:T(1,128)S(1)} %get-tuple-element.159) | copy-start | bytes 24580
  540.0 1.8 copy-start.18

commit v4 on v3

--- a/solution.py
+++ b/solution.py
@@ -825,7 +825,7 @@
     return pl.CostEstimate(flops=0, bytes_accessed=us * 3_000_000, transcendentals=0)
 
 
-def comm(which, limit=48):
+def comm(which, limit=28):
     return pltpu.CompilerParams(collective_id=which, has_side_effects=True, vmem_limit_bytes=limit << 20)
 
 
@@ -1743,7 +1743,7 @@
     gv, dlogits_own = lax.optimization_barrier((gv, dlogits[0]))
     dfinal_part = (dot(dlogits_own, vocab_own, (1, 0)) + dfinal_other).astype(BF16)
     gv = gv.reshape(vcols, n, depth).transpose(1, 0, 2)
-    early_cols = vcols * 368 // 800
+    early_cols = vcols * 336 // 800
     grad_early = exchange(gv[:, :early_cols])
     dbranch, final_vectors = reduce_back_gather(nz, dfinal_part, resid, gf[None])
     gv_late, dbranch, grad_early = lax.optimization_barrier((gv[:, early_cols:], dbranch, grad_early))

time: 552 us -> 549 us (level)
  no operation moved by 1% of the time
where the time goes in v4:
time: 549 us; the launch traced here: 541 us
  Pallas kernels  355 us (65%)
  matrix products  63.3 us (12%)
  local copies, waits for them, and re-layouts  40.7 us (7%)
  other arithmetic  40.1 us (7%)
  starting transfers between devices  33.5 us (6%)
    pallas_call x1, Pallas kernels, reduce_norm_gather(): pl.pallas_call(functools.partial(forward_kernel, nz, half), out_shape=[ja...  94.8 us
    pallas_call x1, Pallas kernels, front(): pl.pallas_call(functools.partial(front_kernel, nz, half), out_shape=[jax....  91.8 us
    pallas_call x1, Pallas kernels, reduce_back_gather(): pl.pallas_call(functools.partial(backward_kernel, nz, half), out_shape=[j...  77.2 us
    pallas_call x1, Pallas kernels, end(): pl.pallas_call(functools.partial(end_kernel, nz, half), out_shape=[jax.Sh...  64.1 us
    dot_general x14, matrix products, dot(): lax.dot_general(a, b, ((contract[:1], contract[1:]), ((), ())), preferred...  63.3 us
    all_to_all x4, starting transfers between devices, exchange(): return lax.all_to_all(value, DP, split_axis=0, concat_axis=0, tiled=True)  24.7 us
    unnamed x99, local copies, waits for them, and re-layouts  14.5 us
    pallas_call x1, Pallas kernels, objective(): pl.pallas_call(functools.partial(objective_kernel, nz, hot.shape[0], seq_...  12.2 us
  transfers between devices with their start and end apart: 7, of which 1 were waited for; matrix products, arithmetic and copies ran while one was open for 19% of the time, Pallas kernels for 46%

profile of v4, /device:TPU:1, one launch (start us, length us, event | category | flops | bytes accessed | tf_op | source)
XLA Modules:
  0.0 541.4 jit_solution(11048320141537753427)
XLA Ops:
  2.6 1.3 maximum_convert_fusion
  4.0 1.3 pad_maximum_fusion.9.info
  5.3 91.8 %shard_map.349 = (bf16[4,2,2,2,32,2048]{5,4,3,2,1,0:T(8,128)(2,1)}, f32[4,2,4,128]{3,2,1,0:T(4,128)}, f32[28,128]{1,0:T(8,128)}, bf16[2048,384]{1,0:T(8,128)(2,1...) custom-call(bf16[128,2048]{1,0:T(8,128)(2,1)} %residual.1, ...), custom_call_target="tpu_custom_call" | custom-call | bytes 135000000 | tf_op jit(solution)/shard_map/pallas_call | solution.py:1206
  97.1 5.4 %all-to-all-start = ((bf16[8,800,256]{2,1,0:T(8,128)(2,1)}), bf16[8,800,256]{2,1,0:T(8,128)(2,1)}, u32[]{:S(2)}, u32[]{:S(2)}) async-start(bf16[8,800,256]{2,1,0:T(8,128)(2,1)} %bitcast.172), calls=%async_computation | async-start | bytes 6553600 | tf_op jit(solution)/shard_map/all_to_all | solution.py:454
  102.8 3.0 convert_reduce_fusion
  106.2 1.3 fusion.1
  108.5 0.7 fusion.23
  111.3 2.0 fusion.10
  113.7 3.5 add_convert_fusion.2
  117.2 2.3 convolution_add_fusion.fused
  119.6 3.6 shard_map.350
  123.2 4.3 fusion.6
  128.2 0.7 convert_add_fusion
  128.9 1.7 constant_dynamic-slice_fusion.3.rows
  130.6 7.0 %convolution_convert_fusion = bf16[1024,2048]{1,0:T(8,128)(2,1)} fusion(bf16[1024,640]{1,0:T(8,128)(2,1)S(1)} %shard_map.351, bf16[640,2048]{1,0:T(8,128)(2,1)} %get-tuple-element.64.wout), kind=kOutput, calls=%fused_computation.14 | convolution fusion | flops 2686451712 | bytes 8126464 | tf_op jit(solution)/shard_map/dot_general | solution.py:434
  137.7 94.8 %shard_map.352 = (bf16[4,2,2,64,2048]{4,3,2,1,0:T(8,128)(2,1)}, f32[64,2048]{1,0:T(8,128)}) custom-call(bf16[4,2,2,64,2048]{4,3,2,1,0:T(8,128)(2,1)} %bitcast.168, bf16[64,2048]{1,0:T(8,128)(2,1)} %constant_dynamic-slice_fusion.3.rows, f32[1,2048]{1,0:T(1,128)} %bitcast.186, f32[1,2048]{1,0:T(1,128)} %bitcast.182, f32[1,2048]{1,0:T(1,128)} %bitcast.185), custom_call_target="tpu_custom_call" | custom-call | bytes 270000000 | tf_op jit(solution)/shard_map/pallas_call | solution.py:835
  232.5 3.8 collective-permute-start
  236.9 2.5 copy.132
  240.1 3.6 fusion.36
  243.7 2.4 copy.133
  246.1 3.6 fusion.37
  249.7 1.7 exponential_reduce_fusion
  251.5 12.2 %shard_map.353 = (f32[8,128]{1,0:T(8,128)S(1)}, f32[8,128]{1,0:T(8,128)S(1)}, f32[2,8,128]{2,1,0:T(8,128)S(1)}) custom-call(f32[3,8,128]{2,1,0:T(8,128)S(1)} %pad_maximum_fusion.3.stats, f32[3,8,128]{2,1,0:T(8,128)S(1)} %fusion.11.hot, f32[8,128]{1,0:T(8,128)S(1)} %pad_convert_fusion.scored, f32[2,8,128]{2,1,0:T(8,128)S(1)} %pad_maximum_fusion.4.refs, ...), custom_call_target="tpu_custom_call" | custom-call | bytes 45000000 | tf_op jit(solution)/shard_map/pallas_call | solution.py:940
  263.7 4.1 convolution_convert_fusion.1
  268.2 0.9 multiply_convert_fusion.1
  269.1 4.6 collective-permute-done.1
  273.7 3.8 add_convert_fusion.4
  277.8 1.7 copy-done.15
  279.5 1.2 slice.160
  280.7 4.3 all-to-all-start.1
  285.0 7.8 %fusion.28 = f32[1024,2048]{1,0:T(8,128)S(1)} fusion(bf16[800,2048]{1,0:T(8,128)(2,1)} %bitcast.176, f32[1024,800]{0,1:T(8,128)} %copy-done.26, f32[1024]{0:T(1024)S(1)} %bitcast.154, f32[1024]{0:T(1024)S(1)} %bitcast.151, s32[1024]{0:T(1024)S(1)} %get-tuple-element.173), kind=kOutput, calls=%fused_computation.129 | convolution fusion | flops 3360358400 | bytes 14954496 | tf_op jit(solution)/shard_map/dot_general | solution.py:434
  292.9 1.4 slice.159
  294.2 1.2 copy-done.24
  295.5 6.4 %add_convert_fusion.1 = bf16[1024,2048]{1,0:T(8,128)(2,1)} fusion(f32[1024,2048]{1,0:T(8,128)S(1)} %fusion.28, bf16[1024,800]{0,1:T(8,128)(2,1)S(1)} %copy-done.28, bf16[800,2048]{1,0:T(8,128)(2,1)S(1)} %bitcast.174), kind=kOutput, calls=%fused_computation.7 | convolution fusion | flops 3359637504 | bytes 17498112 | tf_op jit(solution)/shard_map/dot_general | solution.py:434
  301.9 77.2 %shard_map.354 = (bf16[4,2,2,64,2048]{4,3,2,1,0:T(8,128)(2,1)}, f32[3,2048]{1,0:T(4,128)}) custom-call(bf16[4,2,2,64,2048]{4,3,2,1,0:T(8,128)(2,1)} %bitcast.167, f32[64,2048]{1,0:T(8,128)} %get-tuple-element.73.resid, f32[1,2048]{1,0:T(1,128)} %bitcast.183), custom_call_target="tpu_custom_call" | custom-call | bytes 270000000 | tf_op jit(solution)/shard_map/pallas_call | solution.py:855
  379.2 8.0 %all-to-all-start.2 = ((bf16[8,464,256]{2,1,0:T(8,128)(2,1)}), bf16[8,464,256]{2,1,0:T(8,128)(2,1)}, u32[]{:S(2)}, u32[]{:S(2)}) async-start(bf16[8,464,256]{2,1,0:T(8,128)(2,1)} %slice.159), calls=%async_computation.2 | async-start | bytes 3801088 | tf_op jit(solution)/shard_map/all_to_all | solution.py:454
  387.2 1.1 copy-done.6
  388.4 10.7 %shard_map.355 = (bf16[1024,384]{1,0:T(8,128)(2,1)S(1)}, bf16[1024,512]{1,0:T(8,128)(2,1)S(1)}, f32[1,896]{1,0:T(1,128)S(1)}) custom-call(s32[16]{0:T(128)S(1)} %get-tuple-element.145.order, bf16[1024,2048]{1,0:T(8,128)(2,1)} %bitcast.156, bf16[640,2048]{1,0:T(8,128)(2,1)} %get-tuple-element.64.wout, f32[1024,512]{1,0:T(8,128)} %get-tuple-element.153.slope, ...), custom_call_target="tpu_custom_call" | custom-call | bytes 1000 | tf_op jit(solution)/shard_map/pallas_call | solution.py:1575
  399.1 4.6 fusion.38
  403.9 3.0 copy-done.22
  406.9 2.5 fusion.39
  409.4 2.0 copy-done.17
  411.5 1.5 pad_maximum_fusion.1
  413.0 4.6 collective-permute-start.2
  418.9 0.9 constant_dynamic-slice_fusion.rows
  420.3 1.1 slice.165.dense_in
  421.4 1.7 slice.162
  423.4 1.2 constant_dynamic-slice_fusion.1
  424.9 3.6 fusion.2
  428.5 6.9 %all-to-all-start.3 = ((bf16[8,512,256]{2,1,0:T(8,128)(2,1)}), bf16[8,512,256]{2,1,0:T(8,128)(2,1)}, u32[]{:S(2)}, u32[]{:S(2)}) async-start(bf16[8,512,256]{2,1,0:T(8,128)(2,1)} %fusion.2), calls=%async_computation.3 | async-start | bytes 4194304 | tf_op jit(solution)/shard_map/all_to_all | solution.py:454
  435.5 2.4 fusion.40
  438.0 0.7 copy-done.46
  438.6 6.1 %fusion.29 = (f32[2048]{0:T(1024)S(1)}, f32[2048]{0:T(1024)S(1)}, bf16[1024,2048]{1,0:T(8,128)(2,1)}, f32[2048]{0:T(1024)S(1)}, f32[2048]{0:T(1024)S(1)}) fusion(f32[1024]{0:T(1024)S(1)} %rsqrt.12, f32[1024]{0:T(1024)S(1)} %div.31, bf16[4,2,2,2,32,2048]{5,4,3,2,1,0:T(8,128)(2,1)S(1)} %copy-done.13, f32[2048]{0:T(1024)S(1)} %convert_element_type.219, ...), kind=kOutput, calls=%fused_computation.130 | convolution fusion | flops 2174738432 | bytes 19980288 | tf_op jit(solution)/shard_map/dot_general | solution.py:434
  444.9 4.6 convolution_convert_fusion.2.joined_in
  449.5 3.8 pad_maximum_fusion
  453.3 5.7 %copy.122 = bf16[6400,256]{0,1:T(8,128)(2,1)} copy(bf16[6400,256]{1,0:T(8,128)(2,1)} %bitcast.159) | data formatting | bytes 6553600 | tf_op jit(solution)/shard_map/reshape | solution.py:1751
  459.0 5.3 convert_element_type.238
  464.3 64.1 %shard_map.356 = (bf16[2,2,32,2048]{3,2,1,0:T(8,128)(2,1)S(1)}, f32[8,2048]{1,0:T(8,128)S(1)}, f32[4,2,8,128]{3,2,1,0:T(8,128)S(1)}, bf16[256,1536]{1,0:T(8,128)(2,1)S(1)}, bf16[512,256]{1,0:T(8,128)(2,1)S(1)}) custom-call(bf16[4,2,2,2,32,2048]{5,4,3,2,1,0:T(8,128)(2,1)S(1)} %bitcast.148, bf16[32,2048]{1,0:T(8,128)(2,1)S(1)} %get-tuple-element.152.mine_rows, ...), custom_call_target="tpu_custom_call" | custom-call | bytes 210000000 | tf_op jit(solution)/shard_map/pallas_call | solution.py:1424
  528.4 1.3 convert_element_type.245
  530.4 0.8 convert_element_type.246
  532.5 1.1 bitcast_convert_fusion.1
  533.6 2.7 fusion.31
  537.0 1.8 copy.126
  538.8 1.5 bitcast_convert_fusion
  (181 shorter events, 12.6 us)
Async XLA Ops:
  97.1 5.5 %copy-start.34 = (f32[4,2,4,128]{3,2,1,0:T(4,128)S(1)}, f32[4,2,4,128]{3,2,1,0:T(4,128)}, u32[]{:S(2)}) copy-start(f32[4,2,4,128]{3,2,1,0:T(4,128)} %get-tuple-element.61) | copy-start | bytes 49156
  97.1 135.4 %all-to-all-start = ((bf16[8,800,256]{2,1,0:T(8,128)(2,1)}), bf16[8,800,256]{2,1,0:T(8,128)(2,1)}, u32[]{:S(2)}, u32[]{:S(2)}) async-start(bf16[8,800,256]{2,1,0:T(8,128)(2,1)} %bitcast.172), calls=%async_computation | async-start | bytes 6553600 | tf_op jit(solution)/shard_map/all_to_all | solution.py:454
  102.8 3.5 copy-start.11
  102.8 4.8 copy-start.33
  105.8 2.0 copy-start.35
  105.8 2.0 copy-start.36
  105.8 2.1 copy-start.37
  105.8 2.1 copy-start.38
  105.8 2.6 copy-start.43
  105.8 4.0 copy-start.39
  105.8 4.6 copy-start.40
  111.1 2.5 copy-start.12
  113.6 3.5 copy-start.29
  117.2 2.4 copy-start.20
  117.2 6.0 %copy-start.21 = (bf16[1024,2048]{1,0:T(8,128)(2,1)}, bf16[1024,2048]{1,0:T(8,128)(2,1)S(1)}, u32[]{:S(2)}) copy-start(bf16[1024,2048]{1,0:T(8,128)(2,1)S(1)} %get-tuple-element.149) | copy-start | bytes 12582916
  119.6 3.6 copy-start.45
  123.1 4.4 copy-start.5
  123.1 4.4 copy-start.7
  123.2 5.0 copy-start.41
  123.2 5.0 copy-start.42
  128.2 9.5 %copy-start = (bf16[1024,640]{1,0:T(8,128)(2,1)}, bf16[1024,640]{1,0:T(8,128)(2,1)S(1)}, u32[]{:S(2)}) copy-start(bf16[1024,640]{1,0:T(8,128)(2,1)S(1)} %shard_map.351) | copy-start | bytes 3932164
  232.5 11.2 %collective-permute-start = (bf16[8,800,256]{2,1,0:T(8,128)(2,1)}, bf16[8,800,256]{2,1,0:T(8,128)(2,1)}, u32[]{:S(2)}, u32[]{:S(2)}) collective-permute-start(bf16[8,800,256]{2,1,0:T(8,128)(2,1)} %all-to-all-done), channel_id=1, source_target_pairs={{0,1},{1,0},{2,3},{3,2},{4,5},{5,4},{6,7},{7,6},{8,9},{9,8},{10,11... | collective-permute-start | bytes 9830408 | tf_op jit(solution)/shard_map/ppermute | solution.py:438
  236.9 3.2 copy-start.44
  239.5 4.2 copy-start.23
  246.1 3.6 copy-start.25
  249.7 14.0 %copy-start.26 = (f32[1024,800]{0,1:T(8,128)}, f32[1024,800]{0,1:T(8,128)S(1)}, u32[]{:S(2)}) copy-start(f32[1024,800]{0,1:T(8,128)S(1)} %get-tuple-element.188) | copy-start | bytes 9830404
  267.8 5.9 %collective-permute-start.1 = (bf16[800,2048]{1,0:T(8,128)(2,1)S(1)}, bf16[800,2048]{1,0:T(8,128)(2,1)S(1)}, u32[]{:S(2)}, u32[]{:S(2)}) collective-permute-start(bf16[800,2048]{1,0:T(8,128)(2,1)S(1)} %convolution_convert_fusion.1), channel_id=1, source_target_pairs={{0,1},{1,0},{2,3},{3,2},{4,5},{5,4},{6,7},{7,6},{8,9},{9,8},{10,11... | collective-permute-start | bytes 9830408 | tf_op jit(solution)/shard_map/ppermute | solution.py:438
  269.1 8.5 %copy-start.27 = (bf16[1024,800]{0,1:T(8,128)(2,1)}, bf16[1024,800]{0,1:T(8,128)(2,1)S(1)}, u32[]{:S(2)}) copy-start(bf16[1024,800]{0,1:T(8,128)(2,1)S(1)} %multiply_convert_fusion.1) | copy-start | bytes 4915204
  277.8 1.7 copy-start.15
  280.7 98.5 %all-to-all-start.1 = ((bf16[8,336,256]{2,1,0:T(8,128)(2,1)}), bf16[8,336,256]{2,1,0:T(8,128)(2,1)}, u32[]{:S(2)}, u32[]{:S(2)}) async-start(bf16[8,336,256]{2,1,0:T(8,128)(2,1)} %slice.160), calls=%async_computation.1 | async-start | bytes 2752512 | tf_op jit(solution)/shard_map/all_to_all | solution.py:454
  285.0 7.8 %copy-start.16 = (bf16[100,8,8,256]{3,2,0,1:T(8,128)(2,1)S(1)}, bf16[100,8,8,256]{3,2,0,1:T(8,128)(2,1)}, u32[]{:S(2)}) copy-start(bf16[100,8,8,256]{3,2,0,1:T(8,128)(2,1)} %copy-done.15) | copy-start | bytes 9830404
  285.0 9.2 %copy-start.28 = (bf16[1024,800]{0,1:T(8,128)(2,1)S(1)}, bf16[1024,800]{0,1:T(8,128)(2,1)}, u32[]{:S(2)}) copy-start(bf16[1024,800]{0,1:T(8,128)(2,1)} %copy-done.27) | copy-start | bytes 4915204
  292.9 2.6 copy-start.24
  379.2 8.1 %copy-start.8 = (f32[8,128,128]{2,1,0:T(8,128)S(1)}, f32[8,128,128]{2,1,0:T(8,128)}, u32[]{:S(2)}) copy-start(f32[8,128,128]{2,1,0:T(8,128)} %copy-done.7) | copy-start | bytes 1572868
  379.2 49.3 %all-to-all-start.2 = ((bf16[8,464,256]{2,1,0:T(8,128)(2,1)}), bf16[8,464,256]{2,1,0:T(8,128)(2,1)}, u32[]{:S(2)}, u32[]{:S(2)}) async-start(bf16[8,464,256]{2,1,0:T(8,128)(2,1)} %slice.159), calls=%async_computation.2 | async-start | bytes 3801088 | tf_op jit(solution)/shard_map/all_to_all | solution.py:454
  387.2 1.1 copy-start.6
  388.4 10.7 %copy-start.1 = (bf16[1024,640]{1,0:T(8,128)(2,1)S(1)}, bf16[1024,640]{1,0:T(8,128)(2,1)}, u32[]{:S(2)}) copy-start(bf16[1024,640]{1,0:T(8,128)(2,1)} %copy-done) | copy-start | bytes 3932164
  388.4 10.7 %copy-start.14 = (bf16[4,2,2,64,2048]{4,3,2,1,0:T(8,128)(2,1)S(1)}, bf16[4,2,2,64,2048]{4,3,2,1,0:T(8,128)(2,1)}, u32[]{:S(2)}) copy-start(bf16[4,2,2,64,2048]{4,3,2,1,0:T(8,128)(2,1)} %get-tuple-element.74) | copy-start | bytes 12582916
  399.1 4.8 copy-start.9
  399.1 36.3 %copy-start.3 = (bf16[1024,384]{1,0:T(8,128)(2,1)}, bf16[1024,384]{1,0:T(8,128)(2,1)S(1)}, u32[]{:S(2)}) copy-start(bf16[1024,384]{1,0:T(8,128)(2,1)S(1)} %get-tuple-element.84) | copy-start | bytes 2359300
  403.8 5.6 %copy-start.18 = (bf16[640,2048]{1,0:T(8,128)(2,1)}, bf16[640,2048]{1,0:T(8,128)(2,1)S(1)}, u32[]{:S(2)}) copy-start(bf16[640,2048]{1,0:T(8,128)(2,1)S(1)} %get-tuple-element.189) | copy-start | bytes 7864324
  403.8 3.1 copy-start.22
  409.4 2.0 copy-start.17
  413.0 11.6 %collective-permute-start.2 = (bf16[8,512,256]{2,1,0:T(8,128)(2,1)}, bf16[8,512,256]{2,1,0:T(8,128)(2,1)}, u32[]{:S(2)}, u32[]{:S(2)}) collective-permute-start(bf16[8,512,256]{2,1,0:T(8,128)(2,1)} %pad_maximum_fusion.1), channel_id=1, source_target_pairs={{0,1},{1,0},{2,3},{3,2},{4,5},{5,4},{6,7},{7,6},{8,9},{9,8},{10,11... | collective-permute-start | bytes 6291464 | tf_op jit(solution)/shard_map/ppermute | solution.py:438
  423.1 1.7 slice-start
  428.5 6.9 %copy-start.30 = (bf16[2048,384]{1,0:T(8,128)(2,1)S(1)}, bf16[2048,384]{1,0:T(8,128)(2,1)}, u32[]{:S(2)}) copy-start(bf16[2048,384]{1,0:T(8,128)(2,1)} %get-tuple-element.59) | copy-start | bytes 4718596
  428.5 105.1 %all-to-all-start.3 = ((bf16[8,512,256]{2,1,0:T(8,128)(2,1)}), bf16[8,512,256]{2,1,0:T(8,128)(2,1)}, u32[]{:S(2)}, u32[]{:S(2)}) async-start(bf16[8,512,256]{2,1,0:T(8,128)(2,1)} %fusion.2), calls=%async_computation.3 | async-start | bytes 4194304 | tf_op jit(solution)/shard_map/all_to_all | solution.py:454
  435.4 2.4 copy-start.10
  435.5 2.5 copy-start.13
  435.5 3.2 copy-start.46
  438.6 6.2 %copy-start.32 = (f32[3,2048]{1,0:T(4,128)S(1)}, f32[3,2048]{1,0:T(4,128)}, u32[]{:S(2)}) copy-start(f32[3,2048]{1,0:T(4,128)} %get-tuple-element.87) | copy-start | bytes 73732
  438.6 6.2 %copy-start.4 = (bf16[1024,384]{1,0:T(8,128)(2,1)S(1)}, bf16[1024,384]{1,0:T(8,128)(2,1)}, u32[]{:S(2)}) copy-start(bf16[1024,384]{1,0:T(8,128)(2,1)} %copy-done.3) | copy-start | bytes 2359300
  459.0 5.3 copy-start.2
  532.5 7.9 %copy-start.31 = (f32[1,2048]{1,0:T(1,128)}, f32[1,2048]{1,0:T(1,128)S(1)}, u32[]{:S(2)}) copy-start(f32[1,2048]{1,0:T(1,128)S(1)} %get-tuple-element.159) | copy-start | bytes 24580
  537.0 1.8 copy-start.19

commit v5 on v4

--- a/solution.py
+++ b/solution.py
@@ -825,7 +825,7 @@
     return pl.CostEstimate(flops=0, bytes_accessed=us * 3_000_000, transcendentals=0)
 
 
-def comm(which, limit=28):
+def comm(which, limit=22):
     return pltpu.CompilerParams(collective_id=which, has_side_effects=True, vmem_limit_bytes=limit << 20)
 
 
@@ -1583,7 +1583,7 @@
         out_specs=[vmem()] * 3,
         scratch_shapes=[pltpu.VMEM((total, wout.shape[0]), F32)],
         cost_estimate=pl.CostEstimate(flops=0, bytes_accessed=1000, transcendentals=0),
-        compiler_params=pltpu.CompilerParams(vmem_limit_bytes=48 << 20),
+        compiler_params=pltpu.CompilerParams(vmem_limit_bytes=30 << 20),
     )(order, dbranch, wout, slope, qkv, probs, tables)
 
 

time: 549 us -> 549 us (level)
    unnamed x99 -> x103, local copies, waits for them, and re-layouts: 14.5 us -> 20 us
where the time goes in v5:
time: 549 us; the launch traced here: 541 us
  Pallas kernels  351 us (64%)
  matrix products  63.1 us (11%)
  local copies, waits for them, and re-layouts  46.1 us (8%)
  other arithmetic  40 us (7%)
  starting transfers between devices  32.7 us (6%)
    pallas_call x1, Pallas kernels, reduce_norm_gather(): pl.pallas_call(functools.partial(forward_kernel, nz, half), out_shape=[ja...  94.8 us
    pallas_call x1, Pallas kernels, front(): pl.pallas_call(functools.partial(front_kernel, nz, half), out_shape=[jax....  91.8 us
    pallas_call x1, Pallas kernels, reduce_back_gather(): pl.pallas_call(functools.partial(backward_kernel, nz, half), out_shape=[j...  77.2 us
    dot_general x14, matrix products, dot(): lax.dot_general(a, b, ((contract[:1], contract[1:]), ((), ())), preferred...  63.1 us
    pallas_call x1, Pallas kernels, end(): pl.pallas_call(functools.partial(end_kernel, nz, half), out_shape=[jax.Sh...  62.8 us
    all_to_all x4, starting transfers between devices, exchange(): return lax.all_to_all(value, DP, split_axis=0, concat_axis=0, tiled=True)  23.9 us
    unnamed x103, local copies, waits for them, and re-layouts  20 us
    pallas_call x1, Pallas kernels, objective(): pl.pallas_call(functools.partial(objective_kernel, nz, hot.shape[0], seq_...  12.2 us
  transfers between devices with their start and end apart: 7, of which 1 were waited for; matrix products, arithmetic and copies ran while one was open for 19% of the time, Pallas kernels for 46%

profile of v5, /device:TPU:1, one launch (start us, length us, event | category | flops | bytes accessed | tf_op | source)
XLA Modules:
  0.0 541.3 jit_solution(14202586194234972687)
XLA Ops:
  2.6 1.3 maximum_convert_fusion
  4.0 1.3 pad_maximum_fusion.9.info
  5.3 91.8 %shard_map.349 = (bf16[4,2,2,2,32,2048]{5,4,3,2,1,0:T(8,128)(2,1)}, f32[4,2,4,128]{3,2,1,0:T(4,128)}, f32[28,128]{1,0:T(8,128)}, bf16[2048,384]{1,0:T(8,128)(2,1...) custom-call(bf16[128,2048]{1,0:T(8,128)(2,1)} %residual.1, ...), custom_call_target="tpu_custom_call" | custom-call | bytes 135000000 | tf_op jit(solution)/shard_map/pallas_call | solution.py:1206
  97.1 5.4 %all-to-all-start = ((bf16[8,800,256]{2,1,0:T(8,128)(2,1)}), bf16[8,800,256]{2,1,0:T(8,128)(2,1)}, u32[]{:S(2)}, u32[]{:S(2)}) async-start(bf16[8,800,256]{2,1,0:T(8,128)(2,1)} %bitcast.172), calls=%async_computation | async-start | bytes 6553600 | tf_op jit(solution)/shard_map/all_to_all | solution.py:454
  102.8 3.0 convert_reduce_fusion
  106.2 1.3 fusion.1
  111.3 2.0 fusion.10
  113.6 3.5 add_convert_fusion.2
  117.2 2.3 convolution_add_fusion.fused
  119.6 3.5 shard_map.350
  123.2 4.3 fusion.6
  128.9 1.7 constant_dynamic-slice_fusion.3.rows
  130.6 7.0 %convolution_convert_fusion = bf16[1024,2048]{1,0:T(8,128)(2,1)} fusion(bf16[1024,640]{1,0:T(8,128)(2,1)S(1)} %shard_map.351, bf16[640,2048]{1,0:T(8,128)(2,1)} %get-tuple-element.64.wout), kind=kOutput, calls=%fused_computation.14 | convolution fusion | flops 2686451712 | bytes 8126464 | tf_op jit(solution)/shard_map/dot_general | solution.py:434
  137.7 94.8 %shard_map.352 = (bf16[4,2,2,64,2048]{4,3,2,1,0:T(8,128)(2,1)}, f32[64,2048]{1,0:T(8,128)}) custom-call(bf16[4,2,2,64,2048]{4,3,2,1,0:T(8,128)(2,1)} %bitcast.168, bf16[64,2048]{1,0:T(8,128)(2,1)} %constant_dynamic-slice_fusion.3.rows, f32[1,2048]{1,0:T(1,128)} %bitcast.186, f32[1,2048]{1,0:T(1,128)} %bitcast.182, f32[1,2048]{1,0:T(1,128)} %bitcast.185), custom_call_target="tpu_custom_call" | custom-call | bytes 270000000 | tf_op jit(solution)/shard_map/pallas_call | solution.py:835
  232.5 3.8 collective-permute-start
  236.9 2.5 copy.132
  240.1 3.6 fusion.36
  243.7 2.4 copy.133
  246.1 3.6 fusion.37
  249.7 1.7 exponential_reduce_fusion
  251.5 12.2 %shard_map.353 = (f32[8,128]{1,0:T(8,128)S(1)}, f32[8,128]{1,0:T(8,128)S(1)}, f32[2,8,128]{2,1,0:T(8,128)S(1)}) custom-call(f32[3,8,128]{2,1,0:T(8,128)S(1)} %pad_maximum_fusion.3.stats, f32[3,8,128]{2,1,0:T(8,128)S(1)} %fusion.11.hot, f32[8,128]{1,0:T(8,128)S(1)} %pad_convert_fusion.scored, f32[2,8,128]{2,1,0:T(8,128)S(1)} %pad_maximum_fusion.4.refs, ...), custom_call_target="tpu_custom_call" | custom-call | bytes 45000000 | tf_op jit(solution)/shard_map/pallas_call | solution.py:940
  263.7 4.1 convolution_convert_fusion.1
  268.2 0.9 multiply_convert_fusion.1
  269.1 4.6 collective-permute-done.1
  273.7 3.8 add_convert_fusion.4
  277.8 1.7 copy-done.17
  279.5 1.2 slice.160
  280.7 4.3 all-to-all-start.1
  285.0 7.8 %fusion.28 = f32[1024,2048]{1,0:T(8,128)S(1)} fusion(bf16[800,2048]{1,0:T(8,128)(2,1)} %bitcast.176, f32[1024,800]{0,1:T(8,128)} %copy-done.28, f32[1024]{0:T(1024)S(1)} %bitcast.157, f32[1024]{0:T(1024)S(1)} %bitcast.154, s32[1024]{0:T(1024)S(1)} %get-tuple-element.173), kind=kOutput, calls=%fused_computation.129 | convolution fusion | flops 3360358400 | bytes 14954496 | tf_op jit(solution)/shard_map/dot_general | solution.py:434
  292.8 1.4 slice.159
  294.2 1.2 copy-done.26
  295.4 6.4 %add_convert_fusion.1 = bf16[1024,2048]{1,0:T(8,128)(2,1)} fusion(f32[1024,2048]{1,0:T(8,128)S(1)} %fusion.28, bf16[1024,800]{0,1:T(8,128)(2,1)S(1)} %copy-done.30, bf16[800,2048]{1,0:T(8,128)(2,1)S(1)} %bitcast.174), kind=kOutput, calls=%fused_computation.7 | convolution fusion | flops 3359637504 | bytes 17498112 | tf_op jit(solution)/shard_map/dot_general | solution.py:434
  301.9 77.2 %shard_map.354 = (bf16[4,2,2,64,2048]{4,3,2,1,0:T(8,128)(2,1)}, f32[3,2048]{1,0:T(4,128)}) custom-call(bf16[4,2,2,64,2048]{4,3,2,1,0:T(8,128)(2,1)} %bitcast.167, f32[64,2048]{1,0:T(8,128)} %get-tuple-element.73.resid, f32[1,2048]{1,0:T(1,128)} %bitcast.183), custom_call_target="tpu_custom_call" | custom-call | bytes 270000000 | tf_op jit(solution)/shard_map/pallas_call | solution.py:855
  379.2 8.0 %all-to-all-start.2 = ((bf16[8,464,256]{2,1,0:T(8,128)(2,1)}), bf16[8,464,256]{2,1,0:T(8,128)(2,1)}, u32[]{:S(2)}, u32[]{:S(2)}) async-start(bf16[8,464,256]{2,1,0:T(8,128)(2,1)} %slice.159), calls=%async_computation.2 | async-start | bytes 3801088 | tf_op jit(solution)/shard_map/all_to_all | solution.py:454
  387.2 2.2 copy-done
  389.4 1.7 copy-done.4
  391.1 1.6 copy-done.5
  392.7 1.1 copy-done.9
  393.8 7.5 %shard_map.355 = (bf16[1024,384]{1,0:T(8,128)(2,1)S(1)}, bf16[1024,512]{1,0:T(8,128)(2,1)S(1)}, f32[1,896]{1,0:T(1,128)S(1)}) custom-call(s32[16]{0:T(128)S(1)} %get-tuple-element.145.order, bf16[1024,2048]{1,0:T(8,128)(2,1)S(1)} %bitcast.149, bf16[640,2048]{1,0:T(8,128)(2,1)S(1)} %copy-done.4, f32[1024,512]{1,0:T(8,128)S(1)} %copy-done.5, ...), custom_call_target="tpu_custom_call" | custom-call | bytes 1000 | tf_op jit(solution)/shard_map/pallas_call | solution.py:1575
  401.4 4.6 fusion.38
  406.2 3.0 copy-done.24
  409.1 2.4 fusion.39
  411.5 2.0 copy-done.19
  413.6 1.5 pad_maximum_fusion.1
  415.1 4.6 collective-permute-start.2
  421.0 0.9 constant_dynamic-slice_fusion.rows
  422.5 1.1 slice.165.dense_in
  423.5 1.7 slice.162
  425.5 1.2 constant_dynamic-slice_fusion.1
  427.0 3.6 fusion.2
  430.6 6.2 %all-to-all-start.3 = ((bf16[8,512,256]{2,1,0:T(8,128)(2,1)}), bf16[8,512,256]{2,1,0:T(8,128)(2,1)}, u32[]{:S(2)}, u32[]{:S(2)}) async-start(bf16[8,512,256]{2,1,0:T(8,128)(2,1)} %fusion.2), calls=%async_computation.3 | async-start | bytes 4194304 | tf_op jit(solution)/shard_map/all_to_all | solution.py:454
  436.9 2.4 fusion.40
  440.0 6.1 %fusion.29 = (f32[2048]{0:T(1024)S(1)}, f32[2048]{0:T(1024)S(1)}, bf16[1024,2048]{1,0:T(8,128)(2,1)}, f32[2048]{0:T(1024)S(1)}, f32[2048]{0:T(1024)S(1)}) fusion(f32[1024]{0:T(1024)S(1)} %rsqrt.12, f32[1024]{0:T(1024)S(1)} %div.31, bf16[4,2,2,2,32,2048]{5,4,3,2,1,0:T(8,128)(2,1)S(1)} %copy-done.16, f32[2048]{0:T(1024)S(1)} %convert_element_type.219, ...), kind=kOutput, calls=%fused_computation.130 | convolution fusion | flops 2174738432 | bytes 19980288 | tf_op jit(solution)/shard_map/dot_general | solution.py:434
  446.2 4.6 convolution_convert_fusion.2.joined_in
  450.8 3.8 pad_maximum_fusion
  454.6 5.6 %copy.122 = bf16[6400,256]{0,1:T(8,128)(2,1)} copy(bf16[6400,256]{1,0:T(8,128)(2,1)} %bitcast.159) | data formatting | bytes 6553600 | tf_op jit(solution)/shard_map/reshape | solution.py:1751
  460.3 5.3 convert_element_type.238
  465.6 62.8 %shard_map.356 = (bf16[2,2,32,2048]{3,2,1,0:T(8,128)(2,1)S(1)}, f32[8,2048]{1,0:T(8,128)S(1)}, f32[4,2,8,128]{3,2,1,0:T(8,128)S(1)}, bf16[256,1536]{1,0:T(8,128)(2,1)S(1)}, bf16[512,256]{1,0:T(8,128)(2,1)S(1)}) custom-call(bf16[4,2,2,2,32,2048]{5,4,3,2,1,0:T(8,128)(2,1)S(1)} %bitcast.151, bf16[32,2048]{1,0:T(8,128)(2,1)S(1)} %get-tuple-element.152.mine_rows, ...), custom_call_target="tpu_custom_call" | custom-call | bytes 210000000 | tf_op jit(solution)/shard_map/pallas_call | solution.py:1424
  528.3 1.3 convert_element_type.245
  530.3 0.8 convert_element_type.246
  532.4 1.1 bitcast_convert_fusion.1
  533.5 2.7 fusion.31
  536.9 1.8 copy.126
  538.8 1.5 bitcast_convert_fusion
  (185 shorter events, 14.6 us)
Async XLA Ops:
  97.1 5.5 %copy-start.36 = (f32[4,2,4,128]{3,2,1,0:T(4,128)S(1)}, f32[4,2,4,128]{3,2,1,0:T(4,128)}, u32[]{:S(2)}) copy-start(f32[4,2,4,128]{3,2,1,0:T(4,128)} %get-tuple-element.61) | copy-start | bytes 49156
  97.1 135.3 %all-to-all-start = ((bf16[8,800,256]{2,1,0:T(8,128)(2,1)}), bf16[8,800,256]{2,1,0:T(8,128)(2,1)}, u32[]{:S(2)}, u32[]{:S(2)}) async-start(bf16[8,800,256]{2,1,0:T(8,128)(2,1)} %bitcast.172), calls=%async_computation | async-start | bytes 6553600 | tf_op jit(solution)/shard_map/all_to_all | solution.py:454
  102.8 3.5 copy-start.14
  102.8 4.8 copy-start.35
  105.8 2.0 copy-start.37
  105.8 2.0 copy-start.38
  105.8 2.1 copy-start.39
  105.8 2.1 copy-start.40
  105.8 2.6 copy-start.45
  105.8 4.0 copy-start.41
  105.8 4.6 copy-start.42
  111.1 2.5 copy-start.15
  113.6 3.5 copy-start.31
  117.2 2.4 copy-start.22
  117.2 6.0 %copy-start.23 = (bf16[1024,2048]{1,0:T(8,128)(2,1)}, bf16[1024,2048]{1,0:T(8,128)(2,1)S(1)}, u32[]{:S(2)}) copy-start(bf16[1024,2048]{1,0:T(8,128)(2,1)S(1)} %get-tuple-element.149) | copy-start | bytes 12582916
  119.5 3.6 copy-start.47
  123.1 4.4 copy-start.8
  123.1 4.4 copy-start.10
  123.2 5.0 copy-start.43
  123.2 5.0 copy-start.44
  128.2 9.5 %copy-start.1 = (bf16[1024,640]{1,0:T(8,128)(2,1)}, bf16[1024,640]{1,0:T(8,128)(2,1)S(1)}, u32[]{:S(2)}) copy-start(bf16[1024,640]{1,0:T(8,128)(2,1)S(1)} %shard_map.351) | copy-start | bytes 3932164
  232.5 11.2 %collective-permute-start = (bf16[8,800,256]{2,1,0:T(8,128)(2,1)}, bf16[8,800,256]{2,1,0:T(8,128)(2,1)}, u32[]{:S(2)}, u32[]{:S(2)}) collective-permute-start(bf16[8,800,256]{2,1,0:T(8,128)(2,1)} %all-to-all-done), channel_id=1, source_target_pairs={{0,1},{1,0},{2,3},{3,2},{4,5},{5,4},{6,7},{7,6},{8,9},{9,8},{10,11... | collective-permute-start | bytes 9830408 | tf_op jit(solution)/shard_map/ppermute | solution.py:438
  236.9 3.2 copy-start.46
  239.4 4.2 copy-start.25
  246.1 3.6 copy-start.27
  249.7 14.0 %copy-start.28 = (f32[1024,800]{0,1:T(8,128)}, f32[1024,800]{0,1:T(8,128)S(1)}, u32[]{:S(2)}) copy-start(f32[1024,800]{0,1:T(8,128)S(1)} %get-tuple-element.188) | copy-start | bytes 9830404
  267.8 5.9 %collective-permute-start.1 = (bf16[800,2048]{1,0:T(8,128)(2,1)S(1)}, bf16[800,2048]{1,0:T(8,128)(2,1)S(1)}, u32[]{:S(2)}, u32[]{:S(2)}) collective-permute-start(bf16[800,2048]{1,0:T(8,128)(2,1)S(1)} %convolution_convert_fusion.1), channel_id=1, source_target_pairs={{0,1},{1,0},{2,3},{3,2},{4,5},{5,4},{6,7},{7,6},{8,9},{9,8},{10,11... | collective-permute-start | bytes 9830408 | tf_op jit(solution)/shard_map/ppermute | solution.py:438
  269.1 8.5 %copy-start.29 = (bf16[1024,800]{0,1:T(8,128)(2,1)}, bf16[1024,800]{0,1:T(8,128)(2,1)S(1)}, u32[]{:S(2)}) copy-start(bf16[1024,800]{0,1:T(8,128)(2,1)S(1)} %multiply_convert_fusion.1) | copy-start | bytes 4915204
  277.8 1.7 copy-start.17
  280.7 98.5 %all-to-all-start.1 = ((bf16[8,336,256]{2,1,0:T(8,128)(2,1)}), bf16[8,336,256]{2,1,0:T(8,128)(2,1)}, u32[]{:S(2)}, u32[]{:S(2)}) async-start(bf16[8,336,256]{2,1,0:T(8,128)(2,1)} %slice.160), calls=%async_computation.1 | async-start | bytes 2752512 | tf_op jit(solution)/shard_map/all_to_all | solution.py:454
  285.0 7.8 %copy-start.18 = (bf16[100,8,8,256]{3,2,0,1:T(8,128)(2,1)S(1)}, bf16[100,8,8,256]{3,2,0,1:T(8,128)(2,1)}, u32[]{:S(2)}) copy-start(bf16[100,8,8,256]{3,2,0,1:T(8,128)(2,1)} %copy-done.17) | copy-start | bytes 9830404
  285.0 9.2 %copy-start.30 = (bf16[1024,800]{0,1:T(8,128)(2,1)S(1)}, bf16[1024,800]{0,1:T(8,128)(2,1)}, u32[]{:S(2)}) copy-start(bf16[1024,800]{0,1:T(8,128)(2,1)} %copy-done.29) | copy-start | bytes 4915204
  292.8 2.6 copy-start.26
  379.1 8.1 %copy-start.11 = (f32[8,128,128]{2,1,0:T(8,128)S(1)}, f32[8,128,128]{2,1,0:T(8,128)}, u32[]{:S(2)}) copy-start(f32[8,128,128]{2,1,0:T(8,128)} %copy-done.10) | copy-start | bytes 1572868
  379.2 51.5 %all-to-all-start.2 = ((bf16[8,464,256]{2,1,0:T(8,128)(2,1)}), bf16[8,464,256]{2,1,0:T(8,128)(2,1)}, u32[]{:S(2)}, u32[]{:S(2)}) async-start(bf16[8,464,256]{2,1,0:T(8,128)(2,1)} %slice.159), calls=%async_computation.2 | async-start | bytes 3801088 | tf_op jit(solution)/shard_map/all_to_all | solution.py:454
  387.2 2.2 copy-start
  389.4 1.7 copy-start.4
  391.1 1.6 copy-start.5
  392.7 1.1 copy-start.9
  393.8 7.5 %copy-start.2 = (bf16[1024,640]{1,0:T(8,128)(2,1)S(1)}, bf16[1024,640]{1,0:T(8,128)(2,1)}, u32[]{:S(2)}) copy-start(bf16[1024,640]{1,0:T(8,128)(2,1)} %copy-done.1) | copy-start | bytes 3932164
  401.4 4.8 copy-start.12
  401.4 35.4 %copy-start.6 = (bf16[1024,384]{1,0:T(8,128)(2,1)}, bf16[1024,384]{1,0:T(8,128)(2,1)S(1)}, u32[]{:S(2)}) copy-start(bf16[1024,384]{1,0:T(8,128)(2,1)S(1)} %get-tuple-element.84) | copy-start | bytes 2359300
  406.0 5.5 %copy-start.20 = (bf16[640,2048]{1,0:T(8,128)(2,1)}, bf16[640,2048]{1,0:T(8,128)(2,1)S(1)}, u32[]{:S(2)}) copy-start(bf16[640,2048]{1,0:T(8,128)(2,1)S(1)} %get-tuple-element.189) | copy-start | bytes 7864324
  406.0 3.1 copy-start.24
  411.5 2.0 copy-start.19
  415.1 11.6 %collective-permute-start.2 = (bf16[8,512,256]{2,1,0:T(8,128)(2,1)}, bf16[8,512,256]{2,1,0:T(8,128)(2,1)}, u32[]{:S(2)}, u32[]{:S(2)}) collective-permute-start(bf16[8,512,256]{2,1,0:T(8,128)(2,1)} %pad_maximum_fusion.1), channel_id=1, source_target_pairs={{0,1},{1,0},{2,3},{3,2},{4,5},{5,4},{6,7},{7,6},{8,9},{9,8},{10,11... | collective-permute-start | bytes 6291464 | tf_op jit(solution)/shard_map/ppermute | solution.py:438
  425.3 1.7 slice-start
  430.6 6.2 %copy-start.32 = (bf16[2048,384]{1,0:T(8,128)(2,1)S(1)}, bf16[2048,384]{1,0:T(8,128)(2,1)}, u32[]{:S(2)}) copy-start(bf16[2048,384]{1,0:T(8,128)(2,1)} %get-tuple-element.59) | copy-start | bytes 4718596
  430.6 102.9 %all-to-all-start.3 = ((bf16[8,512,256]{2,1,0:T(8,128)(2,1)}), bf16[8,512,256]{2,1,0:T(8,128)(2,1)}, u32[]{:S(2)}, u32[]{:S(2)}) async-start(bf16[8,512,256]{2,1,0:T(8,128)(2,1)} %fusion.2), calls=%async_computation.3 | async-start | bytes 4194304 | tf_op jit(solution)/shard_map/all_to_all | solution.py:454
  436.8 2.4 copy-start.13
  436.8 2.5 copy-start.16
  436.8 3.2 copy-start.48
  440.0 6.1 %copy-start.34 = (f32[3,2048]{1,0:T(4,128)S(1)}, f32[3,2048]{1,0:T(4,128)}, u32[]{:S(2)}) copy-start(f32[3,2048]{1,0:T(4,128)} %get-tuple-element.87) | copy-start | bytes 73732
  440.0 6.2 %copy-start.7 = (bf16[1024,384]{1,0:T(8,128)(2,1)S(1)}, bf16[1024,384]{1,0:T(8,128)(2,1)}, u32[]{:S(2)}) copy-start(bf16[1024,384]{1,0:T(8,128)(2,1)} %copy-done.6) | copy-start | bytes 2359300
  460.3 5.3 copy-start.3
  532.4 7.9 %copy-start.33 = (f32[1,2048]{1,0:T(1,128)}, f32[1,2048]{1,0:T(1,128)S(1)}, u32[]{:S(2)}) copy-start(f32[1,2048]{1,0:T(1,128)S(1)} %get-tuple-element.159) | copy-start | bytes 24580
  536.9 1.8 copy-start.21
